TPU v7x, 256 devices: a whole 4x4x8 slice. The times are simulated.
256 devices in a mesh: patch: 2 (over y_lo), theta: 32 (over z, x), phi: 4 (over y_hi, core).
Axes of the slice: x: 4, y: 4 (y_hi: 2, y_lo: 2; y = y_hi * 2 + y_lo), z: 8, core: 2. Of those that a mesh axis runs over, the one named last changes fastest.
Arguments:
- fields: float32 [2, 8, 128, 512, 128], P('patch', None, 'theta', 'phi'), may hold values from -2 to 2, as said below
- donor_base: int32 [2, 32, 4, 96], P('patch', 'theta', 'phi'), may hold values from 0 to 380
- weights: float32 [2, 32, 4, 4, 96], P('patch', 'theta', 'phi'), may hold values from 0 to 1, as said below
- frame_angle: float32 [2, 32, 4, 96], P('patch', 'theta', 'phi'), may hold values from -3.140625 to 3.140625
- destination: int32 [2, 32, 4, 96], P('patch', 'theta', 'phi'), may hold values from 0 to 127, as said below
- target_cell: int32 [2, 32, 4, 96], P('patch', 'theta', 'phi'), may hold values from 0 to 511, as said below
Outputs:
- advanced: float32 [2, 8, 128, 512, 128], P('patch', None, 'theta', 'phi')
Inputs may be any that keep to these rules, and one draw needn't show every extreme that they name: `fields`: each log field has a spread of about 0.3, each vector component of about 0.5. The four weights of each border column are positive and sum to one. `destination`: only devices at the patch's edge receive: theta index 0 or 31, or phi index 0 or 3. Each device names any one device of the other patch at most 2 times; in each patch one device of the other patch is named exactly 2 times by every device. `target_cell`: every target cell lies in the outer two colatitude rows or the outer two longitude columns of its patch.
All inputs are finite; a program needn't handle non-finite values.
Results may differ from a plain program's by a relative error of at most 0.0003.
Values sent between devices are 32-bit elements; how exact they have to be, the bound alone decides.
No kernel may reach another device: no remote copies, remote signals or barrier semaphores. Data moves between devices by JAX's collectives and lax.ppermute only.
A program may use at most 64 MiB of HBM per device.

v0:
```python
import math

import jax
import jax.numpy as jnp
from jax import lax
from jax.sharding import PartitionSpec as P

margin = 0.03
inner_radius = 0.35
outer_radius = 1.0
gamma_ratio = 5.0 / 3.0
gravity = 1.0
rotation = 2.0
time_step = 0.002


def with_halo(x, sides, width):
    for axis, dim in sides:
        size, length = (lax.axis_size(axis), x.shape[dim])
        up = [(i, (i + 1) % size) for i in range(size - 1)]
        down = [(j, i) for i, j in up]
        last = lax.slice_in_dim(x, length - width, length, axis=dim)
        initial = lax.slice_in_dim(x, 0, width, axis=dim)
        before = lax.ppermute(last, axis, up)
        after = lax.ppermute(initial, axis, down)
        x = jnp.concatenate([before, x, after], axis=dim)
    return x


def stencil(far_low, near_low, near_high, far_high, spacing):
    return (far_low - 8.0 * near_low + 8.0 * near_high - far_high) / (12.0 * spacing)


def along_theta(extended, spacing):
    return stencil(
        extended[:, :-4, 2:-2],
        extended[:, 1:-3, 2:-2],
        extended[:, 3:-1, 2:-2],
        extended[:, 4:, 2:-2],
        spacing,
    )


def along_phi(extended, spacing):
    return stencil(
        extended[:, 2:-2, :-4],
        extended[:, 2:-2, 1:-3],
        extended[:, 2:-2, 3:-1],
        extended[:, 2:-2, 4:],
        spacing,
    )


def along_radius(centre, spacing):
    padded = jnp.pad(centre, ((0, 0), (0, 0), (0, 0), (2, 2)), mode="edge")
    return stencil(padded[..., :-4], padded[..., 1:-3], padded[..., 3:-1], padded[..., 4:], spacing)


def tendency(extended, theta_rows, phi_cols, patch_flag, theta_step, phi_step):
    shells = extended.shape[3]
    radial_step = (outer_radius - inner_radius) / shells
    radius = inner_radius + radial_step * (
        jnp.arange(shells, dtype=jnp.int32).astype(jnp.float32) + 0.5
    )
    inv_r = (1.0 / radius)[None, None, :]
    sine_theta = jnp.sin(theta_rows)[:, None, None]
    cosine_theta = jnp.cos(theta_rows)[:, None, None]
    cot_theta = cosine_theta / sine_theta
    sine_phi = jnp.sin(phi_cols)[None, :, None]
    cosine_phi = jnp.cos(phi_cols)[None, :, None]
    centre = extended[:, 2:-2, 2:-2]
    grad_r = along_radius(centre, radial_step)
    grad_t = along_theta(extended, theta_step) * inv_r
    grad_p = along_phi(extended, phi_step) * (inv_r / sine_theta)
    log_rho, vel_r, vel_t, vel_p, log_p, mag_r, mag_t, mag_p = [centre[which] for which in range(8)]

    def advect(which):
        return vel_r * grad_r[which] + vel_t * grad_t[which] + vel_p * grad_p[which]

    diverge = grad_r[1] + 2.0 * vel_r * inv_r + grad_t[2] + cot_theta * vel_t * inv_r + grad_p[3]
    cur_r = grad_t[7] + cot_theta * mag_p * inv_r - grad_p[6]
    cur_t = grad_p[5] - grad_r[7] - mag_p * inv_r
    cur_p = grad_r[6] + mag_t * inv_r - grad_t[5]
    electric = jnp.stack(
        [
            extended[2] * extended[7] - extended[3] * extended[6],
            extended[3] * extended[5] - extended[1] * extended[7],
            extended[1] * extended[6] - extended[2] * extended[5],
        ]
    )
    elec_centre = electric[:, 2:-2, 2:-2]
    elec_r = along_radius(elec_centre, radial_step)
    elec_t = along_theta(electric, theta_step) * inv_r
    elec_p = along_phi(electric, phi_step) * (inv_r / sine_theta)
    induce_r = elec_t[2] + cot_theta * elec_centre[2] * inv_r - elec_p[1]
    induce_t = elec_p[0] - elec_r[2] - elec_centre[2] * inv_r
    induce_p = elec_r[1] + elec_centre[1] * inv_r - elec_t[0]
    omega_y = rotation * patch_flag
    omega_z = rotation * (1.0 - patch_flag)
    omega_r = omega_y * sine_theta * sine_phi + omega_z * cosine_theta
    omega_t = omega_y * cosine_theta * sine_phi - omega_z * sine_theta
    omega_p = omega_y * cosine_phi
    inv_rho = jnp.exp(-log_rho)
    temper = jnp.exp(log_p - log_rho)
    rate_rho = -advect(0) - diverge
    rate_p = -advect(4) - gamma_ratio * diverge
    rate_vr = (
        -advect(1)
        + (vel_t * vel_t + vel_p * vel_p) * inv_r
        - temper * grad_r[4]
        + inv_rho * (cur_t * mag_p - cur_p * mag_t)
        - 2.0 * (omega_t * vel_p - omega_p * vel_t)
        - gravity * inv_r * inv_r
    )
    rate_vt = (
        -advect(2)
        - (vel_r * vel_t - cot_theta * vel_p * vel_p) * inv_r
        - temper * grad_t[4]
        + inv_rho * (cur_p * mag_r - cur_r * mag_p)
        - 2.0 * (omega_p * vel_r - omega_r * vel_p)
    )
    rate_vp = (
        -advect(3)
        - (vel_r * vel_p + cot_theta * vel_t * vel_p) * inv_r
        - temper * grad_p[4]
        + inv_rho * (cur_r * mag_t - cur_t * mag_r)
        - 2.0 * (omega_r * vel_t - omega_t * vel_r)
    )
    return jnp.stack([rate_rho, rate_vr, rate_vt, rate_vp, rate_p, induce_r, induce_t, induce_p])


def rotate(values, cosine, sine):
    new_vt = cosine * values[2] - sine * values[3]
    new_vp = sine * values[2] + cosine * values[3]
    new_bt = cosine * values[6] - sine * values[7]
    new_bp = sine * values[6] + cosine * values[7]
    return jnp.stack([values[0], values[1], new_vt, new_vp, values[4], values[5], new_bt, new_bp])


def local(fields, donor_base, weights, frame_angle, destination, target_cell):
    own_block = fields[0]
    rows_dev = own_block.shape[1]
    cols_dev = own_block.shape[2]
    shells = own_block.shape[3]
    n_theta = lax.axis_size("theta")
    n_phi = lax.axis_size("phi")
    theta_step = (0.5 * math.pi + 2.0 * margin) / (rows_dev * n_theta)
    phi_step = (1.5 * math.pi + 2.0 * margin) / (cols_dev * n_phi)
    row_index = lax.axis_index("theta") * rows_dev + jnp.arange(rows_dev, dtype=jnp.int32)
    theta_rows = 0.25 * math.pi - margin + (row_index.astype(jnp.float32) + 0.5) * theta_step
    col_index = lax.axis_index("phi") * cols_dev + jnp.arange(cols_dev, dtype=jnp.int32)
    phi_cols = -0.75 * math.pi - margin + (col_index.astype(jnp.float32) + 0.5) * phi_step
    patch_flag = lax.axis_index("patch").astype(jnp.float32)
    slot_count = donor_base.shape[3]
    dest_count = n_theta * n_phi
    capacity = max(2, 2 * slot_count // dest_count)
    buffer_slots = dest_count * capacity
    block_cells = rows_dev * cols_dev
    corner_base = donor_base[0, 0, 0]
    corner = corner_base // (cols_dev - 1) * cols_dev + corner_base % (cols_dev - 1)
    weight_rows = weights[0, 0, 0]
    cosine = jnp.cos(frame_angle[0, 0, 0])[:, None]
    sine = jnp.sin(frame_angle[0, 0, 0])[:, None]
    receiver_dev = destination[0, 0, 0]
    same_owner = receiver_dev[:, None] == receiver_dev[None, :]
    slot_iota = jnp.arange(slot_count, dtype=jnp.int32)
    earlier = slot_iota[None, :] < slot_iota[:, None]
    slot_rank = jnp.sum((same_owner & earlier).astype(jnp.int32), axis=1)
    position = receiver_dev * capacity + slot_rank
    cell_buffer = (
        jnp.full((1, buffer_slots, 1), block_cells, jnp.int32)
        .at[0, position, 0]
        .set(target_cell[0, 0, 0])
    )

    def evaluate(current):
        extended = with_halo(current, (("theta", 1), ("phi", 2)), 2)
        return tendency(extended, theta_rows, phi_cols, patch_flag, theta_step, phi_step)

    def to_partner(pair):
        gathered = (
            lax.all_gather(pair[0][None], "patch", axis=0, tiled=True),
            lax.all_gather(pair[1][None], "patch", axis=0, tiled=True),
        )
        other_patch = 1 - lax.axis_index("patch")
        return (
            lax.dynamic_index_in_dim(gathered[0], other_patch, 0, keepdims=False),
            lax.dynamic_index_in_dim(gathered[1], other_patch, 0, keepdims=False),
        )

    def route(pair):
        return (
            lax.all_to_all(pair[0], ("theta", "phi"), split_axis=1, concat_axis=1, tiled=True),
            lax.all_to_all(pair[1], ("theta", "phi"), split_axis=1, concat_axis=1, tiled=True),
        )

    def overset(updated):
        flat_fields = updated.reshape(8, block_cells, shells)
        donor_value = weight_rows[0][None, :, None] * jnp.take(flat_fields, corner, axis=1)
        donor_value = donor_value + weight_rows[1][None, :, None] * jnp.take(
            flat_fields, corner + 1, axis=1
        )
        donor_value = donor_value + weight_rows[2][None, :, None] * jnp.take(
            flat_fields, corner + cols_dev, axis=1
        )
        donor_value = donor_value + weight_rows[3][None, :, None] * jnp.take(
            flat_fields, corner + cols_dev + 1, axis=1
        )
        donor_value = rotate(donor_value, cosine, sine)
        send_values = (
            jnp.zeros((8, buffer_slots, shells), jnp.float32).at[:, position, :].set(donor_value)
        )
        moved = route(to_partner((send_values, cell_buffer)))
        cell_flat = moved[1].reshape(-1)
        summed = (
            jnp.zeros((8, block_cells, shells), jnp.float32)
            .at[:, cell_flat, :]
            .add(moved[0], mode="drop")
        )
        counts = jnp.zeros((block_cells,), jnp.float32).at[cell_flat].add(1.0, mode="drop")
        merged = jnp.where(counts[None, :, None] > 0.0, summed / counts[None, :, None], flat_fields)
        return merged.reshape(8, rows_dev, cols_dev, shells)

    section_one = overset(own_block + time_step * evaluate(own_block))
    section_two = 0.5 * (own_block + section_one + time_step * evaluate(section_one))
    return overset(section_two)[None]


def solution(mesh):
    placed = (
        P("patch", None, "theta", "phi", None),
        P("patch", "theta", "phi", None),
        P("patch", "theta", "phi", None, None),
        P("patch", "theta", "phi", None),
        P("patch", "theta", "phi", None),
        P("patch", "theta", "phi", None),
    )
    return jax.shard_map(
        local,
        mesh=mesh,
        in_specs=placed,
        out_specs=P("patch", None, "theta", "phi", None),
        check_vma=False,
    )
```

profile of v0, /device:TPU:2, one launch (start us, length us, event | category | flops | bytes accessed | tf_op | source)
XLA Modules:
  0.0 421.8 jit_solution(4705241022663164749)
XLA Ops:
  6.5 3.3 fusion.184
  9.8 3.4 collective-permute-start
  13.2 2.5 collective-permute-start.1
  15.8 2.8 fusion.183
  19.1 2.5 copy.528
  21.7 2.2 copy.529
  23.9 2.2 copy.531
  27.1 9.7 %collective-permute-done = f32[8,2,128,128]{3,2,1,0:T(8,128)S(1)} collective-permute-done((f32[8,2,128,128]{3,2,1,0:T(8,128)}, f32[8,2,128,128]{3,2,1,0:T(8,128)S(1)}, u32[]{:S(2)}, u32[]{:S(2)}) %collective-permute-start) | collective-permute-done | bytes 1048608 | tf_op jit(solution)/shard_map/ppermute | solution.py:24
  36.8 3.2 collective-permute-done.1
  41.0 1.3 collective-permute-start.2
  42.3 1.8 collective-permute-start.3
  45.3 5.6 %fusion.25 = (f32[8,4,128,128]{3,2,1,0:T(8,128)S(1)}, f32[8,4,128,128]{3,2,1,0:T(8,128)S(1)}) fusion(f32[8,4,128,128]{3,2,1,0:T(8,128)S(1)} %bitcast.341, f32[8,4,128,2]{3,2,1,0:T(8,128)S(1)} %reshape.1063, f32[8,4,128,2]{3,2,1,0:T(8,128)S(1)} %reshape.1062, f32[128]{0:T(128)S(1)} %broadcast_multiply_fusion.5, f32[8,2,128,128]{3,2,1,0:T(8,128)} %collective-permute-done.1, ...), kind=kLoop, calls=%fused_computation.55 | loop fusion | flops 10485760 | bytes 8454656 | tf_op jit(solution)/shard_map/div | solution.py:31
  51.0 1.3 multiply_subtract_fusion.5
  55.1 1.5 fusion.36
  58.9 1.5 fusion.55
  61.4 6.4 %stack.91 = f32[8,512,128]{2,0,1:T(8,128)} concatenate(f32[1,512,128]{2,0,1:T(1,128)S(1)} %bitcast.390, f32[1,512,128]{2,0,1:T(1,128)S(1)} %bitcast.389, f32[1,512,128]{2,0,1:T(1,128)S(1)} %bitcast.388, f32[1,512,128]{2,0,1:T(1,128)S(1)} %bitcast.387, f32[1,512,128]{2,0,1:T(1,128)S(1)} %bitcast.386, f32[1,512,128]{2,0,1:T(1,128)} %bitcast.395, f32[1,512,128]{2,0,1:T(1,128)} %bitcast.394, ...), dimensions={0} | concatenate | bytes 4194304 | tf_op jit(solution)/shard_map/stack | solution.py:129
  67.8 3.4 bitcast_add_fusion.1
  71.2 2.4 gather_fusion.2
  73.6 2.2 gather_fusion.3
  75.8 2.2 gather_fusion
  78.1 1.5 gather_fusion.1
  79.6 1.4 fusion.75
  81.7 3.5 scatter_fusion
  86.2 1.2 scatter_custom_fusion
  87.4 4.2 %all-gather.3 = s32[2,1,256]{2,1,0:T(1,128)S(1)} all-gather(s32[1,1,256]{2,1,0:T(1,128)S(1)} %bitcast.409), channel_id=2, replica_groups=mesh['patch'=2,'theta'=32,'phi'=4] {'patch'}, dimensions={0}, use_global_device_ids=true | all-gather | bytes 3072 | tf_op jit(solution)/shard_map/all_gather | solution.py:183
  92.4 22.0 %all-to-all-start = ((s32[1,256,1]{2,0,1:T(1,128)}), s32[1,256,1]{2,0,1:T(1,128)S(1)}, u32[]{:S(2)}, u32[]{:S(2)}) async-start(s32[1,256,1]{2,0,1:T(1,128)} %copy.527), calls=%async_computation | async-start | bytes 262144 | tf_op jit(solution)/shard_map/all_to_all | solution.py:194
  114.4 21.0 %all-gather.7.cloned.1.call-done = f32[16,256,128]{2,0,1:T(8,128)} async-done(((f32[8,256,128]{2,0,1:T(8,128)}), f32[16,256,128]{2,0,1:T(8,128)}) %all-gather.7.cloned.1.call-update) | async-done | bytes 2097168 | tf_op jit(solution)/shard_map/all_gather | solution.py:182
  135.4 2.3 dynamic-slice_bitcast_fusion.1
  137.7 13.5 %all-to-all-start.1 = ((f32[8,256,128]{2,0,1:T(8,128)}), f32[8,256,128]{2,0,1:T(8,128)S(1)}, u32[]{:S(2)}, u32[]{:S(2)}) async-start(f32[8,256,128]{2,0,1:T(8,128)} %dynamic-slice_bitcast_fusion.1), calls=%async_computation.1 | async-start | bytes 2097152 | tf_op jit(solution)/shard_map/all_to_all | solution.py:193
  151.2 4.6 %reduce = s32[256]{0:T(256)S(1)} reduce(s32[1,256,1]{2,0,1:T(1,128)S(1)} %all-to-all-done, s32[]{:T(128)} %constant.43.clone.1), dimensions={0,2}, to_apply=%all_to_all.10.reduce_sub_computation | reduce | bytes 2052 | tf_op jit(solution)/shard_map/all_to_all | solution.py:194
  155.9 2.3 scatter_custom_fusion.1
  158.2 24.5 %all-to-all-done.1 = f32[8,256,128]{2,0,1:T(8,128)S(1)} async-done(((f32[8,256,128]{2,0,1:T(8,128)}), f32[8,256,128]{2,0,1:T(8,128)S(1)}, u32[]{:S(2)}, u32[]{:S(2)}) %all-to-all-start.1) | async-done | bytes 1048608 | tf_op jit(solution)/shard_map/all_to_all | solution.py:193
  182.8 1.5 broadcast.814.clone
  184.2 27.6 %scatter_fusion.1 = f32[8,512,128]{2,0,1:T(8,128)} fusion(f32[8,512,128]{2,0,1:T(8,128)} %broadcast.814.clone, s32[256]{0:T(256)S(1)} %bitcast.406, f32[256,8,128]{2,1,0:T(8,128)S(1)} %bitcast.377), kind=kCustom, calls=%fused_computation.11 | custom fusion | flops 262144 | bytes 3146752 | tf_op jit(solution)/shard_map/scatter-add | solution.py:218
  211.9 3.9 divide_select_fusion.1
  217.1 1.5 fusion.182
  218.6 1.9 collective-permute-start.4
  220.5 4.0 collective-permute-start.5
  224.5 2.7 fusion.181
  227.2 2.2 copy.553
  229.4 2.2 copy.555
  231.6 9.7 %fusion.180 = (f32[1,512,128]{2,0,1:T(1,128)S(1)}, f32[1,512,128]{2,0,1:T(1,128)S(1)}, f32[1,512,128]{2,0,1:T(1,128)S(1)}, f32[1,512,128]{2,0,1:T(1,128)S(1)}, f...) fusion(f32[8,512,128]{2,0,1:T(8,128)} %copy-done.1), kind=kLoop, calls=%fused_computation.442 | loop fusion | flops 131072 | bytes 4194304 | tf_op jit(solution)/shard_map/slice | solution.py:75
  242.1 2.0 collective-permute-done.5
  245.1 1.3 collective-permute-start.6
  246.4 1.5 collective-permute-start.7
  249.1 5.6 %fusion.18 = (f32[8,4,128,128]{3,2,1,0:T(8,128)S(1)}, f32[8,4,128,128]{3,2,1,0:T(8,128)S(1)}) fusion(f32[8,4,128,128]{3,2,1,0:T(8,128)S(1)} %bitcast.348, f32[8,4,128,2]{3,2,1,0:T(8,128)S(1)} %reshape.1068, f32[8,4,128,2]{3,2,1,0:T(8,128)S(1)} %reshape.1067, f32[128]{0:T(128)S(1)} %copy-done.21, f32[8,2,128,128]{3,2,1,0:T(8,128)} %collective-permute-done.5, ...), kind=kLoop, calls=%fused_computation.48 | loop fusion | flops 10485760 | bytes 8454656 | tf_op jit(solution)/shard_map/div | solution.py:31
  254.8 1.4 multiply_subtract_fusion.2
  258.9 1.5 fusion.29
  263.1 1.5 fusion.48
  265.6 6.4 %stack.102 = f32[8,512,128]{2,0,1:T(8,128)} concatenate(f32[1,512,128]{2,0,1:T(1,128)S(1)} %bitcast.385, f32[1,512,128]{2,0,1:T(1,128)S(1)} %bitcast.383, f32[1,512,128]{2,0,1:T(1,128)S(1)} %bitcast.382, f32[1,512,128]{2,0,1:T(1,128)S(1)} %bitcast.381, f32[1,512,128]{2,0,1:T(1,128)S(1)} %bitcast.384, f32[1,512,128]{2,0,1:T(1,128)} %bitcast.392, f32[1,512,128]{2,0,1:T(1,128)} %bitcast.391, ...), dimensions={0} | concatenate | bytes 4194304 | tf_op jit(solution)/shard_map/stack | solution.py:129
  272.0 3.9 fusion.43
  276.0 2.5 gather_fusion.6
  278.5 2.3 gather_fusion.7
  280.8 2.3 gather_fusion.4
  283.2 1.6 gather_fusion.5
  284.8 1.4 fusion.72
  286.9 3.4 scatter_fusion.2
  291.3 41.9 %all-gather.9.cloned.1.call-done = f32[16,256,128]{2,0,1:T(8,128)} async-done(((f32[8,256,128]{2,0,1:T(8,128)}), f32[16,256,128]{2,0,1:T(8,128)}) %all-gather.9.cloned.1.call-update) | async-done | bytes 2097168 | tf_op jit(solution)/shard_map/all_gather | solution.py:182
  333.2 1.3 dynamic-slice_bitcast_fusion
  334.5 45.1 %all_to_all.16 = f32[8,256,128]{2,0,1:T(8,128)S(1)} all-to-all(f32[8,256,128]{2,0,1:T(8,128)S(1)} %dynamic-slice_bitcast_fusion), channel_id=1, replica_groups=mesh['patch'=2,'theta'=32,'phi'=4] {'theta','phi'}, dimensions={1} | all-to-all | bytes 2097152 | tf_op jit(solution)/shard_map/all_to_all | solution.py:193
  379.6 1.5 broadcast.814
  381.1 28.1 %scatter_fusion.3 = f32[8,512,128]{2,0,1:T(8,128)} fusion(f32[8,512,128]{2,0,1:T(8,128)} %broadcast.814, s32[256]{0:T(256)S(1)} %bitcast.407, f32[256,8,128]{2,1,0:T(8,128)S(1)} %bitcast.378), kind=kCustom, calls=%fused_computation.13 | custom fusion | flops 262144 | bytes 3146752 | tf_op jit(solution)/shard_map/scatter-add | solution.py:218
  409.2 3.9 divide_select_fusion
  413.0 1.7 copy.576
  (200 shorter events, 24.4 us)
Async XLA Ops:
  6.5 128.9 %all-gather.7.cloned.1.call-start = ((), (), s32[]{:S(2)}) async-start(), calls=%async_computation.3 | async-start | bytes 3145728 | tf_op jit(solution)/shard_map/all_gather | solution.py:182
  6.5 9.2 %copy-start = (f32[1,8,4,128,128]{4,3,2,1,0:T(8,128)S(1)}, f32[1,8,4,128,128]{4,3,2,1,0:T(8,128)}, u32[]{:S(2)}) copy-start(f32[1,8,4,128,128]{4,3,2,1,0:T(8,128)} %param.8) | copy-start | bytes 6291460
  9.8 27.0 %collective-permute-start = (f32[8,2,128,128]{3,2,1,0:T(8,128)}, f32[8,2,128,128]{3,2,1,0:T(8,128)S(1)}, u32[]{:S(2)}, u32[]{:S(2)}) collective-permute-start(f32[8,2,128,128]{3,2,1,0:T(8,128)} %get-tuple-element.59), channel_id=1, source_target_pairs={{0,4},{4,8},{8,12},{12,16},{16,20},{20,24},{24,28},{28,32},{32,36}... | collective-permute-start | bytes 3145736 | tf_op jit(solution)/shard_map/ppermute | solution.py:24
  13.2 26.8 %collective-permute-start.1 = (f32[8,2,128,128]{3,2,1,0:T(8,128)}, f32[8,2,128,128]{3,2,1,0:T(8,128)}, u32[]{:S(2)}, u32[]{:S(2)}) collective-permute-start(f32[8,2,128,128]{3,2,1,0:T(8,128)} %get-tuple-element.60), channel_id=1, source_target_pairs={{4,0},{8,4},{12,8},{16,12},{20,16},{24,20},{28,24},{32,28},{36,32}... | collective-permute-start | bytes 3145736 | tf_op jit(solution)/shard_map/ppermute | solution.py:25
  15.7 40.8 %copy-start.46 = (f32[128]{0:T(128)}, f32[128]{0:T(128)S(1)}, u32[]{:S(2)}) copy-start(f32[128]{0:T(128)S(1)} %get-tuple-element.91) | copy-start | bytes 1540
  15.8 38.7 %copy-start.20 = (f32[128]{0:T(128)}, f32[128]{0:T(128)S(1)}, u32[]{:S(2)}) copy-start(f32[128]{0:T(128)S(1)} %broadcast_multiply_fusion.5) | copy-start | bytes 1540
  15.8 2.8 copy-start.50
  15.8 3.2 copy-start.51
  18.6 60.9 %copy-start.30 = (pred[96]{0:T(512)(128)(4,1)}, pred[96]{0:T(512)(128)(4,1)S(1)}, u32[]{:S(2)}) copy-start(pred[96]{0:T(512)(128)(4,1)S(1)} %get-tuple-element.18) | copy-start | bytes 292
  18.7 60.9 %copy-start.32 = (pred[96]{0:T(512)(128)(4,1)}, pred[96]{0:T(512)(128)(4,1)S(1)}, u32[]{:S(2)}) copy-start(pred[96]{0:T(512)(128)(4,1)S(1)} %get-tuple-element.21) | copy-start | bytes 292
  18.7 60.9 %copy-start.34 = (pred[96]{0:T(512)(128)(4,1)}, pred[96]{0:T(512)(128)(4,1)S(1)}, u32[]{:S(2)}) copy-start(pred[96]{0:T(512)(128)(4,1)S(1)} %get-tuple-element.79) | copy-start | bytes 292
  18.7 60.8 %copy-start.36 = (pred[96]{0:T(512)(128)(4,1)}, pred[96]{0:T(512)(128)(4,1)S(1)}, u32[]{:S(2)}) copy-start(pred[96]{0:T(512)(128)(4,1)S(1)} %get-tuple-element.80) | copy-start | bytes 292
  18.8 41.6 %copy-start.14 = (f32[4]{0:T(128)}, f32[4]{0:T(128)S(1)}, u32[]{:S(2)}) copy-start(f32[4]{0:T(128)S(1)} %get-tuple-element.89) | copy-start | bytes 52
  18.9 39.0 %copy-start.16 = (f32[128]{0:T(128)}, f32[128]{0:T(128)S(1)}, u32[]{:S(2)}) copy-start(f32[128]{0:T(128)S(1)} %get-tuple-element.92) | copy-start | bytes 1540
  18.9 39.0 %copy-start.28 = (f32[128]{0:T(128)}, f32[128]{0:T(128)S(1)}, u32[]{:S(2)}) copy-start(f32[128]{0:T(128)S(1)} %get-tuple-element.93) | copy-start | bytes 1540
  19.0 56.9 %copy-start.22 = (s32[1024]{0:T(1024)}, s32[1024]{0:T(1024)S(1)}, u32[]{:S(2)}) copy-start(s32[1024]{0:T(1024)S(1)} %pad_clamp_fusion.3) | copy-start | bytes 12292
  19.0 59.0 %copy-start.23 = (s32[1024]{0:T(1024)}, s32[1024]{0:T(1024)S(1)}, u32[]{:S(2)}) copy-start(s32[1024]{0:T(1024)S(1)} %pad_clamp_fusion.2) | copy-start | bytes 12292
  19.0 62.2 %copy-start.8 = (f32[96]{0:T(128)}, f32[96]{0:T(128)S(1)}, u32[]{:S(2)}) copy-start(f32[96]{0:T(128)S(1)} %get-tuple-element.77) | copy-start | bytes 1156
  19.1 62.2 %copy-start.10 = (f32[96]{0:T(128)}, f32[96]{0:T(128)S(1)}, u32[]{:S(2)}) copy-start(f32[96]{0:T(128)S(1)} %get-tuple-element.78) | copy-start | bytes 1156
  19.1 52.1 %copy-start.25 = (s32[1024]{0:T(1024)}, s32[1024]{0:T(1024)S(1)}, u32[]{:S(2)}) copy-start(s32[1024]{0:T(1024)S(1)} %get-tuple-element.95) | copy-start | bytes 12292
  19.1 54.5 %copy-start.24 = (s32[1024]{0:T(1024)}, s32[1024]{0:T(1024)S(1)}, u32[]{:S(2)}) copy-start(s32[1024]{0:T(1024)S(1)} %get-tuple-element.94) | copy-start | bytes 12292
  21.7 4.5 %copy-start.52 = (s32[1,1,1,96]{3,2,1,0:T(1,128)S(1)}, s32[1,1,1,96]{3,2,1,0:T(1,128)}, u32[]{:S(2)}) copy-start(s32[1,1,1,96]{3,2,1,0:T(1,128)} %param.12) | copy-start | bytes 1156
  21.7 5.3 %copy-start.49 = (f32[1,1,1,4,96]{4,3,2,1,0:T(4,128)S(1)}, f32[1,1,1,4,96]{4,3,2,1,0:T(4,128)}, u32[]{:S(2)}) copy-start(f32[1,1,1,4,96]{4,3,2,1,0:T(4,128)} %param.10) | copy-start | bytes 4612
  27.0 52.5 %copy-start.38 = (f32[96]{0:T(128)}, f32[96]{0:T(128)S(1)}, u32[]{:S(2)}) copy-start(f32[96]{0:T(128)S(1)} %get-tuple-element.73) | copy-start | bytes 1156
  27.0 52.5 %copy-start.40 = (f32[96]{0:T(128)}, f32[96]{0:T(128)S(1)}, u32[]{:S(2)}) copy-start(f32[96]{0:T(128)S(1)} %get-tuple-element.74) | copy-start | bytes 1156
  27.0 52.5 %copy-start.42 = (f32[96]{0:T(128)}, f32[96]{0:T(128)S(1)}, u32[]{:S(2)}) copy-start(f32[96]{0:T(128)S(1)} %get-tuple-element.75) | copy-start | bytes 1156
  27.0 52.5 %copy-start.44 = (f32[96]{0:T(128)}, f32[96]{0:T(128)S(1)}, u32[]{:S(2)}) copy-start(f32[96]{0:T(128)S(1)} %get-tuple-element.76) | copy-start | bytes 1156
  41.0 10.0 %collective-permute-start.2 = (f32[8,8,2,128]{3,1,2,0:T(8,128)S(1)}, f32[8,8,2,128]{3,1,2,0:T(8,128)S(1)}, u32[]{:S(2)}, u32[]{:S(2)}) collective-permute-start(f32[8,8,2,128]{3,1,2,0:T(8,128)S(1)} %copy.533), channel_id=1, source_target_pairs={{0,1},{1,2},{2,3},{4,5},{5,6},{6,7},{8,9},{9,10},{10,11},{12,13},{... | collective-permute-start | bytes 196616 | tf_op jit(solution)/shard_map/ppermute | solution.py:24
  42.3 8.7 %collective-permute-start.3 = (f32[8,8,2,128]{3,1,2,0:T(8,128)S(1)}, f32[8,8,2,128]{3,1,2,0:T(8,128)S(1)}, u32[]{:S(2)}, u32[]{:S(2)}) collective-permute-start(f32[8,8,2,128]{3,1,2,0:T(8,128)S(1)} %copy.535), channel_id=1, source_target_pairs={{1,0},{2,1},{3,2},{5,4},{6,5},{7,6},{9,8},{10,9},{11,10},{13,12},{... | collective-permute-start | bytes 196616 | tf_op jit(solution)/shard_map/ppermute | solution.py:25
  61.4 6.4 %copy-start.3 = (f32[1,8,4,128,128]{4,1,3,2,0:T(8,128)S(1)}, f32[1,8,4,128,128]{4,1,3,2,0:T(8,128)}, u32[]{:S(2)}) copy-start(f32[1,8,4,128,128]{4,1,3,2,0:T(8,128)} %copy.528) | copy-start | bytes 6291460
  71.2 6.8 %copy-start.4 = (f32[8,512,128]{2,0,1:T(8,128)S(1)}, f32[8,512,128]{2,0,1:T(8,128)}, u32[]{:S(2)}) copy-start(f32[8,512,128]{2,0,1:T(8,128)} %bitcast_add_fusion.1) | copy-start | bytes 6291460
  85.2 1.0 copy-start.7
  92.4 45.3 %all-to-all-start = ((s32[1,256,1]{2,0,1:T(1,128)}), s32[1,256,1]{2,0,1:T(1,128)S(1)}, u32[]{:S(2)}, u32[]{:S(2)}) async-start(s32[1,256,1]{2,0,1:T(1,128)} %copy.527), calls=%async_computation | async-start | bytes 262144 | tf_op jit(solution)/shard_map/all_to_all | solution.py:194
  137.7 45.1 %all-to-all-start.1 = ((f32[8,256,128]{2,0,1:T(8,128)}), f32[8,256,128]{2,0,1:T(8,128)S(1)}, u32[]{:S(2)}, u32[]{:S(2)}) async-start(f32[8,256,128]{2,0,1:T(8,128)} %dynamic-slice_bitcast_fusion.1), calls=%async_computation.1 | async-start | bytes 2097152 | tf_op jit(solution)/shard_map/all_to_all | solution.py:193
  151.2 182.0 %all-gather.9.cloned.1.call-start = ((), (), s32[]{:S(2)}) async-start(), calls=%async_computation.4 | async-start | bytes 3145728 | tf_op jit(solution)/shard_map/all_gather | solution.py:182
  155.9 56.0 %copy-start.18 = (s32[256,1]{0,1:T(1,128)}, s32[256,1]{0,1:T(1,128)S(1)}, u32[]{:S(2)}) copy-start(s32[256,1]{0,1:T(1,128)S(1)} %compare_select_fusion) | copy-start | bytes 3076
  158.2 53.7 %copy-start.12 = (f32[512]{0:T(512)}, f32[512]{0:T(512)S(1)}, u32[]{:S(2)}) copy-start(f32[512]{0:T(512)S(1)} %scatter_custom_fusion.1) | copy-start | bytes 6148
  158.2 53.6 %copy-start.26 = (pred[512]{0:T(512)(128)(4,1)}, pred[512]{0:T(512)(128)(4,1)S(1)}, u32[]{:S(2)}) copy-start(pred[512]{0:T(512)(128)(4,1)S(1)} %broadcast_compare_fusion) | copy-start | bytes 1540
  215.7 1.3 copy-start.1
  218.6 23.5 %collective-permute-start.4 = (f32[8,2,128,128]{3,2,1,0:T(8,128)}, f32[8,2,128,128]{3,2,1,0:T(8,128)S(1)}, u32[]{:S(2)}, u32[]{:S(2)}) collective-permute-start(f32[8,2,128,128]{3,2,1,0:T(8,128)} %get-tuple-element.53), channel_id=1, source_target_pairs={{0,4},{4,8},{8,12},{12,16},{16,20},{20,24},{24,28},{28,32},{32,36}... | collective-permute-start | bytes 3145736 | tf_op jit(solution)/shard_map/ppermute | solution.py:24
  220.5 23.6 %collective-permute-start.5 = (f32[8,2,128,128]{3,2,1,0:T(8,128)}, f32[8,2,128,128]{3,2,1,0:T(8,128)}, u32[]{:S(2)}, u32[]{:S(2)}) collective-permute-start(f32[8,2,128,128]{3,2,1,0:T(8,128)} %get-tuple-element.54), channel_id=1, source_target_pairs={{4,0},{8,4},{12,8},{16,12},{20,16},{24,20},{28,24},{32,28},{36,32}... | collective-permute-start | bytes 3145736 | tf_op jit(solution)/shard_map/ppermute | solution.py:25
  245.1 9.7 %collective-permute-start.6 = (f32[8,8,2,128]{3,1,2,0:T(8,128)S(1)}, f32[8,8,2,128]{3,1,2,0:T(8,128)S(1)}, u32[]{:S(2)}, u32[]{:S(2)}) collective-permute-start(f32[8,8,2,128]{3,1,2,0:T(8,128)S(1)} %copy.557), channel_id=1, source_target_pairs={{0,1},{1,2},{2,3},{4,5},{5,6},{6,7},{8,9},{9,10},{10,11},{12,13},{... | collective-permute-start | bytes 196616 | tf_op jit(solution)/shard_map/ppermute | solution.py:24
  246.4 2.7 copy-start.21
  246.4 8.4 %collective-permute-start.7 = (f32[8,8,2,128]{3,1,2,0:T(8,128)S(1)}, f32[8,8,2,128]{3,1,2,0:T(8,128)S(1)}, u32[]{:S(2)}, u32[]{:S(2)}) collective-permute-start(f32[8,8,2,128]{3,1,2,0:T(8,128)S(1)} %copy.559), channel_id=1, source_target_pairs={{1,0},{2,1},{3,2},{5,4},{6,5},{7,6},{9,8},{10,9},{11,10},{13,12},{... | collective-permute-start | bytes 196616 | tf_op jit(solution)/shard_map/ppermute | solution.py:25
  258.9 1.5 copy-start.15
  260.4 0.6 copy-start.17
  261.0 0.7 copy-start.29
  265.6 6.4 %copy-start.2 = (f32[8,512,128]{2,0,1:T(8,128)S(1)}, f32[8,512,128]{2,0,1:T(8,128)}, u32[]{:S(2)}) copy-start(f32[8,512,128]{2,0,1:T(8,128)} %copy-done.1) | copy-start | bytes 6291460
  275.9 7.2 %copy-start.5 = (f32[8,512,128]{2,0,1:T(8,128)S(1)}, f32[8,512,128]{2,0,1:T(8,128)}, u32[]{:S(2)}) copy-start(f32[8,512,128]{2,0,1:T(8,128)} %fusion.43) | copy-start | bytes 6291460
  275.9 8.8 %copy-start.31 = (pred[96]{0:T(512)(128)(4,1)S(1)}, pred[96]{0:T(512)(128)(4,1)}, u32[]{:S(2)}) copy-start(pred[96]{0:T(512)(128)(4,1)} %copy-done.30) | copy-start | bytes 292
  275.9 8.8 %copy-start.33 = (pred[96]{0:T(512)(128)(4,1)S(1)}, pred[96]{0:T(512)(128)(4,1)}, u32[]{:S(2)}) copy-start(pred[96]{0:T(512)(128)(4,1)} %copy-done.32) | copy-start | bytes 292
  275.9 8.8 %copy-start.35 = (pred[96]{0:T(512)(128)(4,1)S(1)}, pred[96]{0:T(512)(128)(4,1)}, u32[]{:S(2)}) copy-start(pred[96]{0:T(512)(128)(4,1)} %copy-done.34) | copy-start | bytes 292
  275.9 8.8 %copy-start.37 = (pred[96]{0:T(512)(128)(4,1)S(1)}, pred[96]{0:T(512)(128)(4,1)}, u32[]{:S(2)}) copy-start(pred[96]{0:T(512)(128)(4,1)} %copy-done.36) | copy-start | bytes 292
  275.9 8.8 %copy-start.39 = (f32[96]{0:T(128)S(1)}, f32[96]{0:T(128)}, u32[]{:S(2)}) copy-start(f32[96]{0:T(128)} %copy-done.38) | copy-start | bytes 1156
  276.0 8.8 %copy-start.41 = (f32[96]{0:T(128)S(1)}, f32[96]{0:T(128)}, u32[]{:S(2)}) copy-start(f32[96]{0:T(128)} %copy-done.40) | copy-start | bytes 1156
  276.0 8.8 %copy-start.43 = (f32[96]{0:T(128)S(1)}, f32[96]{0:T(128)}, u32[]{:S(2)}) copy-start(f32[96]{0:T(128)} %copy-done.42) | copy-start | bytes 1156
  276.0 8.8 %copy-start.45 = (f32[96]{0:T(128)S(1)}, f32[96]{0:T(128)}, u32[]{:S(2)}) copy-start(f32[96]{0:T(128)} %copy-done.44) | copy-start | bytes 1156
  278.5 7.7 %copy-start.9 = (f32[96]{0:T(128)S(1)}, f32[96]{0:T(128)}, u32[]{:S(2)}) copy-start(f32[96]{0:T(128)} %copy-done.8) | copy-start | bytes 1156
  278.5 7.7 %copy-start.11 = (f32[96]{0:T(128)S(1)}, f32[96]{0:T(128)}, u32[]{:S(2)}) copy-start(f32[96]{0:T(128)} %copy-done.10) | copy-start | bytes 1156
  284.8 2.1 copy-start.48
  290.3 1.0 copy-start.6
  334.5 46.6 %copy-start.19 = (s32[256,1]{0,1:T(1,128)S(1)}, s32[256,1]{0,1:T(1,128)}, u32[]{:S(2)}) copy-start(s32[256,1]{0,1:T(1,128)} %copy-done.18) | copy-start | bytes 3076
  381.1 28.1 %copy-start.13 = (f32[512]{0:T(512)S(1)}, f32[512]{0:T(512)}, u32[]{:S(2)}) copy-start(f32[512]{0:T(512)} %copy-done.12) | copy-start | bytes 6148
  381.1 28.1 %copy-start.27 = (pred[512]{0:T(512)(128)(4,1)S(1)}, pred[512]{0:T(512)(128)(4,1)}, u32[]{:S(2)}) copy-start(pred[512]{0:T(512)(128)(4,1)} %copy-done.26) | copy-start | bytes 1540
  (1 other events, 0.6 us)
Sparse Core Ops, SparseCore 0:
  86.3 49.0 all-gather.6
  291.4 41.7 all-gather.8
where the time goes:
time: 429 us; the launch traced here: 422 us
  other arithmetic  123 us (29%)
  waiting for transfers between devices  103 us (24%)
  local copies, waits for them, and re-layouts  78.3 us (18%)
  starting transfers between devices  53.2 us (12%)
  blocking collectives  49.4 us (12%)
  between operations  14.9 us (3%)
    all_gather x2, waiting for transfers between devices, to_partner(): lax.all_gather(pair[0][None], 'patch', axis=0, tiled=True)  62.9 us
    scatter-add x2, other arithmetic, overset(): summed = jnp.zeros((8, block_cells, shells), jnp.float32).at[:, cell_flat...  55.7 us
    all_to_all x1, blocking collectives, route(): lax.all_to_all(pair[0], ('theta', 'phi'), split_axis=1, concat_axis=1, ti...  45.1 us
    all_to_all x1, waiting for transfers between devices, route(): lax.all_to_all(pair[0], ('theta', 'phi'), split_axis=1, concat_axis=1, ti...  24.5 us
    all_to_all x1, starting transfers between devices, route(): lax.all_to_all(pair[1], ('theta', 'phi'), split_axis=1, concat_axis=1, ti...  22 us
    slice x12, local copies, waits for them, and re-layouts, along_radius(): padded = jnp.pad(centre, ((0, 0), (0, 0), (0, 0), (2, 2)), mode='edge')  15.8 us
    div x4, other arithmetic, stencil(): (far_low - 8.0 * near_low + 8.0 * near_high - far_high) / (12.0 * spacing)  14.2 us
    all_to_all x1, starting transfers between devices, route(): lax.all_to_all(pair[0], ('theta', 'phi'), split_axis=1, concat_axis=1, ti...  13.5 us
  transfers between devices with their start and end apart: 12, of which 7 were waited for; matrix products, arithmetic and copies ran while one was open for 13% of the time, Pallas kernels for 0%

commit v1 on v0

v1 whole, which is shorter than its diff:
```python
import math

import jax
import jax.numpy as jnp
from jax import lax
from jax.experimental import pallas as pl
from jax.experimental.pallas import tpu as pltpu
from jax.sharding import PartitionSpec as P

margin = 0.03
inner_radius = 0.35
outer_radius = 1.0
gamma_ratio = 5.0 / 3.0
gravity = 1.0
rotation = 2.0
time_step = 0.002

ROWS, COLS, SHELLS, FIELDS, SLOTS = 4, 128, 128, 8, 96
CELLS = ROWS * COLS
N_THETA, N_PHI = 32, 4
DEVS = N_THETA * N_PHI
CAPACITY = 2
PAD = 8
EXT = COLS + 2 * PAD
THETA_STEP = (0.5 * math.pi + 2.0 * margin) / (ROWS * N_THETA)
PHI_STEP = (1.5 * math.pi + 2.0 * margin) / (COLS * N_PHI)
RADIAL_STEP = (outer_radius - inner_radius) / SHELLS
VMEM = pl.BlockSpec(memory_space=pltpu.VMEM)
SMEM = pl.BlockSpec(memory_space=pltpu.SMEM)


def diff(far_low, near_low, near_high, far_high):
    return (far_low - far_high) + 8.0 * (near_high - near_low)


def step_kernel(second, *refs):
    if second:
        base, refs = refs[0], refs[1:]
    own, above, below, left, right, row_const, phi_const, inv_r_ref, corner, angle, place, updated, send, ext, donor = refs

    for i in range(ROWS):
        for f in range(FIELDS):
            ext[f, i, PAD : PAD + COLS, :] = own[f, i]
            ext[f, i, PAD - 2 : PAD, :] = left[f, i]
            ext[f, i, PAD + COLS : PAD + COLS + 2, :] = right[f, i]

    lane = lax.broadcasted_iota(jnp.int32, (8, SHELLS), 1)
    first, second_lane = lane < 1, lane < 2
    last, before_last = lane > SHELLS - 2, lane > SHELLS - 3
    inv_r = inv_r_ref[...]
    k_r = 1.0 / (12.0 * RADIAL_STEP)
    g_t = inv_r * (1.0 / (12.0 * THETA_STEP))

    def d_r(x):
        near_low = jnp.where(first, x, pltpu.roll(x, 1, 1))
        far_low = jnp.where(second_lane, near_low, pltpu.roll(x, 2, 1))
        near_high = jnp.where(last, x, pltpu.roll(x, SHELLS - 1, 1))
        far_high = jnp.where(before_last, near_high, pltpu.roll(x, SHELLS - 2, 1))
        return diff(far_low, near_low, near_high, far_high) * k_r

    def plane(i):
        if i < 0:
            return above, i + 2
        if i >= ROWS:
            return below, i - ROWS
        return own, i

    for i in range(ROWS):
        sine, cosine, cot, inv_sine = [row_const[i, k] for k in range(4)]
        omega_y, omega_z = row_const[i, 4], row_const[i, 5]
        g_p = inv_r * (inv_sine * (1.0 / (12.0 * PHI_STEP)))
        cot_r = inv_r * cot

        def tile(j, carry):
            start = pl.multiple_of(j * 8, 8)
            rows = pl.ds(start, 8)
            q, ur, ut, up, h, br, bt, bp = [own[f, i, rows, :] for f in range(FIELDS)]
            near = []
            for d in (-2, -1, 1, 2):
                ref, p = plane(i + d)
                near.append([ref[f, p, rows, :] for f in range(FIELDS)])
            tq, tur, tut, tup, th, tbr, _, tbp = [
                diff(*[n[f] for n in near]) * g_t if f != 6 else None for f in range(FIELDS)
            ]
            t_er = diff(*[n[2] * n[7] - n[3] * n[6] for n in near]) * g_t
            t_ep = diff(*[n[1] * n[6] - n[2] * n[5] for n in near]) * g_t
            near = []
            for d in (-2, -1, 1, 2):
                near.append([ext[f, i, pl.ds(start + (PAD + d), 8), :] for f in range(FIELDS)])
            pq, pur, put, pup, ph, pbr, pbt, _ = [
                diff(*[n[f] for n in near]) * g_p if f != 7 else None for f in range(FIELDS)
            ]
            p_er = diff(*[n[2] * n[7] - n[3] * n[6] for n in near]) * g_p
            p_et = diff(*[n[3] * n[5] - n[1] * n[7] for n in near]) * g_p
            er = ut * bp - up * bt
            et = up * br - ur * bp
            ep = ur * bt - ut * br
            rq, rur, rut, rup, rh, rbt, rbp, r_et, r_ep = [d_r(x) for x in (q, ur, ut, up, h, bt, bp, et, ep)]

            div = rur + 2.0 * ur * inv_r + tut + cot_r * ut + pup
            cur_r = tbp + cot_r * bp - pbt
            cur_t = pbr - rbp - bp * inv_r
            cur_p = rbt + bt * inv_r - tbr
            sin_phi = phi_const[0, rows, :]
            cos_phi = phi_const[1, rows, :]
            w_r = (omega_y * sine) * sin_phi + omega_z * cosine
            w_t = (omega_y * cosine) * sin_phi - omega_z * sine
            w_p = omega_y * cos_phi
            inv_rho = jnp.exp(-q)
            temper = jnp.exp(h - q)

            def adv(gr, gt, gp):
                return ur * gr + ut * gt + up * gp

            rates = [
                -adv(rq, tq, pq) - div,
                -adv(rur, tur, pur)
                + (ut * ut + up * up) * inv_r
                - temper * rh
                + inv_rho * (cur_t * bp - cur_p * bt)
                - 2.0 * (w_t * up - w_p * ut)
                - gravity * inv_r * inv_r,
                -adv(rut, tut, put)
                - (ur * ut * inv_r - cot_r * (up * up))
                - temper * th
                + inv_rho * (cur_p * br - cur_r * bp)
                - 2.0 * (w_p * ur - w_r * up),
                -adv(rup, tup, pup)
                - (ur * up * inv_r + cot_r * (ut * up))
                - temper * ph
                + inv_rho * (cur_r * bt - cur_t * br)
                - 2.0 * (w_r * ut - w_t * ur),
                -adv(rh, th, ph) - gamma_ratio * div,
                t_ep + cot_r * ep - p_et,
                p_er - r_ep - ep * inv_r,
                r_et + et * inv_r - t_er,
            ]
            centre = [q, ur, ut, up, h, br, bt, bp]
            for f in range(FIELDS):
                if second:
                    new = 0.5 * (base[f, i, rows, :] + centre[f] + time_step * rates[f])
                else:
                    new = centre[f] + time_step * rates[f]
                updated[f, i, rows, :] = new
            return carry

        lax.fori_loop(0, COLS // 8, tile, 0)

    values = [
        jnp.dot(
            corner[...],
            updated[f].reshape(CELLS, SHELLS),
            precision=lax.Precision.HIGHEST,
            preferred_element_type=jnp.float32,
        )
        for f in range(FIELDS)
    ]
    c, s = angle[0], angle[1]
    for t, p in ((2, 3), (6, 7)):
        values[t], values[p] = c * values[t] - s * values[p], s * values[t] + c * values[p]
    donor[...] = jnp.swapaxes(jnp.stack(values), 0, 1)
    send[...] = jnp.zeros_like(send)

    def put(m, carry):
        send[place[m]] = donor[m]
        return carry

    lax.fori_loop(0, SLOTS, put, 0)


def merge_kernel(updated, moved, pick, mean, other, merged, gathered):
    start = other[0] * (DEVS * CAPACITY)
    gathered[...] = jnp.swapaxes(moved[pl.ds(start, DEVS * CAPACITY)], 0, 1)
    weight = mean[...]
    for f in range(FIELDS):
        v = gathered[f]
        high = v.astype(jnp.bfloat16)
        rest = v - high.astype(jnp.float32)
        middle = rest.astype(jnp.bfloat16)
        low = (rest - middle.astype(jnp.float32)).astype(jnp.bfloat16)
        total = sum(
            jnp.dot(pick[...], x, preferred_element_type=jnp.float32) for x in (low, middle, high)
        )
        kept = updated[f].reshape(CELLS, SHELLS)
        merged[f] = jnp.where(weight > 0.0, total * weight, kept).reshape(ROWS, COLS, SHELLS)


def params():
    return pltpu.CompilerParams(vmem_limit_bytes=48 * 1024 * 1024)


def run_step(second, args):
    return pl.pallas_call(
        lambda *refs: step_kernel(second, *refs),
        out_shape=(
            jax.ShapeDtypeStruct((FIELDS, ROWS, COLS, SHELLS), jnp.float32),
            jax.ShapeDtypeStruct((2 * DEVS * CAPACITY, FIELDS, SHELLS), jnp.float32),
        ),
        in_specs=[VMEM] * (6 if second else 5) + [SMEM] + [VMEM] * 4 + [SMEM],
        out_specs=(VMEM, VMEM),
        scratch_shapes=[
            pltpu.VMEM((FIELDS, ROWS, EXT, SHELLS), jnp.float32),
            pltpu.VMEM((SLOTS, FIELDS, SHELLS), jnp.float32),
        ],
        compiler_params=params(),
    )(*args)


def run_merge(*args):
    return pl.pallas_call(
        merge_kernel,
        out_shape=jax.ShapeDtypeStruct((FIELDS, ROWS, COLS, SHELLS), jnp.float32),
        in_specs=[VMEM] * 4 + [SMEM],
        out_specs=VMEM,
        scratch_shapes=[pltpu.VMEM((FIELDS, DEVS * CAPACITY, SHELLS), jnp.float32)],
        compiler_params=params(),
    )(*args)


def halos(x):
    up = [(i, i + 1) for i in range(N_THETA - 1)]
    down = [(j, i) for i, j in up]
    right = [(i, i + 1) for i in range(N_PHI - 1)]
    left = [(j, i) for i, j in right]
    above = lax.ppermute(x[:, ROWS - 2 :], "theta", up)
    below = lax.ppermute(x[:, :2], "theta", down)
    before = lax.ppermute(x[:, :, COLS - 2 :], "phi", right)
    after = lax.ppermute(x[:, :, :2], "phi", left)
    return above, below, before, after


def local(fields, donor_base, weights, frame_angle, destination, target_cell):
    own = fields[0]
    patch = lax.axis_index("patch")
    other = 1 - patch

    row_index = lax.axis_index("theta") * ROWS + jnp.arange(ROWS, dtype=jnp.int32)
    theta = 0.25 * math.pi - margin + (row_index.astype(jnp.float32) + 0.5) * THETA_STEP
    col_index = lax.axis_index("phi") * COLS + jnp.arange(COLS, dtype=jnp.int32)
    phi = -0.75 * math.pi - margin + (col_index.astype(jnp.float32) + 0.5) * PHI_STEP
    flag = patch.astype(jnp.float32)
    sine, cosine = jnp.sin(theta), jnp.cos(theta)
    ones = jnp.ones_like(sine)
    row_const = jnp.stack(
        [sine, cosine, cosine / sine, 1.0 / sine, ones * (rotation * flag), ones * (rotation * (1.0 - flag))], axis=1
    )
    phi_const = jnp.broadcast_to(jnp.stack([jnp.sin(phi), jnp.cos(phi)])[:, :, None], (2, COLS, SHELLS))
    radius = inner_radius + RADIAL_STEP * (jnp.arange(SHELLS, dtype=jnp.int32).astype(jnp.float32) + 0.5)
    inv_r = jnp.broadcast_to((1.0 / radius)[None, :], (8, SHELLS))

    base = donor_base[0, 0, 0]
    first = base // (COLS - 1) * COLS + base % (COLS - 1)
    w = weights[0, 0, 0]
    cells = jnp.arange(CELLS, dtype=jnp.int32)[None, :]
    corner = sum(
        jnp.where(cells == (first + offset)[:, None], w[k][:, None], 0.0)
        for k, offset in enumerate((0, 1, COLS, COLS + 1))
    )
    angle = frame_angle[0, 0, 0]
    angle = jnp.broadcast_to(jnp.stack([jnp.cos(angle), jnp.sin(angle)])[:, :, None], (2, SLOTS, SHELLS))
    receiver = destination[0, 0, 0]
    slot = jnp.arange(SLOTS, dtype=jnp.int32)
    rank = jnp.sum(
        ((receiver[:, None] == receiver[None, :]) & (slot[None, :] < slot[:, None])).astype(jnp.int32), axis=1
    )
    place = (other * DEVS + receiver) * CAPACITY + rank
    position = jnp.arange(2 * DEVS * CAPACITY, dtype=jnp.int32)
    cell_ids = target_cell[0, 0, 0]
    sent_ids = jnp.sum(jnp.where(position[:, None] == place[None, :], cell_ids[None, :] + 1, 0), axis=1) - 1
    sent_ids = jnp.broadcast_to(sent_ids.reshape(2 * DEVS, CAPACITY, 1), (2 * DEVS, CAPACITY, SHELLS))
    everyone = ("patch", "theta", "phi")
    got_ids = lax.all_to_all(sent_ids, everyone, 0, 0, tiled=True)[:, :, 0].reshape(2, DEVS * CAPACITY)
    got_ids = lax.dynamic_index_in_dim(got_ids, other, 0, keepdims=False)
    picked = got_ids[None, :] == jnp.arange(CELLS, dtype=jnp.int32)[:, None]
    pick = picked.astype(jnp.bfloat16)
    count = jnp.sum(picked.astype(jnp.float32), axis=1)
    mean = jnp.where(count > 0.0, 1.0 / jnp.maximum(count, 1.0), 0.0)
    mean = jnp.broadcast_to(mean[:, None], (CELLS, SHELLS))
    other_ref = other.astype(jnp.int32).reshape(1)

    def overset(updated, send):
        send = send.reshape(2 * DEVS, CAPACITY * FIELDS, SHELLS)
        moved = lax.all_to_all(send, everyone, 0, 0, tiled=True)
        moved = moved.reshape(2 * DEVS * CAPACITY, FIELDS, SHELLS)
        return run_merge(updated, moved, pick, mean, other_ref)

    tail = (row_const, phi_const, inv_r, corner, angle, place)
    one = overset(*run_step(False, (own, *halos(own), *tail)))
    two = overset(*run_step(True, (own, one, *halos(one), *tail)))
    return two[None]


def solution(mesh):
    placed = (
        P("patch", None, "theta", "phi", None),
        P("patch", "theta", "phi", None),
        P("patch", "theta", "phi", None, None),
        P("patch", "theta", "phi", None),
        P("patch", "theta", "phi", None),
        P("patch", "theta", "phi", None),
    )
    return jax.shard_map(
        local,
        mesh=mesh,
        in_specs=placed,
        out_specs=P("patch", None, "theta", "phi", None),
        check_vma=False,
    )
```

time: 429 us -> 258 us (0.60); the launches traced: 422 us -> 255 us
  other arithmetic: 123 us -> 2.94 us
  local copies, waits for them, and re-layouts: 78.3 us -> 14.9 us
  Pallas kernels: 0 us -> 32.5 us
  waiting for transfers between devices: 103 us -> 86.9 us
  between operations: 14.9 us -> 0.35 us
  blocking collectives: 49.4 us -> 63.8 us
    all_gather x2 -> x0, waiting for transfers between devices: 62.9 us -> none  [to_partner(): lax.all_gather(pair[0][None], 'patch', axis=0, tiled=True)]
    scatter-add x3 -> x0, other arithmetic: 58 us -> none  [the longest x2 55.7 us: overset(): summed = jnp.zeros((8, block_cells, shells), jnp.float32).at[:, cell_flat...]
    pallas_call x0 -> x4, Pallas kernels: none -> 32.5 us  [the longest x2 25.8 us: run_step(): pl.pallas_call(lambda *refs: step_kernel(second, *refs), out_shape=(jax.S...]
    ppermute x8, waiting for transfers between devices: 15.7 us -> 41 us  [the longest x2 37.5 us: halos(): below = lax.ppermute(x[:, :2], 'theta', down)]
    all_to_all x2, waiting for transfers between devices: 24.5 us -> 45.9 us  [the longest x1 45.9 us: overset(): moved = lax.all_to_all(send, everyone, 0, 0, tiled=True)]
    all_to_all x1, blocking collectives: 45.1 us -> 63.8 us  [overset(): moved = lax.all_to_all(send, everyone, 0, 0, tiled=True)]
    another operation x10 -> x4, local copies, waits for them, and re-layouts: 18.1 us -> 0.25 us  [the longest x1 0.14 us: local(): lax.all_to_all(sent_ids, everyone, 0, 0, tiled=True)[:, :, 0]]
    gather x8 -> x0, local copies, waits for them, and re-layouts: 16.9 us -> none  [the longest x2 4.83 us: overset(): jnp.take(flat_fields, corner + cols_dev, axis=1)]
  transfers between devices with their start and end apart: 12 -> 10, of which waited for: 7 -> 6; matrix products, arithmetic and copies ran while one was open for 13% -> 5% of each run, Pallas kernels for 0% -> 5%
where the time goes in v1:
time: 258 us; the launch traced here: 255 us
  waiting for transfers between devices  86.9 us (34%)
  blocking collectives  63.8 us (25%)
  starting transfers between devices  53.8 us (21%)
  Pallas kernels  32.5 us (13%)
  local copies, waits for them, and re-layouts  14.9 us (6%)
  other arithmetic  2.94 us (1%)
    all_to_all x1, blocking collectives, overset(): moved = lax.all_to_all(send, everyone, 0, 0, tiled=True)  63.8 us
    all_to_all x1, waiting for transfers between devices, overset(): moved = lax.all_to_all(send, everyone, 0, 0, tiled=True)  45.9 us
    ppermute x2, waiting for transfers between devices, halos(): below = lax.ppermute(x[:, :2], 'theta', down)  37.5 us
    pallas_call x2, Pallas kernels, run_step(): pl.pallas_call(lambda *refs: step_kernel(second, *refs), out_shape=(jax.S...  25.8 us
    all_to_all x1, starting transfers between devices, overset(): moved = lax.all_to_all(send, everyone, 0, 0, tiled=True)  17.6 us
    all_to_all x1, starting transfers between devices, local(): lax.all_to_all(sent_ids, everyone, 0, 0, tiled=True)[:, :, 0]  15.3 us
    ppermute x2, starting transfers between devices, halos(): below = lax.ppermute(x[:, :2], 'theta', down)  8.3 us
    pallas_call x2, Pallas kernels, run_merge(): pl.pallas_call(merge_kernel, out_shape=jax.ShapeDtypeStruct((FIELDS, ROWS...  6.72 us
  transfers between devices with their start and end apart: 10, of which 6 were waited for; matrix products, arithmetic and copies ran while one was open for 5% of the time, Pallas kernels for 5%

profile of v1, /device:TPU:2, one launch (start us, length us, event | category | flops | bytes accessed | tf_op | source)
XLA Modules:
  0.0 255.2 jit_solution(13172704402770370807)
XLA Ops:
  0.0 1.0 fusion.12
  1.0 1.3 collective-permute-start.3
  2.3 3.0 %collective-permute-start.2 = (f32[8,4,2,128]{3,2,1,0:T(2,128)S(1)}, f32[8,4,2,128]{3,2,1,0:T(2,128)S(1)}, u32[]{:S(2)}, u32[]{:S(2)}) collective-permute-start(f32[8,4,2,128]{3,2,1,0:T(2,128)S(1)} %get-tuple-element.20), channel_id=1, source_target_pairs={{0,1},{1,2},{2,3},{4,5},{5,6},{6,7},{8,9},{9,10},{10,11},{12,13},{... | collective-permute-start | bytes 98312 | tf_op jit(solution)/shard_map/ppermute | solution.py:227
  5.3 0.7 add_bitcast_fusion
  6.0 0.9 convert_reduce_fusion.1
  6.9 0.7 multiply_add_fusion.1.refs_10_.refs_11_
  7.6 0.1 select_reduce_fusion
  7.7 0.1 sub.22
  7.9 1.0 broadcast_in_dim.111
  8.9 15.3 %all-to-all-start.1 = ((s32[256,2,128]{2,1,0:T(2,128)}), s32[256,2,128]{2,1,0:T(2,128)S(1)}, u32[]{:S(2)}, u32[]{:S(2)}) async-start(s32[256,2,128]{2,1,0:T(2,128)} %broadcast_in_dim.111), calls=%async_computation.1 | async-start | bytes 524288 | tf_op jit(solution)/shard_map/all_to_all | solution.py:272
  24.2 0.0 copy-start.6
  24.2 0.0 copy-start.7
  24.2 0.0 copy-start.5
  24.2 3.1 %fusion.13 = (f32[8,2,128,128]{3,2,1,0:T(8,128)}, f32[8,2,128,128]{3,2,1,0:T(8,128)}) fusion(f32[8,4,128,128]{3,2,1,0:T(8,128)} %bitcast.44), kind=kLoop, calls=%fused_computation.46 | loop fusion | bytes 4194304 | tf_op jit(solution)/shard_map/slice | solution.py:226
  27.3 4.0 %collective-permute-start.1 = (f32[8,2,128,128]{3,2,1,0:T(8,128)}, f32[8,2,128,128]{3,2,1,0:T(8,128)S(1)}, u32[]{:S(2)}, u32[]{:S(2)}) collective-permute-start(f32[8,2,128,128]{3,2,1,0:T(8,128)} %get-tuple-element.21), channel_id=1, source_target_pairs={{4,0},{8,4},{12,8},{16,12},{20,16},{24,20},{28,24},{32,28},{36,32}... | collective-permute-start | bytes 3145736 | tf_op jit(solution)/shard_map/ppermute | solution.py:226
  31.3 1.9 collective-permute-start
  33.3 0.1 broadcast_divide_fusion
  33.4 0.0 copy-done.6
  33.5 0.0 copy-done.7
  33.6 0.0 copy-done.5
  33.6 0.2 select_add_fusion.refs_8_.refs_9_
  33.8 0.1 stack.12.refs_5_.refs_6_
  33.9 0.0 collective-permute-done.3.refs_4_
  33.9 0.0 collective-permute-done.2.refs_3_
  33.9 21.5 %collective-permute-done.1.refs_2_ = f32[8,2,128,128]{3,2,1,0:T(8,128)S(1)} collective-permute-done((f32[8,2,128,128]{3,2,1,0:T(8,128)}, f32[8,2,128,128]{3,2,1,0:T(8,128)S(1)}, u32[]{:S(2)}, u32[]{:S(2)}) %collective-permute-start.1) | collective-permute-done | bytes 1048608 | tf_op jit(solution)/shard_map/ppermute | solution.py:226
  55.4 0.0 copy-start.1
  55.5 1.0 copy-done.1
  56.4 0.2 collective-permute-done.refs_1_
  56.7 0.0 copy-start.3
  56.7 1.0 copy-done.3
  57.6 0.1 broadcast_in_dim.108.refs_9_.refs_10_
  57.7 0.1 broadcast_in_dim.97.refs_6_.refs_7_
  57.8 0.0 copy-start.2
  57.8 1.2 copy-done.2
  59.1 0.0 copy-start.4
  59.1 1.2 copy-done.4
  60.3 12.4 %shard_map.64 = (f32[8,4,128,128]{3,2,1,0:T(8,128)S(1)}, f32[512,8,128]{2,1,0:T(8,128)}) custom-call(f32[8,4,128,128]{3,2,1,0:T(8,128)} %bitcast.45, f32[8,2,128,128]{3,2,1,0:T(8,128)S(1)} %copy-done.4, f32[8,2,128,128]{3,2,1,0:T(8,128)S(1)} %copy-done.2, f32[8,4,2,128]{3,2,1,0:T(2,128)S(1)} %collective-permute-done.2.refs_3_, ...), custom_call_target="tpu_custom_call" | custom-call | tf_op jit(solution)/shard_map/pallas_call | solution.py:193
  72.7 0.0 all-to-all-done.1
  72.7 17.6 %all-to-all-start = ((f32[256,16,128]{2,1,0:T(8,128)}), f32[256,16,128]{2,1,0:T(8,128)}, u32[]{:S(2)}, u32[]{:S(2)}) async-start(f32[256,16,128]{2,1,0:T(8,128)} %bitcast.47), calls=%async_computation | async-start | bytes 4194304 | tf_op jit(solution)/shard_map/all_to_all | solution.py:283
  90.4 4.4 %slice_reduce_fusion = s32[256,2]{1,0:T(8,128)S(1)} fusion(s32[256,2,128]{2,1,0:T(2,128)S(1)} %all-to-all-done.1), kind=kLoop, calls=%fused_computation.3 | loop fusion | bytes 4096 | tf_op jit(solution)/shard_map/slice | solution.py:272
  94.8 0.1 reshape_squeeze.3
  94.9 0.1 convert_reduce_fusion
  95.1 0.1 fusion.pick
  95.2 45.9 %all-to-all-done = f32[256,16,128]{2,1,0:T(8,128)} async-done(((f32[256,16,128]{2,1,0:T(8,128)}), f32[256,16,128]{2,1,0:T(8,128)}, u32[]{:S(2)}, u32[]{:S(2)}) %all-to-all-start) | async-done | bytes 2097184 | tf_op jit(solution)/shard_map/all_to_all | solution.py:283
  141.1 0.1 broadcast_in_dim.112.mean
  141.2 3.5 %shard_map.65.refs_1_ = f32[8,4,128,128]{3,2,1,0:T(8,128)S(1)} custom-call(f32[8,4,128,128]{3,2,1,0:T(8,128)S(1)} %get-tuple-element.9.updated, f32[512,8,128]{2,1,0:T(8,128)} %bitcast.12.moved, bf16[512,256]{1,0:T(8,128)(2,1)S(1)} %fusion.pick, f32[512,128]{1,0:T(8,128)S(1)} %broadcast_in_dim.112.mean, s32[1]{0:T(128)} %bitcast.15.other), custom_call_target="tpu_custom_call" | custom-call | tf_op jit(solution)/shard_map/pallas_call | solution.py:210
  144.7 0.0 copy-start
  144.7 0.2 fusion.11
  144.9 4.3 %collective-permute-start.5 = (f32[8,2,128,128]{3,2,1,0:T(8,128)S(1)}, f32[8,2,128,128]{3,2,1,0:T(8,128)S(1)}, u32[]{:S(2)}, u32[]{:S(2)}) collective-permute-start(f32[8,2,128,128]{3,2,1,0:T(8,128)S(1)} %get-tuple-element.17), channel_id=1, source_target_pairs={{4,0},{8,4},{12,8},{16,12},{20,16},{24,20},{28,24},{32,28},{36,32}... | collective-permute-start | bytes 3145736 | tf_op jit(solution)/shard_map/ppermute | solution.py:226
  149.1 1.9 collective-permute-start.4
  151.1 0.0 copy-done
  151.1 1.3 collective-permute-start.7
  152.4 3.2 %collective-permute-start.6 = (f32[8,4,2,128]{3,2,1,0:T(2,128)S(1)}, f32[8,4,2,128]{3,2,1,0:T(2,128)S(1)}, u32[]{:S(2)}, u32[]{:S(2)}) collective-permute-start(f32[8,4,2,128]{3,2,1,0:T(2,128)S(1)} %get-tuple-element.16), channel_id=1, source_target_pairs={{0,1},{1,2},{2,3},{4,5},{5,6},{6,7},{8,9},{9,10},{10,11},{12,13},{... | collective-permute-start | bytes 98312 | tf_op jit(solution)/shard_map/ppermute | solution.py:227
  155.6 0.0 collective-permute-done.7.refs_5_
  155.6 0.6 collective-permute-done.6.refs_4_
  156.3 16.0 %collective-permute-done.5.refs_3_ = f32[8,2,128,128]{3,2,1,0:T(8,128)S(1)} collective-permute-done((f32[8,2,128,128]{3,2,1,0:T(8,128)S(1)}, f32[8,2,128,128]{3,2,1,0:T(8,128)S(1)}, u32[]{:S(2)}, u32[]{:S(2)}) %collective-permute-start.5) | collective-permute-done | bytes 1048608 | tf_op jit(solution)/shard_map/ppermute | solution.py:226
  172.3 2.6 %collective-permute-done.4.refs_2_ = f32[8,2,128,128]{3,2,1,0:T(8,128)S(1)} collective-permute-done((f32[8,2,128,128]{3,2,1,0:T(8,128)S(1)}, f32[8,2,128,128]{3,2,1,0:T(8,128)S(1)}, u32[]{:S(2)}, u32[]{:S(2)}) %collective-permute-start.4) | collective-permute-done | bytes 1048608 | tf_op jit(solution)/shard_map/ppermute | solution.py:225
  174.9 13.3 %shard_map.66 = (f32[8,4,128,128]{3,2,1,0:T(8,128)S(1)}, f32[512,8,128]{2,1,0:T(8,128)}) custom-call(f32[8,4,128,128]{3,2,1,0:T(8,128)} %bitcast.46, f32[8,4,128,128]{3,2,1,0:T(8,128)} %copy-done, f32[8,2,128,128]{3,2,1,0:T(8,128)S(1)} %collective-permute-done.4.refs_2_, f32[8,2,128,128]{3,2,1,0:T(8,128)S(1)} %collective-permute-done.5.refs_3_, ...), custom_call_target="tpu_custom_call" | custom-call | tf_op jit(solution)/shard_map/pallas_call | solution.py:193
  188.2 63.8 %all_to_all.15 = f32[256,16,128]{2,1,0:T(8,128)S(1)} all-to-all(f32[256,16,128]{2,1,0:T(8,128)} %bitcast.48), channel_id=1, replica_groups=mesh['patch'=2,'theta'=32,'phi'=4] {'patch','theta','phi'}, dimensions={0} | all-to-all | bytes 4194304 | tf_op jit(solution)/shard_map/all_to_all | solution.py:283
  252.0 3.2 %shard_map.67 = f32[8,4,128,128]{3,2,1,0:T(8,128)} custom-call(f32[8,4,128,128]{3,2,1,0:T(8,128)S(1)} %get-tuple-element.11.updated, f32[512,8,128]{2,1,0:T(8,128)S(1)} %bitcast.42, bf16[512,256]{1,0:T(8,128)(2,1)S(1)} %fusion.pick, f32[512,128]{1,0:T(8,128)S(1)} %broadcast_in_dim.112.mean, s32[1]{0:T(128)} %bitcast.15.other), custom_call_target="tpu_custom_call" | custom-call | tf_op jit(solution)/shard_map/pallas_call | solution.py:210
  (16 shorter events, 0.3 us)
Async XLA Ops:
  1.0 32.9 %collective-permute-start.3 = (f32[8,4,2,128]{3,2,1,0:T(2,128)S(1)}, f32[8,4,2,128]{3,2,1,0:T(2,128)S(1)}, u32[]{:S(2)}, u32[]{:S(2)}) collective-permute-start(f32[8,4,2,128]{3,2,1,0:T(2,128)S(1)} %get-tuple-element.19), channel_id=1, source_target_pairs={{1,0},{2,1},{3,2},{5,4},{6,5},{7,6},{9,8},{10,9},{11,10},{13,12},{... | collective-permute-start | bytes 98312 | tf_op jit(solution)/shard_map/ppermute | solution.py:228
  2.3 31.6 %collective-permute-start.2 = (f32[8,4,2,128]{3,2,1,0:T(2,128)S(1)}, f32[8,4,2,128]{3,2,1,0:T(2,128)S(1)}, u32[]{:S(2)}, u32[]{:S(2)}) collective-permute-start(f32[8,4,2,128]{3,2,1,0:T(2,128)S(1)} %get-tuple-element.20), channel_id=1, source_target_pairs={{0,1},{1,2},{2,3},{4,5},{5,6},{6,7},{8,9},{9,10},{10,11},{12,13},{... | collective-permute-start | bytes 98312 | tf_op jit(solution)/shard_map/ppermute | solution.py:227
  8.9 63.8 %all-to-all-start.1 = ((s32[256,2,128]{2,1,0:T(2,128)}), s32[256,2,128]{2,1,0:T(2,128)S(1)}, u32[]{:S(2)}, u32[]{:S(2)}) async-start(s32[256,2,128]{2,1,0:T(2,128)} %broadcast_in_dim.111), calls=%async_computation.1 | async-start | bytes 524288 | tf_op jit(solution)/shard_map/all_to_all | solution.py:272
  24.2 9.3 %copy-start.6 = (f32[1,1,1,96]{3,2,1,0:T(1,128)S(1)}, f32[1,1,1,96]{3,2,1,0:T(1,128)}, u32[]{:S(2)}) copy-start(f32[1,1,1,96]{3,2,1,0:T(1,128)} %param.9) | copy-start | bytes 1156
  24.2 9.4 %copy-start.7 = (s32[1,1,1,96]{3,2,1,0:T(1,128)S(1)}, s32[1,1,1,96]{3,2,1,0:T(1,128)}, u32[]{:S(2)}) copy-start(s32[1,1,1,96]{3,2,1,0:T(1,128)} %param.7) | copy-start | bytes 1156
  24.2 9.4 %copy-start.5 = (f32[1,1,1,4,96]{4,3,2,1,0:T(4,128)S(1)}, f32[1,1,1,4,96]{4,3,2,1,0:T(4,128)}, u32[]{:S(2)}) copy-start(f32[1,1,1,4,96]{4,3,2,1,0:T(4,128)} %param.8) | copy-start | bytes 4612
  27.3 28.1 %collective-permute-start.1 = (f32[8,2,128,128]{3,2,1,0:T(8,128)}, f32[8,2,128,128]{3,2,1,0:T(8,128)S(1)}, u32[]{:S(2)}, u32[]{:S(2)}) collective-permute-start(f32[8,2,128,128]{3,2,1,0:T(8,128)} %get-tuple-element.21), channel_id=1, source_target_pairs={{4,0},{8,4},{12,8},{16,12},{20,16},{24,20},{28,24},{32,28},{36,32}... | collective-permute-start | bytes 3145736 | tf_op jit(solution)/shard_map/ppermute | solution.py:226
  31.3 25.3 %collective-permute-start = (f32[8,2,128,128]{3,2,1,0:T(8,128)}, f32[8,2,128,128]{3,2,1,0:T(8,128)S(1)}, u32[]{:S(2)}, u32[]{:S(2)}) collective-permute-start(f32[8,2,128,128]{3,2,1,0:T(8,128)} %get-tuple-element.22), channel_id=1, source_target_pairs={{0,4},{4,8},{8,12},{12,16},{16,20},{20,24},{24,28},{28,32},{32,36}... | collective-permute-start | bytes 3145736 | tf_op jit(solution)/shard_map/ppermute | solution.py:225
  55.4 1.0 copy-start.1
  56.7 1.0 copy-start.3
  57.8 1.2 copy-start.2
  59.1 1.2 copy-start.4
  72.7 68.3 %all-to-all-start = ((f32[256,16,128]{2,1,0:T(8,128)}), f32[256,16,128]{2,1,0:T(8,128)}, u32[]{:S(2)}, u32[]{:S(2)}) async-start(f32[256,16,128]{2,1,0:T(8,128)} %bitcast.47), calls=%async_computation | async-start | bytes 4194304 | tf_op jit(solution)/shard_map/all_to_all | solution.py:283
  144.7 6.4 %copy-start = (f32[8,4,128,128]{3,2,1,0:T(8,128)}, f32[8,4,128,128]{3,2,1,0:T(8,128)S(1)}, u32[]{:S(2)}) copy-start(f32[8,4,128,128]{3,2,1,0:T(8,128)S(1)} %shard_map.65.refs_1_) | copy-start | bytes 6291460
  144.9 27.4 %collective-permute-start.5 = (f32[8,2,128,128]{3,2,1,0:T(8,128)S(1)}, f32[8,2,128,128]{3,2,1,0:T(8,128)S(1)}, u32[]{:S(2)}, u32[]{:S(2)}) collective-permute-start(f32[8,2,128,128]{3,2,1,0:T(8,128)S(1)} %get-tuple-element.17), channel_id=1, source_target_pairs={{4,0},{8,4},{12,8},{16,12},{20,16},{24,20},{28,24},{32,28},{36,32}... | collective-permute-start | bytes 3145736 | tf_op jit(solution)/shard_map/ppermute | solution.py:226
  149.1 25.8 %collective-permute-start.4 = (f32[8,2,128,128]{3,2,1,0:T(8,128)S(1)}, f32[8,2,128,128]{3,2,1,0:T(8,128)S(1)}, u32[]{:S(2)}, u32[]{:S(2)}) collective-permute-start(f32[8,2,128,128]{3,2,1,0:T(8,128)S(1)} %get-tuple-element.18), channel_id=1, source_target_pairs={{0,4},{4,8},{8,12},{12,16},{16,20},{20,24},{24,28},{28,32},{32,36}... | collective-permute-start | bytes 3145736 | tf_op jit(solution)/shard_map/ppermute | solution.py:225
  151.1 4.5 %collective-permute-start.7 = (f32[8,4,2,128]{3,2,1,0:T(2,128)S(1)}, f32[8,4,2,128]{3,2,1,0:T(2,128)S(1)}, u32[]{:S(2)}, u32[]{:S(2)}) collective-permute-start(f32[8,4,2,128]{3,2,1,0:T(2,128)S(1)} %get-tuple-element.15), channel_id=1, source_target_pairs={{1,0},{2,1},{3,2},{5,4},{6,5},{7,6},{9,8},{10,9},{11,10},{13,12},{... | collective-permute-start | bytes 98312 | tf_op jit(solution)/shard_map/ppermute | solution.py:228
  152.4 3.9 %collective-permute-start.6 = (f32[8,4,2,128]{3,2,1,0:T(2,128)S(1)}, f32[8,4,2,128]{3,2,1,0:T(2,128)S(1)}, u32[]{:S(2)}, u32[]{:S(2)}) collective-permute-start(f32[8,4,2,128]{3,2,1,0:T(2,128)S(1)} %get-tuple-element.16), channel_id=1, source_target_pairs={{0,1},{1,2},{2,3},{4,5},{5,6},{6,7},{8,9},{9,10},{10,11},{12,13},{... | collective-permute-start | bytes 98312 | tf_op jit(solution)/shard_map/ppermute | solution.py:227

commit v2 on v1

v2 whole, which is shorter than its diff:
```python
import math

import jax
import jax.numpy as jnp
from jax import lax
from jax.experimental import pallas as pl
from jax.experimental.pallas import tpu as pltpu
from jax.sharding import PartitionSpec as P

margin = 0.03
inner_radius = 0.35
outer_radius = 1.0
gamma_ratio = 5.0 / 3.0
gravity = 1.0
rotation = 2.0
time_step = 0.002

ROWS, COLS, SHELLS, FIELDS, SLOTS = 4, 128, 128, 8, 96
HALF = ROWS // 2
CELLS = ROWS * COLS
N_THETA, N_PHI = 32, 4
DEVS = N_THETA * N_PHI
PAD = 8
EXT = COLS + 2 * PAD
THETA_STEP = (0.5 * math.pi + 2.0 * margin) / (ROWS * N_THETA)
PHI_STEP = (1.5 * math.pi + 2.0 * margin) / (COLS * N_PHI)
RADIAL_STEP = (outer_radius - inner_radius) / SHELLS
VMEM = pl.BlockSpec(memory_space=pltpu.VMEM)
SMEM = pl.BlockSpec(memory_space=pltpu.SMEM)
ANY = pl.BlockSpec(memory_space=pl.ANY)
EVERYONE = ("patch", "theta", "phi")


def struct(*shape):
    return jax.ShapeDtypeStruct(shape, jnp.float32)


HALF_BLOCK = (FIELDS, HALF, COLS, SHELLS)
RIM = (FIELDS, 8, SHELLS)


def params(mib):
    return pltpu.CompilerParams(vmem_limit_bytes=mib * 1024 * 1024)


def store_rims(top, bottom, west, east):
    for f in range(FIELDS):
        for i in range(ROWS):
            ref = (top, bottom)[i // HALF]
            west[f, 2 * i : 2 * i + 2, :] = ref[f, i % HALF, :2, :]
            east[f, 2 * i : 2 * i + 2, :] = ref[f, i % HALF, COLS - 2 :, :]


def split_kernel(fields, top, bottom, west, east, sems):
    copies = [
        pltpu.make_async_copy(fields.at[:, :HALF], top, sems.at[0]),
        pltpu.make_async_copy(fields.at[:, HALF:], bottom, sems.at[1]),
    ]
    for copy in copies:
        copy.start()
    for copy in copies:
        copy.wait()
    store_rims(top, bottom, west, east)


def run_split(fields):
    return pl.pallas_call(
        split_kernel,
        out_shape=(struct(*HALF_BLOCK), struct(*HALF_BLOCK), struct(*RIM), struct(*RIM)),
        in_specs=[ANY],
        out_specs=(VMEM,) * 4,
        scratch_shapes=[pltpu.SemaphoreType.DMA((2,))],
        compiler_params=params(16),
    )(fields)


def diff(far_low, near_low, near_high, far_high):
    return (far_low - far_high) + 8.0 * (near_high - near_low)


def step_kernel(second, *refs):
    if second:
        base_hbm, fix_above, fix_below, *refs = refs
    (
        top, bottom, above, below, before, after, edge, row_const, phi_const, inv_r_ref, corner, angle, place,
        new_top, new_bottom, send, ext, donor, base, sems,
    ) = refs
    inside = pl.ds(PAD, COLS)
    copies = [
        pltpu.make_async_copy(ref, ext.at[:, start : start + HALF, inside], sems.at[n])
        for n, (ref, start) in enumerate(((above, 0), (top, 2), (bottom, 4), (below, 6)))
    ]
    if second:
        copies.append(pltpu.make_async_copy(base_hbm, base, sems.at[4]))
    for copy in copies:
        copy.start()
    send[...] = jnp.zeros_like(send)
    west_edge, east_edge = edge[2] > 0, edge[3] > 0
    for f in range(FIELDS):
        for i in range(ROWS):
            pair = slice(2 * i, 2 * i + 2)
            ext[f, 2 + i, PAD - 2 : PAD, :] = jnp.where(west_edge, 0.0, before[f, pair, :])
            ext[f, 2 + i, PAD + COLS : PAD + COLS + 2, :] = jnp.where(east_edge, 0.0, after[f, pair, :])
    for copy in copies:
        copy.wait()
    if second:
        for f in range(FIELDS):
            for i in range(HALF):
                for start, ref in ((0, fix_above), (6, fix_below)):
                    ext[f, start + i, PAD : PAD + 2, :] = ref[f, 4 * i : 4 * i + 2, :]
                    ext[f, start + i, PAD + COLS - 2 : PAD + COLS, :] = ref[f, 4 * i + 2 : 4 * i + 4, :]

    @pl.when(edge[0] > 0)
    def _():
        ext[:, 0:HALF] = jnp.zeros((FIELDS, HALF, EXT, SHELLS), jnp.float32)

    @pl.when(edge[1] > 0)
    def _():
        ext[:, 6 : 6 + HALF] = jnp.zeros((FIELDS, HALF, EXT, SHELLS), jnp.float32)

    lane = lax.broadcasted_iota(jnp.int32, (8, SHELLS), 1)
    first, second_lane = lane < 1, lane < 2
    last, before_last = lane > SHELLS - 2, lane > SHELLS - 3
    inv_r = inv_r_ref[...]
    k_r = 1.0 / (12.0 * RADIAL_STEP)
    g_t = inv_r * (1.0 / (12.0 * THETA_STEP))

    def d_r(x):
        near_low = jnp.where(first, x, pltpu.roll(x, 1, 1))
        far_low = jnp.where(second_lane, near_low, pltpu.roll(x, 2, 1))
        near_high = jnp.where(last, x, pltpu.roll(x, SHELLS - 1, 1))
        far_high = jnp.where(before_last, near_high, pltpu.roll(x, SHELLS - 2, 1))
        return diff(far_low, near_low, near_high, far_high) * k_r

    for i in range(ROWS):
        sine, cosine, cot, inv_sine = [row_const[i, k] for k in range(4)]
        omega_y, omega_z = row_const[i, 4], row_const[i, 5]
        g_p = inv_r * (inv_sine * (1.0 / (12.0 * PHI_STEP)))
        cot_r = inv_r * cot
        out = (new_top, new_bottom)[i // HALF]

        def tile(j, carry):
            start = pl.multiple_of(j * 8, 8)
            rows = pl.ds(start, 8)
            padded = pl.ds(pl.multiple_of(start + PAD, 8), 8)
            q, ur, ut, up, h, br, bt, bp = [ext[f, 2 + i, padded, :] for f in range(FIELDS)]
            near = [[ext[f, 2 + i + d, padded, :] for f in range(FIELDS)] for d in (-2, -1, 1, 2)]
            tq, tur, tut, tup, th, tbr, _, tbp = [
                diff(*[n[f] for n in near]) * g_t if f != 6 else None for f in range(FIELDS)
            ]
            t_er = diff(*[n[2] * n[7] - n[3] * n[6] for n in near]) * g_t
            t_ep = diff(*[n[1] * n[6] - n[2] * n[5] for n in near]) * g_t
            near = [[ext[f, 2 + i, pl.ds(start + (PAD + d), 8), :] for f in range(FIELDS)] for d in (-2, -1, 1, 2)]
            pq, pur, put, pup, ph, pbr, pbt, _ = [
                diff(*[n[f] for n in near]) * g_p if f != 7 else None for f in range(FIELDS)
            ]
            p_er = diff(*[n[2] * n[7] - n[3] * n[6] for n in near]) * g_p
            p_et = diff(*[n[3] * n[5] - n[1] * n[7] for n in near]) * g_p
            er = ut * bp - up * bt
            et = up * br - ur * bp
            ep = ur * bt - ut * br
            rq, rur, rut, rup, rh, rbt, rbp, r_et, r_ep = [d_r(x) for x in (q, ur, ut, up, h, bt, bp, et, ep)]

            div = rur + 2.0 * ur * inv_r + tut + cot_r * ut + pup
            cur_r = tbp + cot_r * bp - pbt
            cur_t = pbr - rbp - bp * inv_r
            cur_p = rbt + bt * inv_r - tbr
            sin_phi = phi_const[0, rows, :]
            cos_phi = phi_const[1, rows, :]
            w_r = (omega_y * sine) * sin_phi + omega_z * cosine
            w_t = (omega_y * cosine) * sin_phi - omega_z * sine
            w_p = omega_y * cos_phi
            inv_rho = jnp.exp(-q)
            temper = jnp.exp(h - q)

            def adv(gr, gt, gp):
                return ur * gr + ut * gt + up * gp

            rates = [
                -adv(rq, tq, pq) - div,
                -adv(rur, tur, pur)
                + (ut * ut + up * up) * inv_r
                - temper * rh
                + inv_rho * (cur_t * bp - cur_p * bt)
                - 2.0 * (w_t * up - w_p * ut)
                - gravity * inv_r * inv_r,
                -adv(rut, tut, put)
                - (ur * ut * inv_r - cot_r * (up * up))
                - temper * th
                + inv_rho * (cur_p * br - cur_r * bp)
                - 2.0 * (w_p * ur - w_r * up),
                -adv(rup, tup, pup)
                - (ur * up * inv_r + cot_r * (ut * up))
                - temper * ph
                + inv_rho * (cur_r * bt - cur_t * br)
                - 2.0 * (w_r * ut - w_t * ur),
                -adv(rh, th, ph) - gamma_ratio * div,
                t_ep + cot_r * ep - p_et,
                p_er - r_ep - ep * inv_r,
                r_et + et * inv_r - t_er,
            ]
            centre = [q, ur, ut, up, h, br, bt, bp]
            for f in range(FIELDS):
                if second:
                    new = 0.5 * (base[f, i, rows, :] + centre[f] + time_step * rates[f])
                else:
                    new = centre[f] + time_step * rates[f]
                out[f, i % HALF, rows, :] = new
            return carry

        lax.fori_loop(0, COLS // 8, tile, 0)

    def product(f):
        total = None
        for n, ref in enumerate((new_top, new_bottom)):
            part = jnp.dot(
                corner[:, n * HALF * COLS : (n + 1) * HALF * COLS],
                ref[f].reshape(HALF * COLS, SHELLS),
                precision=lax.Precision.HIGHEST,
                preferred_element_type=jnp.float32,
            )
            total = part if total is None else total + part
        return total

    values = [product(f) for f in range(FIELDS)]
    c, s = angle[0], angle[1]
    for t, p in ((2, 3), (6, 7)):
        values[t], values[p] = c * values[t] - s * values[p], s * values[t] + c * values[p]
    donor[...] = jnp.swapaxes(jnp.stack(values), 0, 1)

    def put(m, carry):
        for k in range(8):
            send[place[8 * m + k]] = donor[8 * m + k]
        return carry

    lax.fori_loop(0, SLOTS // 8, put, 0)


def run_step(second, args):
    return pl.pallas_call(
        lambda *refs: step_kernel(second, *refs),
        out_shape=(struct(*HALF_BLOCK), struct(*HALF_BLOCK), struct(2 * DEVS, FIELDS, SHELLS)),
        in_specs=([ANY, VMEM, VMEM] if second else []) + [VMEM] * 6 + [SMEM] * 2 + [VMEM] * 4 + [SMEM],
        out_specs=(VMEM,) * 3,
        scratch_shapes=[
            pltpu.VMEM((FIELDS, ROWS + 4, EXT, SHELLS), jnp.float32),
            pltpu.VMEM((SLOTS, FIELDS, SHELLS), jnp.float32),
            pltpu.VMEM((FIELDS, ROWS if second else 1, COLS, SHELLS), jnp.float32),
            pltpu.SemaphoreType.DMA((5,)),
        ],
        compiler_params=params(24),
    )(*args)


def merge_kernel(last, top, bottom, direct, mate, early, late, pick, mean, edge, *refs):
    if last:
        merged, gathered = refs
    else:
        new_top, new_bottom, west, east, head, foot, gathered = refs
    gathered[:, :DEVS, :] = jnp.swapaxes(direct[...], 0, 1)
    on_edge = edge[0] + edge[1] > 0

    @pl.when(on_edge)
    def _():
        gathered[:, DEVS : DEVS + DEVS // 2, :] = jnp.swapaxes(early[...], 0, 1)
        gathered[:, DEVS + DEVS // 2 :, :] = jnp.swapaxes(late[...], 0, 1)

    @pl.when(jnp.logical_not(on_edge))
    def _():
        gathered[:, DEVS:, :] = jnp.swapaxes(mate[...], 0, 1)

    weight = mean[...]
    for f in range(FIELDS):
        v = gathered[f]
        high = v.astype(jnp.bfloat16)
        rest = v - high.astype(jnp.float32)
        middle = rest.astype(jnp.bfloat16)
        low = (rest - middle.astype(jnp.float32)).astype(jnp.bfloat16)
        total = sum(jnp.dot(pick[...], x, preferred_element_type=jnp.float32) for x in (low, middle, high))
        for n, ref in enumerate((top, bottom)):
            part = slice(n * HALF * COLS, (n + 1) * HALF * COLS)
            kept = ref[f].reshape(HALF * COLS, SHELLS)
            result = jnp.where(weight[part] > 0.0, total[part] * weight[part], kept).reshape(HALF, COLS, SHELLS)
            if last:
                merged[f, n * HALF : (n + 1) * HALF] = result
            else:
                (new_top, new_bottom)[n][f] = result
    if not last:
        store_rims(new_top, new_bottom, west, east)
        for f in range(FIELDS):
            for i in range(HALF):
                for ref, fix in ((new_top, head), (new_bottom, foot)):
                    fix[f, 4 * i : 4 * i + 2, :] = ref[f, i, :2, :]
                    fix[f, 4 * i + 2 : 4 * i + 4, :] = ref[f, i, COLS - 2 :, :]


def run_merge(last, *args):
    if last:
        shapes = (struct(FIELDS, ROWS, COLS, SHELLS),)
    else:
        shapes = (struct(*HALF_BLOCK),) * 2 + (struct(*RIM),) * 4
    return pl.pallas_call(
        lambda *refs: merge_kernel(last, *refs),
        out_shape=shapes,
        in_specs=[VMEM] * 8 + [SMEM],
        out_specs=(VMEM,) * len(shapes),
        scratch_shapes=[pltpu.VMEM((FIELDS, 2 * DEVS, SHELLS), jnp.float32)],
        compiler_params=params(16),
    )(*args)


def shift(x, axis, size, by):
    return lax.ppermute(x, axis, [(i, (i + by) % size) for i in range(size)])


def local(fields, donor_base, weights, frame_angle, destination, target_cell):
    own = fields[0]
    patch, ti, pi = [lax.axis_index(axis) for axis in EVERYONE]
    other = 1 - patch

    top, bottom, west, east = run_split(own)
    above, below = shift(bottom, "theta", N_THETA, 1), shift(top, "theta", N_THETA, -1)
    before, after = shift(east, "phi", N_PHI, 1), shift(west, "phi", N_PHI, -1)
    edge = jnp.stack([ti == 0, ti == N_THETA - 1, pi == 0, pi == N_PHI - 1]).astype(jnp.int32)

    row_index = ti * ROWS + jnp.arange(ROWS, dtype=jnp.int32)
    theta = 0.25 * math.pi - margin + (row_index.astype(jnp.float32) + 0.5) * THETA_STEP
    col_index = pi * COLS + jnp.arange(COLS, dtype=jnp.int32)
    phi = -0.75 * math.pi - margin + (col_index.astype(jnp.float32) + 0.5) * PHI_STEP
    flag = patch.astype(jnp.float32)
    sine, cosine = jnp.sin(theta), jnp.cos(theta)
    ones = jnp.ones_like(sine)
    row_const = jnp.stack(
        [sine, cosine, cosine / sine, 1.0 / sine, ones * (rotation * flag), ones * (rotation * (1.0 - flag))], axis=1
    )
    phi_const = jnp.broadcast_to(jnp.stack([jnp.sin(phi), jnp.cos(phi)])[:, :, None], (2, COLS, SHELLS))
    radius = inner_radius + RADIAL_STEP * (jnp.arange(SHELLS, dtype=jnp.int32).astype(jnp.float32) + 0.5)
    inv_r = jnp.broadcast_to((1.0 / radius)[None, :], (8, SHELLS))

    base = donor_base[0, 0, 0]
    first = base // (COLS - 1) * COLS + base % (COLS - 1)
    w = weights[0, 0, 0]
    cells = jnp.arange(CELLS, dtype=jnp.int32)[None, :]
    corner = sum(
        jnp.where(cells == (first + offset)[:, None], w[k][:, None], 0.0)
        for k, offset in enumerate((0, 1, COLS, COLS + 1))
    )
    angle = frame_angle[0, 0, 0]
    angle = jnp.broadcast_to(jnp.stack([jnp.cos(angle), jnp.sin(angle)])[:, :, None], (2, SLOTS, SHELLS))

    receiver = destination[0, 0, 0]
    slot = jnp.arange(SLOTS, dtype=jnp.int32)
    rank = jnp.sum(
        ((receiver[:, None] == receiver[None, :]) & (slot[None, :] < slot[:, None])).astype(jnp.int32), axis=1
    )
    to_row, to_col = receiver // N_PHI, receiver % N_PHI
    at_end = (to_row == 0) | (to_row == N_THETA - 1)
    mate = other * DEVS + to_row * N_PHI + jnp.where(to_col % 2 == 0, to_col + 1, to_col - 1)
    relay = patch * DEVS + to_row * N_PHI + jnp.where(ti < N_THETA // 2, to_col, (to_col + 2) % N_PHI)
    place = jnp.where(rank == 0, other * DEVS + receiver, jnp.where(at_end, relay, mate))

    def exchange(x):
        moved = lax.all_to_all(x, EVERYONE, 0, 0, tiled=True)
        direct = lax.dynamic_slice_in_dim(moved, other * DEVS, DEVS, 0)
        relayed = lax.dynamic_slice_in_dim(moved, patch * DEVS, DEVS, 0)
        from_mate = lax.ppermute(direct, "phi", [(0, 1), (1, 0), (2, 3), (3, 2)])
        early = lax.ppermute(relayed[: DEVS // 2], "patch", [(0, 1), (1, 0)])
        across = [(a * N_PHI + p, (1 - a) * N_PHI + (p + 2) % N_PHI) for a in range(2) for p in range(N_PHI)]
        late = lax.ppermute(relayed[DEVS // 2 :], ("patch", "phi"), across)
        return direct, from_mate, early, late

    position = jnp.arange(2 * DEVS, dtype=jnp.int32)
    target = target_cell[0, 0, 0]
    sent = jnp.sum(jnp.where(position[:, None] == place[None, :], target[None, :] + 1, 0), axis=1) - 1
    sent = jnp.broadcast_to(sent[:, None, None], (2 * DEVS, 1, SHELLS))
    sent, _ = lax.optimization_barrier((sent, (before, after)))
    direct, from_mate, early, late = [x[:, 0, 0] for x in exchange(sent)]
    ids = jnp.concatenate([direct, jnp.where(edge[0] + edge[1] > 0, jnp.concatenate([early, late]), from_mate)])
    ids = jnp.where(jnp.sum(edge) > 0, ids, -1)
    picked = ids[None, :] == jnp.arange(CELLS, dtype=jnp.int32)[:, None]
    pick = picked.astype(jnp.bfloat16)
    count = jnp.sum(picked.astype(jnp.float32), axis=1)
    mean = jnp.where(count > 0.0, 1.0 / jnp.maximum(count, 1.0), 0.0)
    mean = jnp.broadcast_to(mean[:, None], (CELLS, SHELLS))

    tail = (edge, row_const, phi_const, inv_r, corner, angle, place)
    top, bottom, send = run_step(False, (top, bottom, above, below, before, after, *tail))
    above, below = shift(bottom, "theta", N_THETA, 1), shift(top, "theta", N_THETA, -1)
    top, bottom, west, east, head, foot = run_merge(False, top, bottom, *exchange(send), pick, mean, edge)
    fix_above, fix_below = shift(foot, "theta", N_THETA, 1), shift(head, "theta", N_THETA, -1)
    before, after = shift(east, "phi", N_PHI, 1), shift(west, "phi", N_PHI, -1)
    top, bottom, send = run_step(
        True, (own, fix_above, fix_below, top, bottom, above, below, before, after, *tail)
    )
    (result,) = run_merge(True, top, bottom, *exchange(send), pick, mean, edge)
    return result[None]


def solution(mesh):
    placed = (
        P("patch", None, "theta", "phi", None),
        P("patch", "theta", "phi", None),
        P("patch", "theta", "phi", None, None),
        P("patch", "theta", "phi", None),
        P("patch", "theta", "phi", None),
        P("patch", "theta", "phi", None),
    )
    return jax.shard_map(
        local,
        mesh=mesh,
        in_specs=placed,
        out_specs=P("patch", None, "theta", "phi", None),
        check_vma=False,
    )
```

time: 258 us -> 187 us (0.72)
  waiting for transfers between devices: 86.9 us -> 37.6 us
  blocking collectives: 63.8 us -> 40.4 us
  local copies, waits for them, and re-layouts: 14.9 us -> 20.8 us
  Pallas kernels: 32.5 us -> 28.9 us
    all_to_all x2, waiting for transfers between devices: 45.9 us -> 10.1 us  [exchange(): moved = lax.all_to_all(x, EVERYONE, 0, 0, tiled=True)]
    all_to_all x1, blocking collectives: 63.8 us -> 40.4 us  [exchange(): moved = lax.all_to_all(x, EVERYONE, 0, 0, tiled=True)]
    ppermute x8 -> x19, waiting for transfers between devices: 41 us -> 27.4 us  [the longest x3 16.9 us: exchange(): late = lax.ppermute(relayed[DEVS // 2:], ('patch', 'phi'), across)]
    pallas_call x4 -> x5, Pallas kernels: 32.5 us -> 28.9 us  [the longest x2 22.2 us: run_step(): pl.pallas_call(lambda *refs: step_kernel(second, *refs), out_shape=(struc...]
    slice x5 -> x8, local copies, waits for them, and re-layouts: 8.67 us -> 10.8 us  [the longest x4 8.28 us: local(): direct, from_mate, early, late = [x[:, 0, 0] for x in exchange(sent)]]
    unnamed x16 -> x26, local copies, waits for them, and re-layouts: 4.42 us -> 6.57 us
    ppermute x8 -> x19, starting transfers between devices: 21 us -> 21.1 us  [the longest x10 13.4 us: shift(): return lax.ppermute(x, axis, [(i, (i + by) % size) for i in range(size)])]
  transfers between devices with their start and end apart: 10 -> 21, of which waited for: 6 -> 6; matrix products, arithmetic and copies ran while one was open for 5% -> 9% of each run, Pallas kernels for 5% -> 8%
where the time goes in v2:
time: 187 us; the launch traced here: 184 us
  starting transfers between devices  52 us (28%)
  blocking collectives  40.4 us (22%)
  waiting for transfers between devices  37.6 us (20%)
  Pallas kernels  28.9 us (15%)
  local copies, waits for them, and re-layouts  20.8 us (11%)
  between operations  2.31 us (1%)
    all_to_all x1, blocking collectives, exchange(): moved = lax.all_to_all(x, EVERYONE, 0, 0, tiled=True)  40.4 us
    all_to_all x2, starting transfers between devices, exchange(): moved = lax.all_to_all(x, EVERYONE, 0, 0, tiled=True)  30.9 us
    pallas_call x2, Pallas kernels, run_step(): pl.pallas_call(lambda *refs: step_kernel(second, *refs), out_shape=(struc...  22.2 us
    ppermute x3, waiting for transfers between devices, exchange(): late = lax.ppermute(relayed[DEVS // 2:], ('patch', 'phi'), across)  16.9 us
    ppermute x10, starting transfers between devices, shift(): return lax.ppermute(x, axis, [(i, (i + by) % size) for i in range(size)])  13.4 us
    ppermute x10, waiting for transfers between devices, shift(): return lax.ppermute(x, axis, [(i, (i + by) % size) for i in range(size)])  10.5 us
    all_to_all x2, waiting for transfers between devices, exchange(): moved = lax.all_to_all(x, EVERYONE, 0, 0, tiled=True)  10.1 us
    slice x4, local copies, waits for them, and re-layouts, local(): direct, from_mate, early, late = [x[:, 0, 0] for x in exchange(sent)]  8.28 us
  transfers between devices with their start and end apart: 21, of which 6 were waited for; matrix products, arithmetic and copies ran while one was open for 9% of the time, Pallas kernels for 8%

profile of v2, /device:TPU:2, one launch (start us, length us, event | category | flops | bytes accessed | tf_op | source)
XLA Modules:
  0.0 183.7 jit_solution(7445686859798563194)
XLA Ops:
  0.0 0.0 copy-start
  0.0 1.6 copy-done
  1.6 0.2 shard_map.64
  1.8 0.1 collective-permute-start.2
  1.9 3.2 %collective-permute-start.3 = (f32[8,8,128]{2,1,0:T(8,128)S(1)}, f32[8,8,128]{2,1,0:T(8,128)S(1)}, u32[]{:S(2)}, u32[]{:S(2)}) collective-permute-start(f32[8,8,128]{2,1,0:T(8,128)S(1)} %get-tuple-element.25), channel_id=1, source_target_pairs={{0,3},{1,0},{2,1},{3,2},{4,7},{5,4},{6,5},{7,6},{8,11},{9,8},{10,9... | collective-permute-start | bytes 98312 | tf_op jit(solution)/shard_map/ppermute | solution.py:313
  5.2 2.3 %collective-permute-start.1 = (f32[8,2,128,128]{3,2,1,0:T(8,128)S(1)}, f32[8,2,128,128]{3,2,1,0:T(8,128)S(1)}, u32[]{:S(2)}, u32[]{:S(2)}) collective-permute-start(f32[8,2,128,128]{3,2,1,0:T(8,128)S(1)} %get-tuple-element.22.refs_0_), channel_id=1, source_target_pairs={{0,124},{4,0},{8,4},{12,8},{16,12},{20,16},{24,20},{28,24},{32,28}... | collective-permute-start | bytes 3145736 | tf_op jit(solution)/shard_map/ppermute | solution.py:313
  7.4 0.0 collective-permute-start
  7.4 1.0 copy-done.2
  8.5 0.1 broadcast_divide_fusion
  8.6 0.2 convert_reduce_fusion.1
  8.7 0.1 fusion.9
  8.9 0.1 select_reduce_fusion
  9.1 0.0 collective-permute-done.2.refs_4_
  9.1 1.0 broadcast_in_dim.114
  10.1 17.3 %all-to-all-start.1 = ((s32[256,1,128]{2,1,0:T(1,128)}), s32[256,1,128]{2,1,0:T(1,128)}, u32[]{:S(2)}, u32[]{:S(2)}) async-start(s32[256,1,128]{2,1,0:T(1,128)} %broadcast_in_dim.114), calls=%async_computation.1 | async-start | bytes 262144 | tf_op jit(solution)/shard_map/all_to_all | solution.py:363
  27.4 0.7 fusion.11
  28.1 0.1 stack.45.refs_7_.refs_10_
  28.2 0.2 select_add_fusion.refs_10_.refs_13_
  28.4 2.1 %collective-permute-done.1.refs_3_ = f32[8,2,128,128]{3,2,1,0:T(8,128)S(1)} collective-permute-done((f32[8,2,128,128]{3,2,1,0:T(8,128)S(1)}, f32[8,2,128,128]{3,2,1,0:T(8,128)S(1)}, u32[]{:S(2)}, u32[]{:S(2)}) %collective-permute-start.1) | collective-permute-done | bytes 1048608 | tf_op jit(solution)/shard_map/ppermute | solution.py:313
  30.5 1.0 copy-done.4
  31.5 6.8 %collective-permute-done.refs_2_ = f32[8,2,128,128]{3,2,1,0:T(8,128)} collective-permute-done((f32[8,2,128,128]{3,2,1,0:T(8,128)S(1)}, f32[8,2,128,128]{3,2,1,0:T(8,128)}, u32[]{:S(2)}, u32[]{:S(2)}) %collective-permute-start) | collective-permute-done | bytes 1048608 | tf_op jit(solution)/shard_map/ppermute | solution.py:313
  38.3 0.1 broadcast_in_dim.111.refs_11_.refs_14_
  38.4 0.1 broadcast_in_dim.100.refs_8_.refs_11_
  38.5 0.5 copy-done.6
  39.0 1.2 copy-done.3
  40.2 1.2 copy-done.5
  41.5 11.5 %shard_map.65 = (f32[8,2,128,128]{3,2,1,0:T(8,128)S(1)}, f32[8,2,128,128]{3,2,1,0:T(8,128)S(1)}, f32[256,8,128]{2,1,0:T(8,128)}) custom-call(f32[8,2,128,128]{3,2,1,0:T(8,128)S(1)} %get-tuple-element.22.refs_0_, f32[8,2,128,128]{3,2,1,0:T(8,128)S(1)} %copy-done.3, f32[8,2,128,128]{3,2,1,0:T(8,128)} %collective-permute-done.refs_2_, ...), custom_call_target="tpu_custom_call" | custom-call | tf_op jit(solution)/shard_map/pallas_call | solution.py:240
  53.0 13.6 %all-to-all-start = ((f32[256,8,128]{2,1,0:T(8,128)}), f32[256,8,128]{2,1,0:T(8,128)}, u32[]{:S(2)}, u32[]{:S(2)}) async-start(f32[256,8,128]{2,1,0:T(8,128)} %get-tuple-element.28), calls=%async_computation | async-start | bytes 2097152 | tf_op jit(solution)/shard_map/all_to_all | solution.py:363
  67.2 0.7 fusion.13
  69.2 0.8 constant_dynamic-slice_fusion.6
  70.0 1.5 collective-permute-start.7
  71.5 2.1 %collective-permute-start.8 = (s32[64,1,128]{2,1,0:T(1,128)S(1)}, s32[64,1,128]{2,1,0:T(1,128)S(1)}, u32[]{:S(2)}, u32[]{:S(2)}) collective-permute-start(s32[64,1,128]{2,1,0:T(1,128)S(1)} %get-tuple-element.48), channel_id=1, source_target_pairs={{0,130},{1,131},{2,128},{3,129},{128,2},{129,3},{130,0},{131,1},{4... | collective-permute-start | bytes 98312 | tf_op jit(solution)/shard_map/ppermute | solution.py:369
  73.7 0.8 constant_dynamic-slice_fusion.5
  74.5 0.0 collective-permute-start.9
  74.5 3.3 %dynamic-slice_reduce_fusion = s32[128]{0:T(128)S(1)} fusion(s32[256,1,128]{2,1,0:T(1,128)} %all-to-all-done.1, s32[]{:T(128)S(6)} %select_n.170), kind=kLoop, calls=%fused_computation.11 | loop fusion | bytes 1028 | tf_op jit(solution)/shard_map/slice | solution.py:377
  77.8 1.3 slice_reduce_fusion.2
  79.1 1.3 slice_reduce_fusion.1
  80.4 2.5 %slice_reduce_fusion = s32[128]{0:T(128)S(1)} fusion(s32[128,1,128]{2,1,0:T(1,128)S(1)} %collective-permute-done.9), kind=kLoop, calls=%fused_computation.10 | loop fusion | bytes 1024 | tf_op jit(solution)/shard_map/slice | solution.py:377
  82.8 0.6 collective-permute-start.13
  83.5 1.5 collective-permute-start.12
  84.9 0.1 broadcast_select_fusion
  85.0 0.2 convert_reduce_fusion
  85.2 10.1 %all-to-all-done = f32[256,8,128]{2,1,0:T(8,128)} async-done(((f32[256,8,128]{2,1,0:T(8,128)}), f32[256,8,128]{2,1,0:T(8,128)}, u32[]{:S(2)}, u32[]{:S(2)}) %all-to-all-start) | async-done | bytes 1048608 | tf_op jit(solution)/shard_map/all_to_all | solution.py:363
  95.3 1.1 constant_dynamic-slice_fusion.8.refs_2_
  96.4 1.0 collective-permute-start.4
  97.4 1.1 constant_dynamic-slice_fusion.7
  98.5 1.0 collective-permute-start.6
  99.5 0.1 fusion.refs_6_
  99.6 8.5 %collective-permute-done.6.refs_5_ = f32[64,8,128]{2,1,0:T(8,128)S(1)} collective-permute-done((f32[64,8,128]{2,1,0:T(8,128)S(1)}, f32[64,8,128]{2,1,0:T(8,128)S(1)}, u32[]{:S(2)}, u32[]{:S(2)}) %collective-permute-start.6) | collective-permute-done | bytes 262176 | tf_op jit(solution)/shard_map/ppermute | solution.py:369
  108.0 0.1 broadcast_in_dim.115.refs_7_
  108.2 0.0 copy-start.1
  108.2 2.6 %shard_map.66 = (f32[8,2,128,128]{3,2,1,0:T(8,128)S(1)}, f32[8,2,128,128]{3,2,1,0:T(8,128)S(1)}, f32[8,8,128]{2,1,0:T(8,128)S(1)}, f32[8,8,128]{2,1,0:T(8,128)S(...) custom-call(f32[8,2,128,128]{3,2,1,0:T(8,128)S(1)} %get-tuple-element.26.refs_0_, ...), custom_call_target="tpu_custom_call" | custom-call | tf_op jit(solution)/shard_map/pallas_call | solution.py:302
  110.8 1.7 collective-permute-start.10
  112.5 0.8 collective-permute-start.11
  113.3 3.2 %collective-permute-start.15 = (f32[8,8,128]{2,1,0:T(8,128)S(1)}, f32[8,8,128]{2,1,0:T(8,128)S(1)}, u32[]{:S(2)}, u32[]{:S(2)}) collective-permute-start(f32[8,8,128]{2,1,0:T(8,128)S(1)} %get-tuple-element.35), channel_id=1, source_target_pairs={{0,3},{1,0},{2,1},{3,2},{4,7},{5,4},{6,5},{7,6},{8,11},{9,8},{10,9... | collective-permute-start | bytes 98312 | tf_op jit(solution)/shard_map/ppermute | solution.py:313
  116.5 0.0 collective-permute-done.11.refs_2_
  116.6 1.5 collective-permute-done.14.refs_7_
  118.1 0.0 collective-permute-done.15.refs_8_
  118.1 10.8 %shard_map.67 = (f32[8,2,128,128]{3,2,1,0:T(8,128)S(1)}, f32[8,2,128,128]{3,2,1,0:T(8,128)S(1)}, f32[256,8,128]{2,1,0:T(8,128)S(1)}) custom-call(f32[8,4,128,128]{3,2,1,0:T(8,128)S(1)} %bitcast.42, f32[8,8,128]{2,1,0:T(8,128)S(1)} %collective-permute-done.10.refs_1_, f32[8,8,128]{2,1,0:T(8,128)S(1)} %collective-permute-done.11.refs_2_, ...), custom_call_target="tpu_custom_call" | custom-call | tf_op jit(solution)/shard_map/pallas_call | solution.py:240
  128.9 40.4 %all_to_all.15 = f32[256,8,128]{2,1,0:T(8,128)S(1)} all-to-all(f32[256,8,128]{2,1,0:T(8,128)S(1)} %get-tuple-element.38), channel_id=1, replica_groups=mesh['patch'=2,'theta'=32,'phi'=4] {'patch','theta','phi'}, dimensions={0} | all-to-all | bytes 2097152 | tf_op jit(solution)/shard_map/all_to_all | solution.py:363
  169.3 0.9 collective-permute-start.16
  170.3 1.1 collective-permute-start.18
  171.4 8.4 %collective-permute-done.18.refs_5_ = f32[64,8,128]{2,1,0:T(8,128)S(1)} collective-permute-done((f32[64,8,128]{2,1,0:T(8,128)S(1)}, f32[64,8,128]{2,1,0:T(8,128)S(1)}, u32[]{:S(2)}, u32[]{:S(2)}) %collective-permute-start.18) | collective-permute-done | bytes 262176 | tf_op jit(solution)/shard_map/ppermute | solution.py:369
  179.8 3.9 %shard_map.68 = f32[8,4,128,128]{3,2,1,0:T(8,128)} custom-call(f32[8,2,128,128]{3,2,1,0:T(8,128)S(1)} %get-tuple-element.36.refs_0_, f32[8,2,128,128]{3,2,1,0:T(8,128)S(1)} %get-tuple-element.37.refs_1_, f32[128,8,128]{2,1,0:T(8,128)S(1)} %constant_dynamic-slice_fusion.3.refs_2_, f32[128,8,128]{2,1,0:T(8,128)S(1)} %collective-permute-done.16.refs_3_, ...), custom_call_target="tpu_custom_call" | custom-call | tf_op jit(solution)/shard_map/pallas_call | solution.py:302
  (51 shorter events, 0.3 us)
Async XLA Ops:
  0.0 8.5 %copy-start.10 = (s32[1,1,1,96]{3,2,1,0:T(1,128)S(1)}, s32[1,1,1,96]{3,2,1,0:T(1,128)}, u32[]{:S(2)}) copy-start(s32[1,1,1,96]{3,2,1,0:T(1,128)} %param.11) | copy-start | bytes 1156
  0.0 8.5 %copy-start.9 = (s32[1,1,1,96]{3,2,1,0:T(1,128)S(1)}, s32[1,1,1,96]{3,2,1,0:T(1,128)}, u32[]{:S(2)}) copy-start(s32[1,1,1,96]{3,2,1,0:T(1,128)} %param.10) | copy-start | bytes 1156
  0.0 8.8 %copy-start.11 = (s32[1,1,1,96]{3,2,1,0:T(1,128)S(1)}, s32[1,1,1,96]{3,2,1,0:T(1,128)}, u32[]{:S(2)}) copy-start(s32[1,1,1,96]{3,2,1,0:T(1,128)} %param.7) | copy-start | bytes 1156
  0.0 1.6 copy-start
  1.6 7.2 %copy-start.12 = (f32[1,1,1,96]{3,2,1,0:T(1,128)S(1)}, f32[1,1,1,96]{3,2,1,0:T(1,128)}, u32[]{:S(2)}) copy-start(f32[1,1,1,96]{3,2,1,0:T(1,128)} %param.9) | copy-start | bytes 1156
  1.6 7.4 %copy-start.8 = (f32[1,1,1,4,96]{4,3,2,1,0:T(4,128)S(1)}, f32[1,1,1,4,96]{4,3,2,1,0:T(4,128)}, u32[]{:S(2)}) copy-start(f32[1,1,1,4,96]{4,3,2,1,0:T(4,128)} %param.8) | copy-start | bytes 4612
  1.8 7.3 %collective-permute-start.2 = (f32[8,8,128]{2,1,0:T(8,128)S(1)}, f32[8,8,128]{2,1,0:T(8,128)S(1)}, u32[]{:S(2)}, u32[]{:S(2)}) collective-permute-start(f32[8,8,128]{2,1,0:T(8,128)S(1)} %get-tuple-element.24), channel_id=1, source_target_pairs={{0,1},{1,2},{2,3},{3,0},{4,5},{5,6},{6,7},{7,4},{8,9},{9,10},{10,1... | collective-permute-start | bytes 98312 | tf_op jit(solution)/shard_map/ppermute | solution.py:313
  1.9 7.2 %collective-permute-start.3 = (f32[8,8,128]{2,1,0:T(8,128)S(1)}, f32[8,8,128]{2,1,0:T(8,128)S(1)}, u32[]{:S(2)}, u32[]{:S(2)}) collective-permute-start(f32[8,8,128]{2,1,0:T(8,128)S(1)} %get-tuple-element.25), channel_id=1, source_target_pairs={{0,3},{1,0},{2,1},{3,2},{4,7},{5,4},{6,5},{7,6},{8,11},{9,8},{10,9... | collective-permute-start | bytes 98312 | tf_op jit(solution)/shard_map/ppermute | solution.py:313
  5.2 25.3 %collective-permute-start.1 = (f32[8,2,128,128]{3,2,1,0:T(8,128)S(1)}, f32[8,2,128,128]{3,2,1,0:T(8,128)S(1)}, u32[]{:S(2)}, u32[]{:S(2)}) collective-permute-start(f32[8,2,128,128]{3,2,1,0:T(8,128)S(1)} %get-tuple-element.22.refs_0_), channel_id=1, source_target_pairs={{0,124},{4,0},{8,4},{12,8},{16,12},{20,16},{24,20},{28,24},{32,28}... | collective-permute-start | bytes 3145736 | tf_op jit(solution)/shard_map/ppermute | solution.py:313
  7.4 30.8 %collective-permute-start = (f32[8,2,128,128]{3,2,1,0:T(8,128)S(1)}, f32[8,2,128,128]{3,2,1,0:T(8,128)}, u32[]{:S(2)}, u32[]{:S(2)}) collective-permute-start(f32[8,2,128,128]{3,2,1,0:T(8,128)S(1)} %get-tuple-element.23.refs_1_), channel_id=1, source_target_pairs={{0,4},{4,8},{8,12},{12,16},{16,20},{20,24},{24,28},{28,32},{32,36}... | collective-permute-start | bytes 3145736 | tf_op jit(solution)/shard_map/ppermute | solution.py:313
  7.4 1.0 copy-start.2
  10.1 42.8 %all-to-all-start.1 = ((s32[256,1,128]{2,1,0:T(1,128)}), s32[256,1,128]{2,1,0:T(1,128)}, u32[]{:S(2)}, u32[]{:S(2)}) async-start(s32[256,1,128]{2,1,0:T(1,128)} %broadcast_in_dim.114), calls=%async_computation.1 | async-start | bytes 262144 | tf_op jit(solution)/shard_map/all_to_all | solution.py:363
  30.5 1.0 copy-start.4
  38.4 0.6 copy-start.6
  39.0 1.2 copy-start.3
  40.2 1.2 copy-start.5
  53.0 42.4 %all-to-all-start = ((f32[256,8,128]{2,1,0:T(8,128)}), f32[256,8,128]{2,1,0:T(8,128)}, u32[]{:S(2)}, u32[]{:S(2)}) async-start(f32[256,8,128]{2,1,0:T(8,128)} %get-tuple-element.28), calls=%async_computation | async-start | bytes 2097152 | tf_op jit(solution)/shard_map/all_to_all | solution.py:363
  70.0 7.8 %collective-permute-start.7 = (s32[64,1,128]{2,1,0:T(1,128)S(1)}, s32[64,1,128]{2,1,0:T(1,128)S(1)}, u32[]{:S(2)}, u32[]{:S(2)}) collective-permute-start(s32[64,1,128]{2,1,0:T(1,128)S(1)} %get-tuple-element.47), channel_id=1, source_target_pairs={{0,128},{128,0},{1,129},{129,1},{2,130},{130,2},{3,131},{131,3},{4... | collective-permute-start | bytes 98312 | tf_op jit(solution)/shard_map/ppermute | solution.py:367
  71.5 7.5 %collective-permute-start.8 = (s32[64,1,128]{2,1,0:T(1,128)S(1)}, s32[64,1,128]{2,1,0:T(1,128)S(1)}, u32[]{:S(2)}, u32[]{:S(2)}) collective-permute-start(s32[64,1,128]{2,1,0:T(1,128)S(1)} %get-tuple-element.48), channel_id=1, source_target_pairs={{0,130},{1,131},{2,128},{3,129},{128,2},{129,3},{130,0},{131,1},{4... | collective-permute-start | bytes 98312 | tf_op jit(solution)/shard_map/ppermute | solution.py:369
  74.5 5.8 %collective-permute-start.9 = (s32[128,1,128]{2,1,0:T(1,128)S(1)}, s32[128,1,128]{2,1,0:T(1,128)S(1)}, u32[]{:S(2)}, u32[]{:S(2)}) collective-permute-start(s32[128,1,128]{2,1,0:T(1,128)S(1)} %constant_dynamic-slice_fusion.5), channel_id=1, source_target_pairs={{0,1},{1,0},{2,3},{3,2},{4,5},{5,4},{6,7},{7,6},{8,9},{9,8},{10,11... | collective-permute-start | bytes 196616 | tf_op jit(solution)/shard_map/ppermute | solution.py:366
  82.8 30.4 %collective-permute-start.13 = (f32[8,2,128,128]{3,2,1,0:T(8,128)S(1)}, f32[8,2,128,128]{3,2,1,0:T(8,128)S(1)}, u32[]{:S(2)}, u32[]{:S(2)}) collective-permute-start(f32[8,2,128,128]{3,2,1,0:T(8,128)S(1)} %get-tuple-element.26.refs_0_), channel_id=1, source_target_pairs={{0,124},{4,0},{8,4},{12,8},{16,12},{20,16},{24,20},{28,24},{32,28}... | collective-permute-start | bytes 3145736 | tf_op jit(solution)/shard_map/ppermute | solution.py:313
  83.5 33.1 %collective-permute-start.12 = (f32[8,2,128,128]{3,2,1,0:T(8,128)S(1)}, f32[8,2,128,128]{3,2,1,0:T(8,128)}, u32[]{:S(2)}, u32[]{:S(2)}) collective-permute-start(f32[8,2,128,128]{3,2,1,0:T(8,128)S(1)} %get-tuple-element.27.refs_1_), channel_id=1, source_target_pairs={{0,4},{4,8},{8,12},{12,16},{16,20},{20,24},{24,28},{28,32},{32,36}... | collective-permute-start | bytes 3145736 | tf_op jit(solution)/shard_map/ppermute | solution.py:313
  96.4 11.6 %collective-permute-start.4 = (f32[128,8,128]{2,1,0:T(8,128)S(1)}, f32[128,8,128]{2,1,0:T(8,128)S(1)}, u32[]{:S(2)}, u32[]{:S(2)}) collective-permute-start(f32[128,8,128]{2,1,0:T(8,128)S(1)} %constant_dynamic-slice_fusion.8.refs_2_), channel_id=1, source_target_pairs={{0,1},{1,0},{2,3},{3,2},{4,5},{5,4},{6,7},{7,6},{8,9},{9,8},{10,11... | collective-permute-start | bytes 1572872 | tf_op jit(solution)/shard_map/ppermute | solution.py:366
  98.5 9.5 %collective-permute-start.6 = (f32[64,8,128]{2,1,0:T(8,128)S(1)}, f32[64,8,128]{2,1,0:T(8,128)S(1)}, u32[]{:S(2)}, u32[]{:S(2)}) collective-permute-start(f32[64,8,128]{2,1,0:T(8,128)S(1)} %get-tuple-element.45), channel_id=1, source_target_pairs={{0,130},{1,131},{2,128},{3,129},{128,2},{129,3},{130,0},{131,1},{4... | collective-permute-start | bytes 786440 | tf_op jit(solution)/shard_map/ppermute | solution.py:369
  99.5 8.5 %collective-permute-start.5 = (f32[64,8,128]{2,1,0:T(8,128)S(1)}, f32[64,8,128]{2,1,0:T(8,128)S(1)}, u32[]{:S(2)}, u32[]{:S(2)}) collective-permute-start(f32[64,8,128]{2,1,0:T(8,128)S(1)} %get-tuple-element.46), channel_id=1, source_target_pairs={{0,128},{128,0},{1,129},{129,1},{2,130},{130,2},{3,131},{131,3},{4... | collective-permute-start | bytes 786440 | tf_op jit(solution)/shard_map/ppermute | solution.py:367
  108.2 10.0 %copy-start.1 = (f32[1,8,4,128,128]{4,3,2,1,0:T(8,128)S(1)}, f32[1,8,4,128,128]{4,3,2,1,0:T(8,128)}, u32[]{:S(2)}) copy-start(f32[1,8,4,128,128]{4,3,2,1,0:T(8,128)} %param.6) | copy-start | bytes 6291460
  108.2 10.0 %copy-start.7 = (f32[2,96,128]{2,1,0:T(8,128)S(1)}, f32[2,96,128]{2,1,0:T(8,128)}, u32[]{:S(2)}) copy-start(f32[2,96,128]{2,1,0:T(8,128)} %copy-done.6) | copy-start | bytes 294916
  110.8 5.8 %collective-permute-start.10 = (f32[8,8,128]{2,1,0:T(8,128)S(1)}, f32[8,8,128]{2,1,0:T(8,128)S(1)}, u32[]{:S(2)}, u32[]{:S(2)}) collective-permute-start(f32[8,8,128]{2,1,0:T(8,128)S(1)} %get-tuple-element.30), channel_id=1, source_target_pairs={{0,4},{4,8},{8,12},{12,16},{16,20},{20,24},{24,28},{28,32},{32,36}... | collective-permute-start | bytes 98312 | tf_op jit(solution)/shard_map/ppermute | solution.py:313
  112.5 4.1 %collective-permute-start.11 = (f32[8,8,128]{2,1,0:T(8,128)S(1)}, f32[8,8,128]{2,1,0:T(8,128)S(1)}, u32[]{:S(2)}, u32[]{:S(2)}) collective-permute-start(f32[8,8,128]{2,1,0:T(8,128)S(1)} %get-tuple-element.31), channel_id=1, source_target_pairs={{0,124},{4,0},{8,4},{12,8},{16,12},{20,16},{24,20},{28,24},{32,28}... | collective-permute-start | bytes 98312 | tf_op jit(solution)/shard_map/ppermute | solution.py:313
  113.3 4.8 %collective-permute-start.14 = (f32[8,8,128]{2,1,0:T(8,128)S(1)}, f32[8,8,128]{2,1,0:T(8,128)S(1)}, u32[]{:S(2)}, u32[]{:S(2)}) collective-permute-start(f32[8,8,128]{2,1,0:T(8,128)S(1)} %get-tuple-element.34), channel_id=1, source_target_pairs={{0,1},{1,2},{2,3},{3,0},{4,5},{5,6},{6,7},{7,4},{8,9},{9,10},{10,1... | collective-permute-start | bytes 98312 | tf_op jit(solution)/shard_map/ppermute | solution.py:313
  113.3 4.8 %collective-permute-start.15 = (f32[8,8,128]{2,1,0:T(8,128)S(1)}, f32[8,8,128]{2,1,0:T(8,128)S(1)}, u32[]{:S(2)}, u32[]{:S(2)}) collective-permute-start(f32[8,8,128]{2,1,0:T(8,128)S(1)} %get-tuple-element.35), channel_id=1, source_target_pairs={{0,3},{1,0},{2,1},{3,2},{4,7},{5,4},{6,5},{7,6},{8,11},{9,8},{10,9... | collective-permute-start | bytes 98312 | tf_op jit(solution)/shard_map/ppermute | solution.py:313
  169.3 10.5 %collective-permute-start.16 = (f32[128,8,128]{2,1,0:T(8,128)S(1)}, f32[128,8,128]{2,1,0:T(8,128)S(1)}, u32[]{:S(2)}, u32[]{:S(2)}) collective-permute-start(f32[128,8,128]{2,1,0:T(8,128)S(1)} %constant_dynamic-slice_fusion.3.refs_2_), channel_id=1, source_target_pairs={{0,1},{1,0},{2,3},{3,2},{4,5},{5,4},{6,7},{7,6},{8,9},{9,8},{10,11... | collective-permute-start | bytes 1572872 | tf_op jit(solution)/shard_map/ppermute | solution.py:366
  170.3 9.5 %collective-permute-start.18 = (f32[64,8,128]{2,1,0:T(8,128)S(1)}, f32[64,8,128]{2,1,0:T(8,128)S(1)}, u32[]{:S(2)}, u32[]{:S(2)}) collective-permute-start(f32[64,8,128]{2,1,0:T(8,128)S(1)} %get-tuple-element.43), channel_id=1, source_target_pairs={{0,130},{1,131},{2,128},{3,129},{128,2},{129,3},{130,0},{131,1},{4... | collective-permute-start | bytes 786440 | tf_op jit(solution)/shard_map/ppermute | solution.py:369
  171.4 8.4 %collective-permute-start.17 = (f32[64,8,128]{2,1,0:T(8,128)S(1)}, f32[64,8,128]{2,1,0:T(8,128)S(1)}, u32[]{:S(2)}, u32[]{:S(2)}) collective-permute-start(f32[64,8,128]{2,1,0:T(8,128)S(1)} %get-tuple-element.44), channel_id=1, source_target_pairs={{0,128},{128,0},{1,129},{129,1},{2,130},{130,2},{3,131},{131,3},{4... | collective-permute-start | bytes 786440 | tf_op jit(solution)/shard_map/ppermute | solution.py:367

commit v3 on v2

--- a/solution.py
+++ b/solution.py
@@ -37,6 +37,8 @@
 
 HALF_BLOCK = (FIELDS, HALF, COLS, SHELLS)
 RIM = (FIELDS, 8, SHELLS)
+PARCEL = 2 * N_THETA + 4
+CHUNK = 8
 
 
 def params(mib):
@@ -80,18 +82,20 @@
 
 def step_kernel(second, *refs):
     if second:
-        base_hbm, fix_above, fix_below, *refs = refs
+        fix_above, fix_below, top, bottom, *refs = refs
     (
-        top, bottom, above, below, before, after, edge, row_const, phi_const, inv_r_ref, corner, angle, place,
-        new_top, new_bottom, send, ext, donor, base, sems,
+        fields, above, below, before, after, edge, row_const, phi_const, inv_r_ref, corner, angle, place,
+        new_top, new_bottom, near_send, far_send, ext, donor, send, base, sems,
     ) = refs
     inside = pl.ds(PAD, COLS)
+    parts = [(above, 0, HALF), (below, ROWS + 2, HALF)]
+    parts += [(top, 2, HALF), (bottom, 4, HALF)] if second else [(fields, 2, ROWS)]
     copies = [
-        pltpu.make_async_copy(ref, ext.at[:, start : start + HALF, inside], sems.at[n])
-        for n, (ref, start) in enumerate(((above, 0), (top, 2), (bottom, 4), (below, 6)))
+        pltpu.make_async_copy(ref, ext.at[:, start : start + rows, inside], sems.at[n])
+        for n, (ref, start, rows) in enumerate(parts)
     ]
     if second:
-        copies.append(pltpu.make_async_copy(base_hbm, base, sems.at[4]))
+        copies.append(pltpu.make_async_copy(fields, base, sems.at[4]))
     for copy in copies:
         copy.start()
     send[...] = jnp.zeros_like(send)
@@ -208,7 +212,7 @@
                 out[f, i % HALF, rows, :] = new
             return carry
 
-        lax.fori_loop(0, COLS // 8, tile, 0)
+        lax.fori_loop(0, COLS // 8, tile, 0, unroll=4)
 
     def product(f):
         total = None
@@ -228,23 +232,25 @@
         values[t], values[p] = c * values[t] - s * values[p], s * values[t] + c * values[p]
     donor[...] = jnp.swapaxes(jnp.stack(values), 0, 1)
 
-    def put(m, carry):
-        for k in range(8):
-            send[place[8 * m + k]] = donor[8 * m + k]
-        return carry
-
-    lax.fori_loop(0, SLOTS // 8, put, 0)
+    for m in range(0, SLOTS, 16):
+        spots = [place[m + k] for k in range(16)]
+        columns = [donor[m + k] for k in range(16)]
+        for spot, column in zip(spots, columns):
+            send[spot] = column
+    near_send[...] = send[:PARCEL]
+    far_send[...] = send[PARCEL:]
 
 
 def run_step(second, args):
     return pl.pallas_call(
         lambda *refs: step_kernel(second, *refs),
-        out_shape=(struct(*HALF_BLOCK), struct(*HALF_BLOCK), struct(2 * DEVS, FIELDS, SHELLS)),
-        in_specs=([ANY, VMEM, VMEM] if second else []) + [VMEM] * 6 + [SMEM] * 2 + [VMEM] * 4 + [SMEM],
-        out_specs=(VMEM,) * 3,
+        out_shape=(struct(*HALF_BLOCK),) * 2 + (struct(PARCEL, FIELDS, SHELLS),) * 2,
+        in_specs=[VMEM] * (4 if second else 0) + [ANY] + [VMEM] * 4 + [SMEM] * 2 + [VMEM] * 4 + [SMEM],
+        out_specs=(VMEM,) * 4,
         scratch_shapes=[
             pltpu.VMEM((FIELDS, ROWS + 4, EXT, SHELLS), jnp.float32),
             pltpu.VMEM((SLOTS, FIELDS, SHELLS), jnp.float32),
+            pltpu.VMEM((2 * PARCEL, FIELDS, SHELLS), jnp.float32),
             pltpu.VMEM((FIELDS, ROWS if second else 1, COLS, SHELLS), jnp.float32),
             pltpu.SemaphoreType.DMA((5,)),
         ],
@@ -252,23 +258,32 @@
     )(*args)
 
 
-def merge_kernel(last, top, bottom, direct, mate, early, late, pick, mean, edge, *refs):
+def sort_kernel(near, far, mate_near, mate_far, core, chunks):
+    for n, ref in enumerate((near, far, mate_near, mate_far)):
+        for k in range(2):
+            own = 2 * core[0] + k
+            chunks[0, 2 * n + k] = ref[own]
+            chunks[N_THETA - 1, 2 * n + k] = ref[PARCEL - 4 + own]
+            for row in range(1, N_THETA - 1):
+                chunks[row, 2 * n + k] = ref[2 + 2 * row + k]
+
+
+def run_sort(*args):
+    return pl.pallas_call(
+        sort_kernel,
+        out_shape=struct(N_THETA, CHUNK, FIELDS, SHELLS),
+        in_specs=[VMEM] * 4 + [SMEM],
+        out_specs=VMEM,
+        compiler_params=params(8),
+    )(*args)
+
+
+def merge_kernel(last, top, bottom, moved, pick, mean, *refs):
     if last:
         merged, gathered = refs
     else:
         new_top, new_bottom, west, east, head, foot, gathered = refs
-    gathered[:, :DEVS, :] = jnp.swapaxes(direct[...], 0, 1)
-    on_edge = edge[0] + edge[1] > 0
-
-    @pl.when(on_edge)
-    def _():
-        gathered[:, DEVS : DEVS + DEVS // 2, :] = jnp.swapaxes(early[...], 0, 1)
-        gathered[:, DEVS + DEVS // 2 :, :] = jnp.swapaxes(late[...], 0, 1)
-
-    @pl.when(jnp.logical_not(on_edge))
-    def _():
-        gathered[:, DEVS:, :] = jnp.swapaxes(mate[...], 0, 1)
-
+    gathered[...] = jnp.swapaxes(moved[...], 0, 1)
     weight = mean[...]
     for f in range(FIELDS):
         v = gathered[f]
@@ -302,9 +317,9 @@
     return pl.pallas_call(
         lambda *refs: merge_kernel(last, *refs),
         out_shape=shapes,
-        in_specs=[VMEM] * 8 + [SMEM],
+        in_specs=[VMEM] * 5,
         out_specs=(VMEM,) * len(shapes),
-        scratch_shapes=[pltpu.VMEM((FIELDS, 2 * DEVS, SHELLS), jnp.float32)],
+        scratch_shapes=[pltpu.VMEM((FIELDS, N_THETA * CHUNK, SHELLS), jnp.float32)],
         compiler_params=params(16),
     )(*args)
 
@@ -316,7 +331,6 @@
 def local(fields, donor_base, weights, frame_angle, destination, target_cell):
     own = fields[0]
     patch, ti, pi = [lax.axis_index(axis) for axis in EVERYONE]
-    other = 1 - patch
 
     top, bottom, west, east = run_split(own)
     above, below = shift(bottom, "theta", N_THETA, 1), shift(top, "theta", N_THETA, -1)
@@ -354,45 +368,59 @@
         ((receiver[:, None] == receiver[None, :]) & (slot[None, :] < slot[:, None])).astype(jnp.int32), axis=1
     )
     to_row, to_col = receiver // N_PHI, receiver % N_PHI
-    at_end = (to_row == 0) | (to_row == N_THETA - 1)
-    mate = other * DEVS + to_row * N_PHI + jnp.where(to_col % 2 == 0, to_col + 1, to_col - 1)
-    relay = patch * DEVS + to_row * N_PHI + jnp.where(ti < N_THETA // 2, to_col, (to_col + 2) % N_PHI)
-    place = jnp.where(rank == 0, other * DEVS + receiver, jnp.where(at_end, relay, mate))
-
-    def exchange(x):
-        moved = lax.all_to_all(x, EVERYONE, 0, 0, tiled=True)
-        direct = lax.dynamic_slice_in_dim(moved, other * DEVS, DEVS, 0)
-        relayed = lax.dynamic_slice_in_dim(moved, patch * DEVS, DEVS, 0)
-        from_mate = lax.ppermute(direct, "phi", [(0, 1), (1, 0), (2, 3), (3, 2)])
-        early = lax.ppermute(relayed[: DEVS // 2], "patch", [(0, 1), (1, 0)])
-        across = [(a * N_PHI + p, (1 - a) * N_PHI + (p + 2) % N_PHI) for a in range(2) for p in range(N_PHI)]
-        late = lax.ppermute(relayed[DEVS // 2 :], ("patch", "phi"), across)
-        return direct, from_mate, early, late
-
-    position = jnp.arange(2 * DEVS, dtype=jnp.int32)
+    end_spot = 2 * (to_col % 2) + rank
+    spot = jnp.where(
+        to_row == 0, end_spot, jnp.where(to_row == N_THETA - 1, PARCEL - 4 + end_spot, 2 + 2 * to_row + rank)
+    )
+    place = jnp.where(to_col // 2 == pi // 2, spot, PARCEL + spot)
+    core = (pi % 2).astype(jnp.int32).reshape(1)
+
+    def across(x, by):
+        pairs = [(a * N_PHI + p, (1 - a) * N_PHI + (p + by) % N_PHI) for a in range(2) for p in range(N_PHI)]
+        return lax.ppermute(x, ("patch", "phi"), pairs)
+
+    def gather_pair(near, far):
+        near, far = across(near, 0), across(far, 2)
+        swap = [(0, 1), (1, 0), (2, 3), (3, 2)]
+        return near, far, lax.ppermute(near, "phi", swap), lax.ppermute(far, "phi", swap)
+
+    def exchange(near, far):
+        chunks = run_sort(*gather_pair(near, far), core)
+        chunks = chunks.reshape(N_THETA, CHUNK * FIELDS, SHELLS)
+        moved = lax.all_to_all(chunks, "theta", 0, 0, tiled=True)
+        return moved.reshape(N_THETA * CHUNK, FIELDS, SHELLS)
+
+    def exchange_ids(sent):
+        lanes = [jnp.pad(sent[n * PARCEL : (n + 1) * PARCEL], (0, SHELLS - PARCEL))[None] for n in range(2)]
+        parts = jnp.concatenate(gather_pair(*lanes))
+        inside = parts[:, 4 : PARCEL - 4].reshape(4, N_THETA - 2, 2)
+        first = lax.dynamic_slice_in_dim(parts, 2 * core[0], 2, 1)[:, None]
+        final = lax.dynamic_slice_in_dim(parts, PARCEL - 4 + 2 * core[0], 2, 1)[:, None]
+        chunks = jnp.concatenate([first, inside, final], axis=1).swapaxes(0, 1).reshape(N_THETA, 1, CHUNK)
+        chunks = jnp.pad(chunks, ((0, 0), (0, 0), (0, SHELLS - CHUNK)))
+        moved = lax.all_to_all(chunks, "theta", 0, 0, tiled=True)
+        return moved[:, 0, :CHUNK].reshape(N_THETA * CHUNK)
+
+    position = jnp.arange(2 * PARCEL, dtype=jnp.int32)
     target = target_cell[0, 0, 0]
     sent = jnp.sum(jnp.where(position[:, None] == place[None, :], target[None, :] + 1, 0), axis=1) - 1
-    sent = jnp.broadcast_to(sent[:, None, None], (2 * DEVS, 1, SHELLS))
     sent, _ = lax.optimization_barrier((sent, (before, after)))
-    direct, from_mate, early, late = [x[:, 0, 0] for x in exchange(sent)]
-    ids = jnp.concatenate([direct, jnp.where(edge[0] + edge[1] > 0, jnp.concatenate([early, late]), from_mate)])
-    ids = jnp.where(jnp.sum(edge) > 0, ids, -1)
+    ids = jnp.where(jnp.sum(edge) > 0, exchange_ids(sent), -1)
     picked = ids[None, :] == jnp.arange(CELLS, dtype=jnp.int32)[:, None]
     pick = picked.astype(jnp.bfloat16)
     count = jnp.sum(picked.astype(jnp.float32), axis=1)
     mean = jnp.where(count > 0.0, 1.0 / jnp.maximum(count, 1.0), 0.0)
     mean = jnp.broadcast_to(mean[:, None], (CELLS, SHELLS))
 
-    tail = (edge, row_const, phi_const, inv_r, corner, angle, place)
-    top, bottom, send = run_step(False, (top, bottom, above, below, before, after, *tail))
+    tail = (own, above, below, before, after, edge, row_const, phi_const, inv_r, corner, angle, place)
+    top, bottom, near, far = run_step(False, tail)
     above, below = shift(bottom, "theta", N_THETA, 1), shift(top, "theta", N_THETA, -1)
-    top, bottom, west, east, head, foot = run_merge(False, top, bottom, *exchange(send), pick, mean, edge)
-    fix_above, fix_below = shift(foot, "theta", N_THETA, 1), shift(head, "theta", N_THETA, -1)
+    top, bottom, west, east, head, foot = run_merge(False, top, bottom, exchange(near, far), pick, mean)
+    fixes = shift(foot, "theta", N_THETA, 1), shift(head, "theta", N_THETA, -1)
     before, after = shift(east, "phi", N_PHI, 1), shift(west, "phi", N_PHI, -1)
-    top, bottom, send = run_step(
-        True, (own, fix_above, fix_below, top, bottom, above, below, before, after, *tail)
-    )
-    (result,) = run_merge(True, top, bottom, *exchange(send), pick, mean, edge)
+    tail = (own, above, below, before, after, *tail[5:])
+    top, bottom, near, far = run_step(True, (*fixes, top, bottom, *tail))
+    (result,) = run_merge(True, top, bottom, exchange(near, far), pick, mean)
     return result[None]
 
 

time: 187 us -> 193 us (1.032); the launches traced: 184 us -> 192 us
  waiting for transfers between devices: 37.6 us -> 67.8 us
  starting transfers between devices: 52 us -> 38.6 us
  local copies, waits for them, and re-layouts: 20.8 us -> 11.9 us
  Pallas kernels: 28.9 us -> 22.1 us
  blocking collectives: 40.4 us -> 45.4 us
  other arithmetic: 1.71 us -> 5.33 us
    all_to_all x2, waiting for transfers between devices: 10.1 us -> 29.2 us  [the longest x1 22 us: exchange(): moved = lax.all_to_all(chunks, 'theta', 0, 0, tiled=True)]
    all_to_all x2, starting transfers between devices: 30.9 us -> 18.8 us  [the longest x1 13.7 us: exchange_ids(): moved = lax.all_to_all(chunks, 'theta', 0, 0, tiled=True)]
    ppermute x10, waiting for transfers between devices: 10.5 us -> 22.6 us  [shift(): return lax.ppermute(x, axis, [(i, (i + by) % size) for i in range(size)])]
    slice x8 -> x2, local copies, waits for them, and re-layouts: 10.8 us -> 0.15 us  [the longest x1 0.07 us: exchange_ids(): inside = parts[:, 4:PARCEL - 4].reshape(4, N_THETA - 2, 2)]
    pallas_call x2, Pallas kernels: 22.2 us -> 15.4 us  [run_step(): pl.pallas_call(lambda *refs: step_kernel(second, *refs), out_shape=(struc...]
    all_to_all x1, blocking collectives: 40.4 us -> 45.4 us  [exchange(): moved = lax.all_to_all(chunks, 'theta', 0, 0, tiled=True)]
    dynamic_slice x3 -> x0, local copies, waits for them, and re-layouts: 1.95 us -> none  [exchange(): direct = lax.dynamic_slice_in_dim(moved, other * DEVS, DEVS, 0)]
    unnamed x26 -> x41, local copies, waits for them, and re-layouts: 6.57 us -> 7.55 us
  transfers between devices with their start and end apart: 21 -> 24, of which waited for: 6 -> 13; matrix products, arithmetic and copies ran while one was open for 9% -> 4% of each run, Pallas kernels for 8% -> 1%
where the time goes in v3:
time: 193 us; the launch traced here: 192 us
  waiting for transfers between devices  67.8 us (35%)
  blocking collectives  45.4 us (24%)
  starting transfers between devices  38.6 us (20%)
  Pallas kernels  22.1 us (11%)
  local copies, waits for them, and re-layouts  11.9 us (6%)
  other arithmetic  5.33 us (3%)
    all_to_all x1, blocking collectives, exchange(): moved = lax.all_to_all(chunks, 'theta', 0, 0, tiled=True)  45.4 us
    ppermute x10, waiting for transfers between devices, shift(): return lax.ppermute(x, axis, [(i, (i + by) % size) for i in range(size)])  22.6 us
    all_to_all x1, waiting for transfers between devices, exchange(): moved = lax.all_to_all(chunks, 'theta', 0, 0, tiled=True)  22 us
    pallas_call x2, Pallas kernels, run_step(): pl.pallas_call(lambda *refs: step_kernel(second, *refs), out_shape=(struc...  15.4 us
    ppermute x6, waiting for transfers between devices, across(): return lax.ppermute(x, ('patch', 'phi'), pairs)  14.1 us
    all_to_all x1, starting transfers between devices, exchange_ids(): moved = lax.all_to_all(chunks, 'theta', 0, 0, tiled=True)  13.7 us
    ppermute x10, starting transfers between devices, shift(): return lax.ppermute(x, axis, [(i, (i + by) % size) for i in range(size)])  13.1 us
    unnamed x41, local copies, waits for them, and re-layouts  7.55 us
  transfers between devices with their start and end apart: 24, of which 13 were waited for; matrix products, arithmetic and copies ran while one was open for 4% of the time, Pallas kernels for 1%

profile of v3, /device:TPU:2, one launch (start us, length us, event | category | flops | bytes accessed | tf_op | source)
XLA Modules:
  0.0 192.1 jit_solution(2024945790862104211)
XLA Ops:
  0.0 1.6 copy-done
  1.6 1.5 shard_map.64
  3.2 3.2 %collective-permute-start.3 = (f32[8,8,128]{2,1,0:T(8,128)S(1)}, f32[8,8,128]{2,1,0:T(8,128)S(1)}, u32[]{:S(2)}, u32[]{:S(2)}) collective-permute-start(f32[8,8,128]{2,1,0:T(8,128)S(1)} %get-tuple-element.27), channel_id=1, source_target_pairs={{0,3},{1,0},{2,1},{3,2},{4,7},{5,4},{6,5},{7,6},{8,11},{9,8},{10,9... | collective-permute-start | bytes 98312 | tf_op jit(solution)/shard_map/ppermute | solution.py:328
  6.5 1.5 collective-permute-start
  8.0 0.8 collective-permute-start.1
  8.9 0.2 convert_reduce_fusion.1
  9.2 0.1 select_reduce_fusion
  9.3 0.5 pad_maximum_fusion
  9.9 0.5 pad_maximum_fusion.1
  10.4 0.5 add_divide_fusion
  11.0 0.2 select_add_fusion.refs_9_.refs_13_
  11.2 0.7 fusion.12
  12.1 19.7 %collective-permute-done.refs_1_ = f32[8,2,128,128]{3,2,1,0:T(8,128)S(1)} collective-permute-done((f32[8,2,128,128]{3,2,1,0:T(8,128)}, f32[8,2,128,128]{3,2,1,0:T(8,128)S(1)}, u32[]{:S(2)}, u32[]{:S(2)}) %collective-permute-start) | collective-permute-done | bytes 1048608 | tf_op jit(solution)/shard_map/ppermute | solution.py:328
  31.8 1.3 collective-permute-done.1.refs_2_
  33.1 0.7 broadcast_in_dim.108.refs_7_.refs_11_
  33.9 0.7 broadcast_in_dim.119.refs_10_.refs_14_
  34.6 0.6 broadcast_in_dim.109.refs_8_.refs_12_
  35.2 7.8 %shard_map.65 = (f32[8,2,128,128]{3,2,1,0:T(8,128)S(1)}, f32[8,2,128,128]{3,2,1,0:T(8,128)S(1)}, f32[68,8,128]{2,1,0:T(8,128)}, f32[68,8,128]{2,1,0:T(8,128)}) custom-call(f32[8,4,128,128]{3,2,1,0:T(8,128)S(1)} %bitcast.57, f32[8,2,128,128]{3,2,1,0:T(8,128)S(1)} %collective-permute-done.refs_1_, f32[8,2,128,128]{3,2,1,0:T(8,128)} %collective-permute-done.1.refs_2_, ...), custom_call_target="tpu_custom_call" | custom-call | tf_op jit(solution)/shard_map/pallas_call | solution.py:245
  43.0 1.0 copy-done.5
  44.0 1.0 copy-done.7
  45.0 0.7 collective-permute-start.4
  45.6 0.4 collective-permute-start.5
  46.0 2.9 %collective-permute-start.9 = (s32[1,128]{1,0:T(1,128)S(1)}, s32[1,128]{1,0:T(1,128)S(1)}, u32[]{:S(2)}, u32[]{:S(2)}) collective-permute-start(s32[1,128]{1,0:T(1,128)S(1)} %pad_bitcast_fusion), channel_id=1, source_target_pairs={{0,130},{1,131},{2,128},{3,129},{128,2},{129,3},{130,0},{131,1},{4... | collective-permute-start | bytes 1544 | tf_op jit(solution)/shard_map/ppermute | solution.py:380
  48.9 0.2 collective-permute-start.8
  49.1 4.8 %collective-permute-done.9 = s32[1,128]{1,0:T(1,128)S(1)} collective-permute-done((s32[1,128]{1,0:T(1,128)S(1)}, s32[1,128]{1,0:T(1,128)S(1)}, u32[]{:S(2)}, u32[]{:S(2)}) %collective-permute-start.9) | collective-permute-done | bytes 544 | tf_op jit(solution)/shard_map/ppermute | solution.py:380
  53.9 0.5 collective-permute-start.10
  54.5 0.4 collective-permute-start.7
  55.0 0.2 collective-permute-done.10
  55.5 0.1 copy.28
  55.6 0.1 copy.27
  55.7 0.1 copy.29
  56.0 0.6 pad.13.clone
  56.6 13.7 %all-to-all-start.1 = ((s32[32,1,128]{2,1,0:T(1,128)}), s32[32,1,128]{2,1,0:T(1,128)}, u32[]{:S(2)}, u32[]{:S(2)}) async-start(s32[32,1,128]{2,1,0:T(1,128)} %pad.13.clone), calls=%async_computation.1 | async-start | bytes 32768 | tf_op jit(solution)/shard_map/all_to_all | solution.py:401
  70.4 0.1 shard_map.66
  70.5 1.0 copy-done.2
  71.5 7.3 %all-to-all-done.1 = s32[32,1,128]{2,1,0:T(1,128)} async-done(((s32[32,1,128]{2,1,0:T(1,128)}), s32[32,1,128]{2,1,0:T(1,128)}, u32[]{:S(2)}, u32[]{:S(2)}) %all-to-all-start.1) | async-done | bytes 16416 | tf_op jit(solution)/shard_map/all_to_all | solution.py:401
  78.8 5.0 %all-to-all-start = ((f32[32,64,128]{2,1,0:T(8,128)}), f32[32,64,128]{2,1,0:T(8,128)S(1)}, u32[]{:S(2)}, u32[]{:S(2)}) async-start(f32[32,64,128]{2,1,0:T(8,128)} %bitcast.60), calls=%async_computation | async-start | bytes 2097152 | tf_op jit(solution)/shard_map/all_to_all | solution.py:390
  83.8 1.5 collective-permute-start.14
  85.4 0.6 collective-permute-start.15
  86.6 0.8 fusion.2
  87.4 0.1 convert_reduce_fusion
  87.6 0.4 copy-done.11
  88.0 0.6 divide_select_fusion
  88.6 0.7 fusion.refs_3_
  89.3 22.0 %all-to-all-done = f32[32,64,128]{2,1,0:T(8,128)S(1)} async-done(((f32[32,64,128]{2,1,0:T(8,128)}), f32[32,64,128]{2,1,0:T(8,128)S(1)}, u32[]{:S(2)}, u32[]{:S(2)}) %all-to-all-start) | async-done | bytes 1048608 | tf_op jit(solution)/shard_map/all_to_all | solution.py:390
  111.3 0.8 broadcast_in_dim.127.refs_4_
  112.1 1.2 copy-done.6
  113.4 1.2 copy-done.8
  114.6 1.9 shard_map.67
  116.5 1.5 collective-permute-start.12
  118.0 0.6 collective-permute-start.13
  118.6 3.2 %collective-permute-start.17 = (f32[8,8,128]{2,1,0:T(8,128)S(1)}, f32[8,8,128]{2,1,0:T(8,128)S(1)}, u32[]{:S(2)}, u32[]{:S(2)}) collective-permute-start(f32[8,8,128]{2,1,0:T(8,128)S(1)} %get-tuple-element.38), channel_id=1, source_target_pairs={{0,3},{1,0},{2,1},{3,2},{4,7},{5,4},{6,5},{7,6},{8,11},{9,8},{10,9... | collective-permute-start | bytes 98312 | tf_op jit(solution)/shard_map/ppermute | solution.py:328
  121.8 0.4 collective-permute-done.13.refs_1_
  122.2 1.2 collective-permute-done.16.refs_7_
  123.4 7.6 %shard_map.68 = (f32[8,2,128,128]{3,2,1,0:T(8,128)S(1)}, f32[8,2,128,128]{3,2,1,0:T(8,128)S(1)}, f32[68,8,128]{2,1,0:T(8,128)S(1)}, f32[68,8,128]{2,1,0:T(8,128)S(1)}) custom-call(f32[8,8,128]{2,1,0:T(8,128)S(1)} %collective-permute-done.12.refs_0_, f32[8,8,128]{2,1,0:T(8,128)S(1)} %collective-permute-done.13.refs_1_, ...), custom_call_target="tpu_custom_call" | custom-call | tf_op jit(solution)/shard_map/pallas_call | solution.py:245
  131.0 0.6 collective-permute-start.18
  131.6 0.9 collective-permute-start.19
  132.5 8.1 %collective-permute-done.18.near = f32[68,8,128]{2,1,0:T(8,128)S(1)} collective-permute-done((f32[68,8,128]{2,1,0:T(8,128)S(1)}, f32[68,8,128]{2,1,0:T(8,128)S(1)}, u32[]{:S(2)}, u32[]{:S(2)}) %collective-permute-start.18) | collective-permute-done | bytes 278560 | tf_op jit(solution)/shard_map/ppermute | solution.py:380
  140.7 1.2 collective-permute-done.19.far
  141.9 0.2 collective-permute-done.20.mate_near
  142.2 1.3 collective-permute-done.21.mate_far
  143.5 0.1 shard_map.69
  143.6 45.4 %all_to_all.15 = f32[32,64,128]{2,1,0:T(8,128)S(1)} all-to-all(f32[32,64,128]{2,1,0:T(8,128)S(1)} %bitcast.61), channel_id=1, replica_groups=mesh['patch'=2,'theta'=32,'phi'=4] {'theta'}, dimensions={0} | all-to-all | bytes 2097152 | tf_op jit(solution)/shard_map/all_to_all | solution.py:390
  189.0 3.1 %shard_map.70 = f32[8,4,128,128]{3,2,1,0:T(8,128)} custom-call(f32[8,2,128,128]{3,2,1,0:T(8,128)S(1)} %get-tuple-element.39.refs_0_, f32[8,2,128,128]{3,2,1,0:T(8,128)S(1)} %get-tuple-element.40.refs_1_, f32[256,8,128]{2,1,0:T(8,128)S(1)} %bitcast.62, bf16[512,256]{1,0:T(8,128)(2,1)S(1)} %fusion.refs_3_, f32[512,128]{1,0:T(8,128)S(1)} %broadcast_in_dim.127.refs_4_), custom_call_target="tpu_custom_call" | custom-call | tf_op jit(solution)/shard_map/pallas_call | solution.py:317
  (75 shorter events, 1.4 us)
Async XLA Ops:
  0.0 8.9 %copy-start.15 = (s32[1,1,1,96]{3,2,1,0:T(1,128)S(1)}, s32[1,1,1,96]{3,2,1,0:T(1,128)}, u32[]{:S(2)}) copy-start(s32[1,1,1,96]{3,2,1,0:T(1,128)} %param.10) | copy-start | bytes 1156
  0.0 9.0 %copy-start.16 = (s32[1,1,1,96]{3,2,1,0:T(1,128)S(1)}, s32[1,1,1,96]{3,2,1,0:T(1,128)}, u32[]{:S(2)}) copy-start(s32[1,1,1,96]{3,2,1,0:T(1,128)} %param.11) | copy-start | bytes 1156
  0.0 9.1 %copy-start.17 = (s32[1,1,1,96]{3,2,1,0:T(1,128)S(1)}, s32[1,1,1,96]{3,2,1,0:T(1,128)}, u32[]{:S(2)}) copy-start(s32[1,1,1,96]{3,2,1,0:T(1,128)} %param.7) | copy-start | bytes 1156
  0.0 1.6 copy-start
  1.6 7.5 %copy-start.18 = (f32[1,1,1,96]{3,2,1,0:T(1,128)S(1)}, f32[1,1,1,96]{3,2,1,0:T(1,128)}, u32[]{:S(2)}) copy-start(f32[1,1,1,96]{3,2,1,0:T(1,128)} %param.9) | copy-start | bytes 1156
  1.6 9.3 %copy-start.12 = (f32[1,1,1,4,96]{4,3,2,1,0:T(4,128)S(1)}, f32[1,1,1,4,96]{4,3,2,1,0:T(4,128)}, u32[]{:S(2)}) copy-start(f32[1,1,1,4,96]{4,3,2,1,0:T(4,128)} %param.8) | copy-start | bytes 4612
  1.6 33.5 %copy-start.1 = (f32[1,8,4,128,128]{4,3,2,1,0:T(8,128)S(1)}, f32[1,8,4,128,128]{4,3,2,1,0:T(8,128)}, u32[]{:S(2)}) copy-start(f32[1,8,4,128,128]{4,3,2,1,0:T(8,128)} %param.6) | copy-start | bytes 6291460
  3.1 8.9 %collective-permute-start.2 = (f32[8,8,128]{2,1,0:T(8,128)S(1)}, f32[8,8,128]{2,1,0:T(8,128)S(1)}, u32[]{:S(2)}, u32[]{:S(2)}) collective-permute-start(f32[8,8,128]{2,1,0:T(8,128)S(1)} %get-tuple-element.26), channel_id=1, source_target_pairs={{0,1},{1,2},{2,3},{3,0},{4,5},{5,6},{6,7},{7,4},{8,9},{9,10},{10,1... | collective-permute-start | bytes 98312 | tf_op jit(solution)/shard_map/ppermute | solution.py:328
  3.2 8.8 %collective-permute-start.3 = (f32[8,8,128]{2,1,0:T(8,128)S(1)}, f32[8,8,128]{2,1,0:T(8,128)S(1)}, u32[]{:S(2)}, u32[]{:S(2)}) collective-permute-start(f32[8,8,128]{2,1,0:T(8,128)S(1)} %get-tuple-element.27), channel_id=1, source_target_pairs={{0,3},{1,0},{2,1},{3,2},{4,7},{5,4},{6,5},{7,6},{8,11},{9,8},{10,9... | collective-permute-start | bytes 98312 | tf_op jit(solution)/shard_map/ppermute | solution.py:328
  6.5 25.3 %collective-permute-start = (f32[8,2,128,128]{3,2,1,0:T(8,128)}, f32[8,2,128,128]{3,2,1,0:T(8,128)S(1)}, u32[]{:S(2)}, u32[]{:S(2)}) collective-permute-start(f32[8,2,128,128]{3,2,1,0:T(8,128)} %get-tuple-element.24), channel_id=1, source_target_pairs={{0,4},{4,8},{8,12},{12,16},{16,20},{20,24},{24,28},{28,32},{32,36}... | collective-permute-start | bytes 3145736 | tf_op jit(solution)/shard_map/ppermute | solution.py:328
  8.0 25.2 %collective-permute-start.1 = (f32[8,2,128,128]{3,2,1,0:T(8,128)}, f32[8,2,128,128]{3,2,1,0:T(8,128)}, u32[]{:S(2)}, u32[]{:S(2)}) collective-permute-start(f32[8,2,128,128]{3,2,1,0:T(8,128)} %get-tuple-element.25), channel_id=1, source_target_pairs={{0,124},{4,0},{8,4},{12,8},{16,12},{20,16},{24,20},{28,24},{32,28}... | collective-permute-start | bytes 3145736 | tf_op jit(solution)/shard_map/ppermute | solution.py:328
  11.0 22.2 %copy-start.13 = (s32[136]{0:T(256)}, s32[136]{0:T(256)S(1)}, u32[]{:S(2)}) copy-start(s32[136]{0:T(256)S(1)} %broadcast_add_fusion) | copy-start | bytes 1636
  11.2 31.8 %copy-start.3 = (f32[96,512]{1,0:T(8,128)}, f32[96,512]{1,0:T(8,128)S(1)}, u32[]{:S(2)}) copy-start(f32[96,512]{1,0:T(8,128)S(1)} %select_add_fusion.refs_9_.refs_13_) | copy-start | bytes 589828
  34.5 8.4 %copy-start.9 = (f32[2,96,128]{2,1,0:T(8,128)}, f32[2,96,128]{2,1,0:T(8,128)S(1)}, u32[]{:S(2)}) copy-start(f32[2,96,128]{2,1,0:T(8,128)S(1)} %broadcast_in_dim.119.refs_10_.refs_14_) | copy-start | bytes 294916
  35.2 13.7 %copy-start.14 = (s32[136]{0:T(256)S(1)}, s32[136]{0:T(256)}, u32[]{:S(2)}) copy-start(s32[136]{0:T(256)} %copy-done.13) | copy-start | bytes 1636
  35.2 13.7 %copy-start.19 = (pred[128]{0:T(512)(128)(4,1)S(1)}, pred[128]{0:T(512)(128)(4,1)}, u32[]{:S(2)}) copy-start(pred[128]{0:T(512)(128)(4,1)} %constant.140.clone.1) | copy-start | bytes 388
  43.0 1.0 copy-start.5
  44.0 1.0 copy-start.7
  45.0 9.5 %collective-permute-start.4 = (f32[68,8,128]{2,1,0:T(8,128)}, f32[68,8,128]{2,1,0:T(8,128)S(1)}, u32[]{:S(2)}, u32[]{:S(2)}) collective-permute-start(f32[68,8,128]{2,1,0:T(8,128)} %get-tuple-element.30), channel_id=1, source_target_pairs={{0,128},{1,129},{2,130},{3,131},{128,0},{129,1},{130,2},{131,3},{4... | collective-permute-start | bytes 835592 | tf_op jit(solution)/shard_map/ppermute | solution.py:380
  45.6 8.9 %collective-permute-start.5 = (f32[68,8,128]{2,1,0:T(8,128)}, f32[68,8,128]{2,1,0:T(8,128)S(1)}, u32[]{:S(2)}, u32[]{:S(2)}) collective-permute-start(f32[68,8,128]{2,1,0:T(8,128)} %get-tuple-element.31), channel_id=1, source_target_pairs={{0,130},{1,131},{2,128},{3,129},{128,2},{129,3},{130,0},{131,1},{4... | collective-permute-start | bytes 835592 | tf_op jit(solution)/shard_map/ppermute | solution.py:380
  46.0 7.9 %collective-permute-start.9 = (s32[1,128]{1,0:T(1,128)S(1)}, s32[1,128]{1,0:T(1,128)S(1)}, u32[]{:S(2)}, u32[]{:S(2)}) collective-permute-start(s32[1,128]{1,0:T(1,128)S(1)} %pad_bitcast_fusion), channel_id=1, source_target_pairs={{0,130},{1,131},{2,128},{3,129},{128,2},{129,3},{130,0},{131,1},{4... | collective-permute-start | bytes 1544 | tf_op jit(solution)/shard_map/ppermute | solution.py:380
  48.9 5.0 %collective-permute-start.8 = (s32[1,128]{1,0:T(1,128)S(1)}, s32[1,128]{1,0:T(1,128)S(1)}, u32[]{:S(2)}, u32[]{:S(2)}) collective-permute-start(s32[1,128]{1,0:T(1,128)S(1)} %select_bitcast_fusion), channel_id=1, source_target_pairs={{0,128},{1,129},{2,130},{3,131},{128,0},{129,1},{130,2},{131,3},{4... | collective-permute-start | bytes 1544 | tf_op jit(solution)/shard_map/ppermute | solution.py:380
  53.9 1.1 collective-permute-start.11
  53.9 1.3 collective-permute-start.10
  54.4 15.9 %collective-permute-start.6 = (f32[68,8,128]{2,1,0:T(8,128)S(1)}, f32[68,8,128]{2,1,0:T(8,128)S(1)}, u32[]{:S(2)}, u32[]{:S(2)}) collective-permute-start(f32[68,8,128]{2,1,0:T(8,128)S(1)} %collective-permute-done.4.near), channel_id=1, source_target_pairs={{0,1},{1,0},{2,3},{3,2},{4,5},{5,4},{6,7},{7,6},{8,9},{9,8},{10,11... | collective-permute-start | bytes 835592 | tf_op jit(solution)/shard_map/ppermute | solution.py:385
  54.5 15.8 %collective-permute-start.7 = (f32[68,8,128]{2,1,0:T(8,128)S(1)}, f32[68,8,128]{2,1,0:T(8,128)S(1)}, u32[]{:S(2)}, u32[]{:S(2)}) collective-permute-start(f32[68,8,128]{2,1,0:T(8,128)S(1)} %collective-permute-done.5.far), channel_id=1, source_target_pairs={{0,1},{1,0},{2,3},{3,2},{4,5},{5,4},{6,7},{7,6},{8,9},{9,8},{10,11... | collective-permute-start | bytes 835592 | tf_op jit(solution)/shard_map/ppermute | solution.py:385
  56.6 22.1 %all-to-all-start.1 = ((s32[32,1,128]{2,1,0:T(1,128)}), s32[32,1,128]{2,1,0:T(1,128)}, u32[]{:S(2)}, u32[]{:S(2)}) async-start(s32[32,1,128]{2,1,0:T(1,128)} %pad.13.clone), calls=%async_computation.1 | async-start | bytes 32768 | tf_op jit(solution)/shard_map/all_to_all | solution.py:401
  70.5 1.0 copy-start.2
  78.8 32.5 %all-to-all-start = ((f32[32,64,128]{2,1,0:T(8,128)}), f32[32,64,128]{2,1,0:T(8,128)S(1)}, u32[]{:S(2)}, u32[]{:S(2)}) async-start(f32[32,64,128]{2,1,0:T(8,128)} %bitcast.60), calls=%async_computation | async-start | bytes 2097152 | tf_op jit(solution)/shard_map/all_to_all | solution.py:390
  83.8 34.8 %collective-permute-start.14 = (f32[8,2,128,128]{3,2,1,0:T(8,128)}, f32[8,2,128,128]{3,2,1,0:T(8,128)}, u32[]{:S(2)}, u32[]{:S(2)}) collective-permute-start(f32[8,2,128,128]{3,2,1,0:T(8,128)} %copy-done.7), channel_id=1, source_target_pairs={{0,4},{4,8},{8,12},{12,16},{16,20},{20,24},{24,28},{28,32},{32,36}... | collective-permute-start | bytes 3145736 | tf_op jit(solution)/shard_map/ppermute | solution.py:328
  85.4 36.5 %collective-permute-start.15 = (f32[8,2,128,128]{3,2,1,0:T(8,128)}, f32[8,2,128,128]{3,2,1,0:T(8,128)}, u32[]{:S(2)}, u32[]{:S(2)}) collective-permute-start(f32[8,2,128,128]{3,2,1,0:T(8,128)} %copy-done.5), channel_id=1, source_target_pairs={{0,124},{4,0},{8,4},{12,8},{16,12},{20,16},{24,20},{28,24},{32,28}... | collective-permute-start | bytes 3145736 | tf_op jit(solution)/shard_map/ppermute | solution.py:328
  87.4 0.6 copy-start.11
  111.3 12.1 %copy-start.4 = (f32[96,512]{1,0:T(8,128)S(1)}, f32[96,512]{1,0:T(8,128)}, u32[]{:S(2)}) copy-start(f32[96,512]{1,0:T(8,128)} %copy-done.3) | copy-start | bytes 589828
  112.1 1.2 copy-start.6
  113.4 1.2 copy-start.8
  114.6 8.8 %copy-start.10 = (f32[2,96,128]{2,1,0:T(8,128)S(1)}, f32[2,96,128]{2,1,0:T(8,128)}, u32[]{:S(2)}) copy-start(f32[2,96,128]{2,1,0:T(8,128)} %copy-done.9) | copy-start | bytes 294916
  116.5 5.4 %collective-permute-start.12 = (f32[8,8,128]{2,1,0:T(8,128)S(1)}, f32[8,8,128]{2,1,0:T(8,128)S(1)}, u32[]{:S(2)}, u32[]{:S(2)}) collective-permute-start(f32[8,8,128]{2,1,0:T(8,128)S(1)} %get-tuple-element.33), channel_id=1, source_target_pairs={{0,4},{4,8},{8,12},{12,16},{16,20},{20,24},{24,28},{28,32},{32,36}... | collective-permute-start | bytes 98312 | tf_op jit(solution)/shard_map/ppermute | solution.py:328
  118.0 4.2 %collective-permute-start.13 = (f32[8,8,128]{2,1,0:T(8,128)S(1)}, f32[8,8,128]{2,1,0:T(8,128)S(1)}, u32[]{:S(2)}, u32[]{:S(2)}) collective-permute-start(f32[8,8,128]{2,1,0:T(8,128)S(1)} %get-tuple-element.34), channel_id=1, source_target_pairs={{0,124},{4,0},{8,4},{12,8},{16,12},{20,16},{24,20},{28,24},{32,28}... | collective-permute-start | bytes 98312 | tf_op jit(solution)/shard_map/ppermute | solution.py:328
  118.6 4.8 %collective-permute-start.16 = (f32[8,8,128]{2,1,0:T(8,128)S(1)}, f32[8,8,128]{2,1,0:T(8,128)S(1)}, u32[]{:S(2)}, u32[]{:S(2)}) collective-permute-start(f32[8,8,128]{2,1,0:T(8,128)S(1)} %get-tuple-element.37), channel_id=1, source_target_pairs={{0,1},{1,2},{2,3},{3,0},{4,5},{5,6},{6,7},{7,4},{8,9},{9,10},{10,1... | collective-permute-start | bytes 98312 | tf_op jit(solution)/shard_map/ppermute | solution.py:328
  118.6 4.8 %collective-permute-start.17 = (f32[8,8,128]{2,1,0:T(8,128)S(1)}, f32[8,8,128]{2,1,0:T(8,128)S(1)}, u32[]{:S(2)}, u32[]{:S(2)}) collective-permute-start(f32[8,8,128]{2,1,0:T(8,128)S(1)} %get-tuple-element.38), channel_id=1, source_target_pairs={{0,3},{1,0},{2,1},{3,2},{4,7},{5,4},{6,5},{7,6},{8,11},{9,8},{10,9... | collective-permute-start | bytes 98312 | tf_op jit(solution)/shard_map/ppermute | solution.py:328
  131.0 9.6 %collective-permute-start.18 = (f32[68,8,128]{2,1,0:T(8,128)S(1)}, f32[68,8,128]{2,1,0:T(8,128)S(1)}, u32[]{:S(2)}, u32[]{:S(2)}) collective-permute-start(f32[68,8,128]{2,1,0:T(8,128)S(1)} %get-tuple-element.41), channel_id=1, source_target_pairs={{0,128},{1,129},{2,130},{3,131},{128,0},{129,1},{130,2},{131,3},{4... | collective-permute-start | bytes 835592 | tf_op jit(solution)/shard_map/ppermute | solution.py:380
  131.6 10.3 %collective-permute-start.19 = (f32[68,8,128]{2,1,0:T(8,128)S(1)}, f32[68,8,128]{2,1,0:T(8,128)S(1)}, u32[]{:S(2)}, u32[]{:S(2)}) collective-permute-start(f32[68,8,128]{2,1,0:T(8,128)S(1)} %get-tuple-element.42), channel_id=1, source_target_pairs={{0,130},{1,131},{2,128},{3,129},{128,2},{129,3},{130,0},{131,1},{4... | collective-permute-start | bytes 835592 | tf_op jit(solution)/shard_map/ppermute | solution.py:380
  140.6 1.6 collective-permute-start.20
  141.9 1.6 collective-permute-start.21

commit v4 on v3

--- a/solution.py
+++ b/solution.py
@@ -35,7 +35,9 @@
     return jax.ShapeDtypeStruct(shape, jnp.float32)
 
 
+BLOCK = (FIELDS, ROWS, COLS, SHELLS)
 HALF_BLOCK = (FIELDS, HALF, COLS, SHELLS)
+QUARTER = (FIELDS, HALF, COLS // 2, SHELLS)
 RIM = (FIELDS, 8, SHELLS)
 PARCEL = 2 * N_THETA + 4
 CHUNK = 8
@@ -45,24 +47,27 @@
     return pltpu.CompilerParams(vmem_limit_bytes=mib * 1024 * 1024)
 
 
-def store_rims(top, bottom, west, east):
+def store_rims(block, west, east, width):
     for f in range(FIELDS):
         for i in range(ROWS):
-            ref = (top, bottom)[i // HALF]
-            west[f, 2 * i : 2 * i + 2, :] = ref[f, i % HALF, :2, :]
-            east[f, 2 * i : 2 * i + 2, :] = ref[f, i % HALF, COLS - 2 :, :]
-
-
-def split_kernel(fields, top, bottom, west, east, sems):
+            west[f, 2 * i : 2 * i + 2, :] = block[f, i, :2, :]
+            east[f, 2 * i : 2 * i + 2, :] = block[f, i, width - 2 : width, :]
+
+
+def split_kernel(fields, top, bottom, west, east, rims, sems):
     copies = [
-        pltpu.make_async_copy(fields.at[:, :HALF], top, sems.at[0]),
-        pltpu.make_async_copy(fields.at[:, HALF:], bottom, sems.at[1]),
+        pltpu.make_async_copy(fields.at[:, :, :8], rims.at[:, :, :8], sems.at[0]),
+        pltpu.make_async_copy(fields.at[:, :, COLS - 8 :], rims.at[:, :, 8:], sems.at[1]),
+        pltpu.make_async_copy(fields.at[:, :HALF], top, sems.at[2]),
+        pltpu.make_async_copy(fields.at[:, HALF:], bottom, sems.at[3]),
     ]
     for copy in copies:
         copy.start()
-    for copy in copies:
+    for copy in copies[:2]:
         copy.wait()
-    store_rims(top, bottom, west, east)
+    store_rims(rims, west, east, 16)
+    for copy in copies[2:]:
+        copy.wait()
 
 
 def run_split(fields):
@@ -70,10 +75,17 @@
         split_kernel,
         out_shape=(struct(*HALF_BLOCK), struct(*HALF_BLOCK), struct(*RIM), struct(*RIM)),
         in_specs=[ANY],
-        out_specs=(VMEM,) * 4,
-        scratch_shapes=[pltpu.SemaphoreType.DMA((2,))],
-        compiler_params=params(16),
+        out_specs=(ANY, ANY, VMEM, VMEM),
+        scratch_shapes=[pltpu.VMEM((FIELDS, ROWS, 16, SHELLS), jnp.float32), pltpu.SemaphoreType.DMA((4,))],
+        compiler_params=params(8),
     )(fields)
+
+
+def thirds(x):
+    high = x.astype(jnp.bfloat16)
+    rest = x - high.astype(jnp.float32)
+    middle = rest.astype(jnp.bfloat16)
+    return (rest - middle.astype(jnp.float32)).astype(jnp.bfloat16), middle, high
 
 
 def diff(far_low, near_low, near_high, far_high):
@@ -82,20 +94,25 @@
 
 def step_kernel(second, *refs):
     if second:
-        fix_above, fix_below, top, bottom, *refs = refs
-    (
-        fields, above, below, before, after, edge, row_const, phi_const, inv_r_ref, corner, angle, place,
-        new_top, new_bottom, near_send, far_send, ext, donor, send, base, sems,
-    ) = refs
-    inside = pl.ds(PAD, COLS)
-    parts = [(above, 0, HALF), (below, ROWS + 2, HALF)]
-    parts += [(top, 2, HALF), (bottom, 4, HALF)] if second else [(fields, 2, ROWS)]
+        fix_above, fix_below, block, above_west, above_east, below_west, below_east, *refs = refs
+    else:
+        above, below, *refs = refs
+    fields, before, after, edge, row_const, phi_const, inv_r_ref, corner, angle, place, new, *refs = refs
+    if not second:
+        pieces, refs = refs[:4], refs[4:]
+    near_send, far_send, ext, donor, send, base, sems = refs
+    west, east, inside = pl.ds(PAD, COLS // 2), pl.ds(PAD + COLS // 2, COLS // 2), pl.ds(PAD, COLS)
+    high, low = slice(0, HALF), slice(ROWS + 2, ROWS + 2 + HALF)
+    if second:
+        parts = [(above_west, high, west), (above_east, high, east), (below_west, low, west), (below_east, low, east)]
+    else:
+        parts = [(above, high, inside), (below, low, inside)]
+    parts.append((block if second else fields, slice(2, 2 + ROWS), inside))
     copies = [
-        pltpu.make_async_copy(ref, ext.at[:, start : start + rows, inside], sems.at[n])
-        for n, (ref, start, rows) in enumerate(parts)
+        pltpu.make_async_copy(ref, ext.at[:, rows, cols], sems.at[n]) for n, (ref, rows, cols) in enumerate(parts)
     ]
     if second:
-        copies.append(pltpu.make_async_copy(fields, base, sems.at[4]))
+        copies.append(pltpu.make_async_copy(fields, base, sems.at[5]))
     for copy in copies:
         copy.start()
     send[...] = jnp.zeros_like(send)
@@ -141,7 +158,6 @@
         omega_y, omega_z = row_const[i, 4], row_const[i, 5]
         g_p = inv_r * (inv_sine * (1.0 / (12.0 * PHI_STEP)))
         cot_r = inv_r * cot
-        out = (new_top, new_bottom)[i // HALF]
 
         def tile(j, carry):
             start = pl.multiple_of(j * 8, 8)
@@ -206,27 +222,28 @@
             centre = [q, ur, ut, up, h, br, bt, bp]
             for f in range(FIELDS):
                 if second:
-                    new = 0.5 * (base[f, i, rows, :] + centre[f] + time_step * rates[f])
+                    value = 0.5 * (base[f, i, rows, :] + centre[f] + time_step * rates[f])
                 else:
-                    new = centre[f] + time_step * rates[f]
-                out[f, i % HALF, rows, :] = new
+                    value = centre[f] + time_step * rates[f]
+                new[f, i, rows, :] = value
             return carry
 
         lax.fori_loop(0, COLS // 8, tile, 0, unroll=4)
 
-    def product(f):
-        total = None
-        for n, ref in enumerate((new_top, new_bottom)):
-            part = jnp.dot(
-                corner[:, n * HALF * COLS : (n + 1) * HALF * COLS],
-                ref[f].reshape(HALF * COLS, SHELLS),
-                precision=lax.Precision.HIGHEST,
-                preferred_element_type=jnp.float32,
-            )
-            total = part if total is None else total + part
-        return total
-
-    values = [product(f) for f in range(FIELDS)]
+    leaving = []
+    if not second:
+        for n, piece in enumerate(pieces):
+            part = new.at[:, pl.ds(HALF * (n // 2), HALF), pl.ds(COLS // 2 * (n % 2), COLS // 2)]
+            leaving.append(pltpu.make_async_copy(part, piece, sems.at[6 + n]))
+            leaving[-1].start()
+
+    values = []
+    for f in range(0, FIELDS, 2):
+        pair = jnp.concatenate([new[f + n].reshape(CELLS, SHELLS) for n in range(2)], axis=1)
+        both = jnp.dot(
+            corner[...], pair, precision=lax.Precision.HIGHEST, preferred_element_type=jnp.float32
+        )
+        values += [both[:, :SHELLS], both[:, SHELLS:]]
     c, s = angle[0], angle[1]
     for t, p in ((2, 3), (6, 7)):
         values[t], values[p] = c * values[t] - s * values[p], s * values[t] + c * values[p]
@@ -239,22 +256,30 @@
             send[spot] = column
     near_send[...] = send[:PARCEL]
     far_send[...] = send[PARCEL:]
+    for copy in leaving:
+        copy.wait()
 
 
 def run_step(second, args):
+    pieces = 0 if second else 4
     return pl.pallas_call(
         lambda *refs: step_kernel(second, *refs),
-        out_shape=(struct(*HALF_BLOCK),) * 2 + (struct(PARCEL, FIELDS, SHELLS),) * 2,
-        in_specs=[VMEM] * (4 if second else 0) + [ANY] + [VMEM] * 4 + [SMEM] * 2 + [VMEM] * 4 + [SMEM],
-        out_specs=(VMEM,) * 4,
+        out_shape=(struct(*BLOCK),) + (struct(*QUARTER),) * pieces + (struct(PARCEL, FIELDS, SHELLS),) * 2,
+        in_specs=([VMEM] * 2 + [ANY] * 5 if second else [ANY] * 2)
+        + [ANY]
+        + [VMEM] * 2
+        + [SMEM] * 2
+        + [VMEM] * 4
+        + [SMEM],
+        out_specs=(VMEM,) + (ANY,) * pieces + (VMEM,) * 2,
         scratch_shapes=[
             pltpu.VMEM((FIELDS, ROWS + 4, EXT, SHELLS), jnp.float32),
             pltpu.VMEM((SLOTS, FIELDS, SHELLS), jnp.float32),
             pltpu.VMEM((2 * PARCEL, FIELDS, SHELLS), jnp.float32),
             pltpu.VMEM((FIELDS, ROWS if second else 1, COLS, SHELLS), jnp.float32),
-            pltpu.SemaphoreType.DMA((5,)),
+            pltpu.SemaphoreType.DMA((10,)),
         ],
-        compiler_params=params(24),
+        compiler_params=params(20),
     )(*args)
 
 
@@ -278,48 +303,45 @@
     )(*args)
 
 
-def merge_kernel(last, top, bottom, moved, pick, mean, *refs):
-    if last:
-        merged, gathered = refs
-    else:
-        new_top, new_bottom, west, east, head, foot, gathered = refs
-    gathered[...] = jnp.swapaxes(moved[...], 0, 1)
+def merge_kernel(last, block, moved, pick, mean, merged, *refs):
+    kept, gathered, sem = refs[-3:]
+    copy = pltpu.make_async_copy(block, kept, sem)
+    copy.start()
+    columns = jnp.swapaxes(moved[...], 0, 1)
+    for f in range(FIELDS):
+        gathered[f // 2, :, f % 2 * SHELLS : (f % 2 + 1) * SHELLS] = columns[f]
+    copy.wait()
     weight = mean[...]
-    for f in range(FIELDS):
-        v = gathered[f]
-        high = v.astype(jnp.bfloat16)
-        rest = v - high.astype(jnp.float32)
-        middle = rest.astype(jnp.bfloat16)
-        low = (rest - middle.astype(jnp.float32)).astype(jnp.bfloat16)
-        total = sum(jnp.dot(pick[...], x, preferred_element_type=jnp.float32) for x in (low, middle, high))
-        for n, ref in enumerate((top, bottom)):
-            part = slice(n * HALF * COLS, (n + 1) * HALF * COLS)
-            kept = ref[f].reshape(HALF * COLS, SHELLS)
-            result = jnp.where(weight[part] > 0.0, total[part] * weight[part], kept).reshape(HALF, COLS, SHELLS)
-            if last:
-                merged[f, n * HALF : (n + 1) * HALF] = result
-            else:
-                (new_top, new_bottom)[n][f] = result
+    for pair in range(FIELDS // 2):
+        parts = thirds(gathered[pair])
+        total = sum(jnp.dot(pick[...], x, preferred_element_type=jnp.float32) for x in parts)
+        for n in range(2):
+            f = 2 * pair + n
+            average = total[:, n * SHELLS : (n + 1) * SHELLS] * weight
+            result = jnp.where(weight > 0.0, average, kept[f].reshape(CELLS, SHELLS))
+            merged[f] = result.reshape(ROWS, COLS, SHELLS)
     if not last:
-        store_rims(new_top, new_bottom, west, east)
+        west, east, head, foot = refs[:4]
+        store_rims(merged, west, east, COLS)
         for f in range(FIELDS):
             for i in range(HALF):
-                for ref, fix in ((new_top, head), (new_bottom, foot)):
-                    fix[f, 4 * i : 4 * i + 2, :] = ref[f, i, :2, :]
-                    fix[f, 4 * i + 2 : 4 * i + 4, :] = ref[f, i, COLS - 2 :, :]
+                for row, fix in ((i, head), (HALF + i, foot)):
+                    fix[f, 4 * i : 4 * i + 2, :] = merged[f, row, :2, :]
+                    fix[f, 4 * i + 2 : 4 * i + 4, :] = merged[f, row, COLS - 2 :, :]
 
 
 def run_merge(last, *args):
-    if last:
-        shapes = (struct(FIELDS, ROWS, COLS, SHELLS),)
-    else:
-        shapes = (struct(*HALF_BLOCK),) * 2 + (struct(*RIM),) * 4
+    shapes = (struct(*BLOCK),) + (() if last else (struct(*RIM),) * 4)
     return pl.pallas_call(
         lambda *refs: merge_kernel(last, *refs),
         out_shape=shapes,
-        in_specs=[VMEM] * 5,
+        in_specs=[ANY] + [VMEM] * 3,
         out_specs=(VMEM,) * len(shapes),
-        scratch_shapes=[pltpu.VMEM((FIELDS, N_THETA * CHUNK, SHELLS), jnp.float32)],
+        scratch_shapes=[
+            pltpu.VMEM(BLOCK, jnp.float32),
+            pltpu.VMEM((FIELDS // 2, N_THETA * CHUNK, 2 * SHELLS), jnp.float32),
+            pltpu.SemaphoreType.DMA,
+        ],
         compiler_params=params(16),
     )(*args)
 
@@ -384,11 +406,12 @@
         swap = [(0, 1), (1, 0), (2, 3), (3, 2)]
         return near, far, lax.ppermute(near, "phi", swap), lax.ppermute(far, "phi", swap)
 
-    def exchange(near, far):
+    def exchange(near, far, *first):
         chunks = run_sort(*gather_pair(near, far), core)
+        chunks, first = lax.optimization_barrier((chunks, first))
         chunks = chunks.reshape(N_THETA, CHUNK * FIELDS, SHELLS)
         moved = lax.all_to_all(chunks, "theta", 0, 0, tiled=True)
-        return moved.reshape(N_THETA * CHUNK, FIELDS, SHELLS)
+        return moved.reshape(N_THETA * CHUNK, FIELDS, SHELLS), *first
 
     def exchange_ids(sent):
         lanes = [jnp.pad(sent[n * PARCEL : (n + 1) * PARCEL], (0, SHELLS - PARCEL))[None] for n in range(2)]
@@ -412,15 +435,18 @@
     mean = jnp.where(count > 0.0, 1.0 / jnp.maximum(count, 1.0), 0.0)
     mean = jnp.broadcast_to(mean[:, None], (CELLS, SHELLS))
 
-    tail = (own, above, below, before, after, edge, row_const, phi_const, inv_r, corner, angle, place)
-    top, bottom, near, far = run_step(False, tail)
-    above, below = shift(bottom, "theta", N_THETA, 1), shift(top, "theta", N_THETA, -1)
-    top, bottom, west, east, head, foot = run_merge(False, top, bottom, exchange(near, far), pick, mean)
+    edge, pick = lax.optimization_barrier((edge, pick))
+    tail = (edge, row_const, phi_const, inv_r, corner, angle, place)
+    block, *pieces, near, far = run_step(False, (above, below, own, before, after, *tail))
+    above_west, above_east = [shift(x, "theta", N_THETA, 1) for x in pieces[2:]]
+    below_west, below_east = [shift(x, "theta", N_THETA, -1) for x in pieces[:2]]
+    moved, above_west, below_west = exchange(near, far, above_west, below_west)
+    block, west, east, head, foot = run_merge(False, block, moved, pick, mean)
     fixes = shift(foot, "theta", N_THETA, 1), shift(head, "theta", N_THETA, -1)
     before, after = shift(east, "phi", N_PHI, 1), shift(west, "phi", N_PHI, -1)
-    tail = (own, above, below, before, after, *tail[5:])
-    top, bottom, near, far = run_step(True, (*fixes, top, bottom, *tail))
-    (result,) = run_merge(True, top, bottom, exchange(near, far), pick, mean)
+    halo = (above_west, above_east, below_west, below_east)
+    block, near, far = run_step(True, (*fixes, block, *halo, own, before, after, *tail))
+    (result,) = run_merge(True, block, *exchange(near, far), pick, mean)
     return result[None]
 
 

time: 193 us -> 171 us (0.89)
  waiting for transfers between devices: 67.8 us -> 52.9 us
  blocking collectives: 45.4 us -> 36.7 us
  starting transfers between devices: 38.6 us -> 47.2 us
  local copies, waits for them, and re-layouts: 11.9 us -> 8.51 us
  other arithmetic: 5.33 us -> 3.11 us
    ppermute x10 -> x12, waiting for transfers between devices: 22.6 us -> 4.31 us  [shift(): return lax.ppermute(x, axis, [(i, (i + by) % size) for i in range(size)])]
    all_to_all x1, blocking collectives: 45.4 us -> 36.7 us  [exchange(): moved = lax.all_to_all(chunks, 'theta', 0, 0, tiled=True)]
    all_to_all x1, starting transfers between devices: 5.04 us -> 10.3 us  [exchange(): moved = lax.all_to_all(chunks, 'theta', 0, 0, tiled=True)]
    ppermute x10 -> x12, starting transfers between devices: 13.1 us -> 15.2 us  [shift(): return lax.ppermute(x, axis, [(i, (i + by) % size) for i in range(size)])]
    unnamed x41 -> x45, local copies, waits for them, and re-layouts: 7.55 us -> 5.99 us
  transfers between devices with their start and end apart: 24 -> 26, of which waited for: 13 -> 15; matrix products, arithmetic and copies ran while one was open for 4% -> 3% of each run, Pallas kernels for 1% -> 1%
where the time goes in v4:
time: 171 us; the launch traced here: 170 us
  waiting for transfers between devices  52.9 us (31%)
  starting transfers between devices  47.2 us (28%)
  blocking collectives  36.7 us (21%)
  Pallas kernels  20.5 us (12%)
  local copies, waits for them, and re-layouts  8.51 us (5%)
  other arithmetic  3.11 us (2%)
    all_to_all x1, blocking collectives, exchange(): moved = lax.all_to_all(chunks, 'theta', 0, 0, tiled=True)  36.7 us
    all_to_all x1, waiting for transfers between devices, exchange(): moved = lax.all_to_all(chunks, 'theta', 0, 0, tiled=True)  22.1 us
    ppermute x6, waiting for transfers between devices, across(): return lax.ppermute(x, ('patch', 'phi'), pairs)  15.4 us
    ppermute x12, starting transfers between devices, shift(): return lax.ppermute(x, axis, [(i, (i + by) % size) for i in range(size)])  15.2 us
    pallas_call x2, Pallas kernels, run_step(): pl.pallas_call(lambda *refs: step_kernel(second, *refs), out_shape=(struc...  14.7 us
    all_to_all x1, starting transfers between devices, exchange_ids(): moved = lax.all_to_all(chunks, 'theta', 0, 0, tiled=True)  12.5 us
    all_to_all x1, starting transfers between devices, exchange(): moved = lax.all_to_all(chunks, 'theta', 0, 0, tiled=True)  10.3 us
    ppermute x6, starting transfers between devices, across(): return lax.ppermute(x, ('patch', 'phi'), pairs)  7.18 us
  transfers between devices with their start and end apart: 26, of which 15 were waited for; matrix products, arithmetic and copies ran while one was open for 3% of the time, Pallas kernels for 1%

profile of v4, /device:TPU:2, one launch (start us, length us, event | category | flops | bytes accessed | tf_op | source)
XLA Modules:
  0.0 170.2 jit_solution(391905912279247257)
XLA Ops:
  0.0 1.6 copy-done
  1.7 1.4 shard_map.64
  3.2 3.2 %collective-permute-start.3 = (f32[8,8,128]{2,1,0:T(8,128)S(1)}, f32[8,8,128]{2,1,0:T(8,128)S(1)}, u32[]{:S(2)}, u32[]{:S(2)}) collective-permute-start(f32[8,8,128]{2,1,0:T(8,128)S(1)} %get-tuple-element.33), channel_id=1, source_target_pairs={{0,3},{1,0},{2,1},{3,2},{4,7},{5,4},{6,5},{7,6},{8,11},{9,8},{10,9... | collective-permute-start | bytes 98312 | tf_op jit(solution)/shard_map/ppermute | solution.py:350
  6.4 1.5 collective-permute-start
  7.9 0.8 collective-permute-start.1
  8.8 0.2 convert_reduce_fusion.1
  9.0 0.1 select_reduce_fusion
  9.3 0.2 select_add_fusion.refs_9_.refs_14_
  9.6 2.8 %collective-permute-start.5 = (s32[1,128]{1,0:T(1,128)S(1)}, s32[1,128]{1,0:T(1,128)S(1)}, u32[]{:S(2)}, u32[]{:S(2)}) collective-permute-start(s32[1,128]{1,0:T(1,128)S(1)} %pad_bitcast_fusion), channel_id=1, source_target_pairs={{0,130},{1,131},{2,128},{3,129},{128,2},{129,3},{130,0},{131,1},{4... | collective-permute-start | bytes 1544 | tf_op jit(solution)/shard_map/ppermute | solution.py:402
  12.5 0.1 collective-permute-start.4
  12.6 1.8 %collective-permute-done.5 = s32[1,128]{1,0:T(1,128)S(1)} collective-permute-done((s32[1,128]{1,0:T(1,128)S(1)}, s32[1,128]{1,0:T(1,128)S(1)}, u32[]{:S(2)}, u32[]{:S(2)}) %collective-permute-start.5) | collective-permute-done | bytes 544 | tf_op jit(solution)/shard_map/ppermute | solution.py:402
  14.4 0.6 collective-permute-start.7
  15.0 1.0 collective-permute-done.4
  16.0 1.1 collective-permute-done.6
  17.3 0.1 copy.27
  17.4 0.1 copy.29
  17.5 0.1 reshape.301
  17.6 0.1 copy.28
  17.9 0.6 pad.13.clone
  18.5 12.5 %all-to-all-start = ((s32[32,1,128]{2,1,0:T(1,128)}), s32[32,1,128]{2,1,0:T(1,128)S(1)}, u32[]{:S(2)}, u32[]{:S(2)}) async-start(s32[32,1,128]{2,1,0:T(1,128)} %pad.13.clone), calls=%async_computation | async-start | bytes 32768 | tf_op jit(solution)/shard_map/all_to_all | solution.py:424
  31.0 0.8 fusion.13
  32.4 0.1 stack.45.refs_6_.refs_11_
  32.5 7.0 %all-to-all-done = s32[32,1,128]{2,1,0:T(1,128)S(1)} async-done(((s32[32,1,128]{2,1,0:T(1,128)}), s32[32,1,128]{2,1,0:T(1,128)S(1)}, u32[]{:S(2)}, u32[]{:S(2)}) %all-to-all-start) | async-done | bytes 16416 | tf_op jit(solution)/shard_map/all_to_all | solution.py:424
  39.6 0.1 select_n.155
  39.9 0.1 broadcast_in_dim.115.refs_7_.refs_12_
  40.0 7.5 %shard_map.65 = (f32[8,4,128,128]{3,2,1,0:T(8,128)S(1)}, f32[8,2,64,128]{3,2,1,0:T(8,128)S(1)}, f32[8,2,64,128]{3,2,1,0:T(8,128)S(1)}, f32[8,2,64,128]{3,2,1,0:T...) custom-call(f32[8,2,128,128]{3,2,1,0:T(8,128)} %collective-permute-done.refs_0_, ...), custom_call_target="tpu_custom_call" | custom-call | tf_op jit(solution)/shard_map/pallas_call | solution.py:265
  47.5 0.8 collective-permute-start.8
  48.3 0.8 collective-permute-start.9
  49.1 0.6 collective-permute-start.12
  49.7 1.4 collective-permute-start.13
  51.1 3.9 %collective-permute-done.8.near = f32[68,8,128]{2,1,0:T(8,128)S(1)} collective-permute-done((f32[68,8,128]{2,1,0:T(8,128)S(1)}, f32[68,8,128]{2,1,0:T(8,128)S(1)}, u32[]{:S(2)}, u32[]{:S(2)}) %collective-permute-start.8) | collective-permute-done | bytes 278560 | tf_op jit(solution)/shard_map/ppermute | solution.py:402
  55.0 1.3 collective-permute-done.9.far
  56.3 0.2 collective-permute-done.10.mate_near
  56.5 1.3 collective-permute-done.11.mate_far
  57.8 0.1 shard_map.66
  58.0 1.0 copy-done.2
  59.0 2.7 %collective-permute-done.12.refs_3_ = f32[8,2,64,128]{3,2,1,0:T(8,128)S(1)} collective-permute-done((f32[8,2,64,128]{3,2,1,0:T(8,128)S(1)}, f32[8,2,64,128]{3,2,1,0:T(8,128)S(1)}, u32[]{:S(2)}, u32[]{:S(2)}) %collective-permute-start.12) | collective-permute-done | bytes 524320 | tf_op jit(solution)/shard_map/ppermute | solution.py:350
  61.7 0.8 copy-done.9
  62.5 0.8 copy-done.11
  63.3 10.3 %all-to-all-start.1 = ((f32[32,64,128]{2,1,0:T(8,128)}), f32[32,64,128]{2,1,0:T(8,128)S(1)}, u32[]{:S(2)}, u32[]{:S(2)}) async-start(f32[32,64,128]{2,1,0:T(8,128)} %bitcast.60), calls=%async_computation.1 | async-start | bytes 2097152 | tf_op jit(solution)/shard_map/all_to_all | solution.py:413
  73.7 1.5 collective-permute-start.16
  75.2 0.6 collective-permute-start.17
  75.8 0.8 convert_reduce_fusion
  76.6 0.6 divide_select_fusion
  77.2 22.1 %all-to-all-done.1 = f32[32,64,128]{2,1,0:T(8,128)S(1)} async-done(((f32[32,64,128]{2,1,0:T(8,128)}), f32[32,64,128]{2,1,0:T(8,128)S(1)}, u32[]{:S(2)}, u32[]{:S(2)}) %all-to-all-start.1) | async-done | bytes 1048608 | tf_op jit(solution)/shard_map/all_to_all | solution.py:413
  99.3 0.8 broadcast_in_dim.127.refs_3_
  100.2 1.6 copy-done.4
  101.7 1.5 shard_map.67
  103.2 1.5 collective-permute-start.14
  104.8 0.7 collective-permute-start.15
  105.5 3.2 %collective-permute-start.19 = (f32[8,8,128]{2,1,0:T(8,128)S(1)}, f32[8,8,128]{2,1,0:T(8,128)S(1)}, u32[]{:S(2)}, u32[]{:S(2)}) collective-permute-start(f32[8,8,128]{2,1,0:T(8,128)S(1)} %get-tuple-element.51), channel_id=1, source_target_pairs={{0,3},{1,0},{2,1},{3,2},{4,7},{5,4},{6,5},{7,6},{8,11},{9,8},{10,9... | collective-permute-start | bytes 98312 | tf_op jit(solution)/shard_map/ppermute | solution.py:350
  108.7 1.4 collective-permute-done.15.refs_1_
  110.1 0.2 collective-permute-done.18.refs_8_
  110.3 7.2 %shard_map.68 = (f32[8,4,128,128]{3,2,1,0:T(8,128)S(1)}, f32[68,8,128]{2,1,0:T(8,128)S(1)}, f32[68,8,128]{2,1,0:T(8,128)S(1)}) custom-call(f32[8,8,128]{2,1,0:T(8,128)S(1)} %collective-permute-done.14.refs_0_, f32[8,8,128]{2,1,0:T(8,128)S(1)} %collective-permute-done.15.refs_1_, f32[8,4,128,128]{3,2,1,0:T(8,128)S(1)} %get-tuple-element.45.refs_2_, ...), custom_call_target="tpu_custom_call" | custom-call | tf_op jit(solution)/shard_map/pallas_call | solution.py:265
  117.5 0.9 collective-permute-start.20
  118.5 1.7 %collective-permute-start.21 = (f32[68,8,128]{2,1,0:T(8,128)S(1)}, f32[68,8,128]{2,1,0:T(8,128)S(1)}, u32[]{:S(2)}, u32[]{:S(2)}) collective-permute-start(f32[68,8,128]{2,1,0:T(8,128)S(1)} %get-tuple-element.54), channel_id=1, source_target_pairs={{0,130},{1,131},{2,128},{3,129},{128,2},{129,3},{130,0},{131,1},{4... | collective-permute-start | bytes 835592 | tf_op jit(solution)/shard_map/ppermute | solution.py:402
  120.2 5.8 %collective-permute-done.20.near = f32[68,8,128]{2,1,0:T(8,128)S(1)} collective-permute-done((f32[68,8,128]{2,1,0:T(8,128)S(1)}, f32[68,8,128]{2,1,0:T(8,128)S(1)}, u32[]{:S(2)}, u32[]{:S(2)}) %collective-permute-start.20) | collective-permute-done | bytes 278560 | tf_op jit(solution)/shard_map/ppermute | solution.py:402
  126.0 1.3 collective-permute-start.22
  127.3 1.6 collective-permute-done.21.far
  128.9 0.1 collective-permute-start.23
  129.1 1.4 collective-permute-done.23.mate_far
  130.5 0.1 shard_map.69
  130.6 36.7 %all_to_all.15 = f32[32,64,128]{2,1,0:T(8,128)S(1)} all-to-all(f32[32,64,128]{2,1,0:T(8,128)S(1)} %bitcast.61), channel_id=1, replica_groups=mesh['patch'=2,'theta'=32,'phi'=4] {'theta'}, dimensions={0} | all-to-all | bytes 2097152 | tf_op jit(solution)/shard_map/all_to_all | solution.py:413
  167.3 2.7 %shard_map.70 = f32[8,4,128,128]{3,2,1,0:T(8,128)} custom-call(f32[8,4,128,128]{3,2,1,0:T(8,128)S(1)} %get-tuple-element.52.refs_0_, f32[256,8,128]{2,1,0:T(8,128)S(1)} %bitcast.62, bf16[512,256]{1,0:T(8,128)(2,1)S(1)} %fusion.refs_2_, f32[512,128]{1,0:T(8,128)S(1)} %broadcast_in_dim.127.refs_3_), custom_call_target="tpu_custom_call" | custom-call | tf_op jit(solution)/shard_map/pallas_call | solution.py:335
  (83 shorter events, 1.1 us)
Async XLA Ops:
  0.0 12.4 %copy-start.21 = (pred[128]{0:T(512)(128)(4,1)S(1)}, pred[128]{0:T(512)(128)(4,1)}, u32[]{:S(2)}) copy-start(pred[128]{0:T(512)(128)(4,1)} %constant.119.clone.1) | copy-start | bytes 388
  0.0 8.8 %copy-start.18 = (s32[1,1,1,96]{3,2,1,0:T(1,128)S(1)}, s32[1,1,1,96]{3,2,1,0:T(1,128)}, u32[]{:S(2)}) copy-start(s32[1,1,1,96]{3,2,1,0:T(1,128)} %param.11) | copy-start | bytes 1156
  0.0 8.8 %copy-start.17 = (s32[1,1,1,96]{3,2,1,0:T(1,128)S(1)}, s32[1,1,1,96]{3,2,1,0:T(1,128)}, u32[]{:S(2)}) copy-start(s32[1,1,1,96]{3,2,1,0:T(1,128)} %param.10) | copy-start | bytes 1156
  0.0 9.2 %copy-start.19 = (s32[1,1,1,96]{3,2,1,0:T(1,128)S(1)}, s32[1,1,1,96]{3,2,1,0:T(1,128)}, u32[]{:S(2)}) copy-start(s32[1,1,1,96]{3,2,1,0:T(1,128)} %param.7) | copy-start | bytes 1156
  0.0 1.6 copy-start
  1.7 7.6 %copy-start.20 = (f32[1,1,1,96]{3,2,1,0:T(1,128)S(1)}, f32[1,1,1,96]{3,2,1,0:T(1,128)}, u32[]{:S(2)}) copy-start(f32[1,1,1,96]{3,2,1,0:T(1,128)} %param.9) | copy-start | bytes 1156
  1.7 7.6 %copy-start.16 = (f32[1,1,1,4,96]{4,3,2,1,0:T(4,128)S(1)}, f32[1,1,1,4,96]{4,3,2,1,0:T(4,128)}, u32[]{:S(2)}) copy-start(f32[1,1,1,4,96]{4,3,2,1,0:T(4,128)} %param.8) | copy-start | bytes 4612
  1.7 38.3 %copy-start.1 = (f32[1,8,4,128,128]{4,3,2,1,0:T(8,128)S(1)}, f32[1,8,4,128,128]{4,3,2,1,0:T(8,128)}, u32[]{:S(2)}) copy-start(f32[1,8,4,128,128]{4,3,2,1,0:T(8,128)} %param.6) | copy-start | bytes 6291460
  3.1 6.5 %collective-permute-start.2 = (f32[8,8,128]{2,1,0:T(8,128)S(1)}, f32[8,8,128]{2,1,0:T(8,128)S(1)}, u32[]{:S(2)}, u32[]{:S(2)}) collective-permute-start(f32[8,8,128]{2,1,0:T(8,128)S(1)} %get-tuple-element.32), channel_id=1, source_target_pairs={{0,1},{1,2},{2,3},{3,0},{4,5},{5,6},{6,7},{7,4},{8,9},{9,10},{10,1... | collective-permute-start | bytes 98312 | tf_op jit(solution)/shard_map/ppermute | solution.py:350
  3.2 6.4 %collective-permute-start.3 = (f32[8,8,128]{2,1,0:T(8,128)S(1)}, f32[8,8,128]{2,1,0:T(8,128)S(1)}, u32[]{:S(2)}, u32[]{:S(2)}) collective-permute-start(f32[8,8,128]{2,1,0:T(8,128)S(1)} %get-tuple-element.33), channel_id=1, source_target_pairs={{0,3},{1,0},{2,1},{3,2},{4,7},{5,4},{6,5},{7,6},{8,11},{9,8},{10,9... | collective-permute-start | bytes 98312 | tf_op jit(solution)/shard_map/ppermute | solution.py:350
  6.4 33.3 %collective-permute-start = (f32[8,2,128,128]{3,2,1,0:T(8,128)}, f32[8,2,128,128]{3,2,1,0:T(8,128)}, u32[]{:S(2)}, u32[]{:S(2)}) collective-permute-start(f32[8,2,128,128]{3,2,1,0:T(8,128)} %get-tuple-element.30), channel_id=1, source_target_pairs={{0,4},{4,8},{8,12},{12,16},{16,20},{20,24},{24,28},{28,32},{32,36}... | collective-permute-start | bytes 3145736 | tf_op jit(solution)/shard_map/ppermute | solution.py:350
  7.9 31.9 %collective-permute-start.1 = (f32[8,2,128,128]{3,2,1,0:T(8,128)}, f32[8,2,128,128]{3,2,1,0:T(8,128)}, u32[]{:S(2)}, u32[]{:S(2)}) collective-permute-start(f32[8,2,128,128]{3,2,1,0:T(8,128)} %get-tuple-element.31), channel_id=1, source_target_pairs={{0,124},{4,0},{8,4},{12,8},{16,12},{20,16},{24,20},{28,24},{32,28}... | collective-permute-start | bytes 3145736 | tf_op jit(solution)/shard_map/ppermute | solution.py:350
  9.5 37.9 %copy-start.5 = (f32[96,512]{1,0:T(8,128)}, f32[96,512]{1,0:T(8,128)S(1)}, u32[]{:S(2)}) copy-start(f32[96,512]{1,0:T(8,128)S(1)} %select_add_fusion.refs_9_.refs_14_) | copy-start | bytes 589828
  9.6 4.8 %collective-permute-start.5 = (s32[1,128]{1,0:T(1,128)S(1)}, s32[1,128]{1,0:T(1,128)S(1)}, u32[]{:S(2)}, u32[]{:S(2)}) collective-permute-start(s32[1,128]{1,0:T(1,128)S(1)} %pad_bitcast_fusion), channel_id=1, source_target_pairs={{0,130},{1,131},{2,128},{3,129},{128,2},{129,3},{130,0},{131,1},{4... | collective-permute-start | bytes 1544 | tf_op jit(solution)/shard_map/ppermute | solution.py:402
  12.5 3.5 %collective-permute-start.4 = (s32[1,128]{1,0:T(1,128)S(1)}, s32[1,128]{1,0:T(1,128)S(1)}, u32[]{:S(2)}, u32[]{:S(2)}) collective-permute-start(s32[1,128]{1,0:T(1,128)S(1)} %select_bitcast_fusion), channel_id=1, source_target_pairs={{0,128},{1,129},{2,130},{3,131},{128,0},{129,1},{130,2},{131,3},{4... | collective-permute-start | bytes 1544 | tf_op jit(solution)/shard_map/ppermute | solution.py:402
  14.4 1.6 collective-permute-start.7
  16.0 1.1 collective-permute-start.6
  18.5 21.0 %all-to-all-start = ((s32[32,1,128]{2,1,0:T(1,128)}), s32[32,1,128]{2,1,0:T(1,128)S(1)}, u32[]{:S(2)}, u32[]{:S(2)}) async-start(s32[32,1,128]{2,1,0:T(1,128)} %pad.13.clone), calls=%async_computation | async-start | bytes 32768 | tf_op jit(solution)/shard_map/all_to_all | solution.py:424
  39.6 23.7 %copy-start.15 = (s32[256]{0:T(256)}, s32[256]{0:T(256)S(1)}, u32[]{:S(2)}) copy-start(s32[256]{0:T(256)S(1)} %select_n.155) | copy-start | bytes 3076
  39.9 7.6 %copy-start.7 = (f32[2,96,128]{2,1,0:T(8,128)}, f32[2,96,128]{2,1,0:T(8,128)S(1)}, u32[]{:S(2)}) copy-start(f32[2,96,128]{2,1,0:T(8,128)S(1)} %broadcast_in_dim.126.refs_10_.refs_15_) | copy-start | bytes 294916
  47.5 10.5 %copy-start.3 = (f32[8,4,128,128]{3,2,1,0:T(8,128)}, f32[8,4,128,128]{3,2,1,0:T(8,128)S(1)}, u32[]{:S(2)}) copy-start(f32[8,4,128,128]{3,2,1,0:T(8,128)S(1)} %get-tuple-element.36.refs_0_) | copy-start | bytes 6291460
  47.5 15.0 %copy-start.13 = (f32[8,2,64,128]{3,2,1,0:T(8,128)}, f32[8,2,64,128]{3,2,1,0:T(8,128)S(1)}, u32[]{:S(2)}) copy-start(f32[8,2,64,128]{3,2,1,0:T(8,128)S(1)} %get-tuple-element.49) | copy-start | bytes 1572868
  47.5 15.0 %copy-start.14 = (f32[8,2,64,128]{3,2,1,0:T(8,128)}, f32[8,2,64,128]{3,2,1,0:T(8,128)S(1)}, u32[]{:S(2)}) copy-start(f32[8,2,64,128]{3,2,1,0:T(8,128)S(1)} %get-tuple-element.47) | copy-start | bytes 1572868
  47.5 7.5 %collective-permute-start.8 = (f32[68,8,128]{2,1,0:T(8,128)S(1)}, f32[68,8,128]{2,1,0:T(8,128)S(1)}, u32[]{:S(2)}, u32[]{:S(2)}) collective-permute-start(f32[68,8,128]{2,1,0:T(8,128)S(1)} %get-tuple-element.37), channel_id=1, source_target_pairs={{0,128},{1,129},{2,130},{3,131},{128,0},{129,1},{130,2},{131,3},{4... | collective-permute-start | bytes 835592 | tf_op jit(solution)/shard_map/ppermute | solution.py:402
  48.3 8.0 %collective-permute-start.9 = (f32[68,8,128]{2,1,0:T(8,128)S(1)}, f32[68,8,128]{2,1,0:T(8,128)S(1)}, u32[]{:S(2)}, u32[]{:S(2)}) collective-permute-start(f32[68,8,128]{2,1,0:T(8,128)S(1)} %get-tuple-element.38), channel_id=1, source_target_pairs={{0,130},{1,131},{2,128},{3,129},{128,2},{129,3},{130,0},{131,1},{4... | collective-permute-start | bytes 835592 | tf_op jit(solution)/shard_map/ppermute | solution.py:402
  49.1 12.6 %collective-permute-start.12 = (f32[8,2,64,128]{3,2,1,0:T(8,128)S(1)}, f32[8,2,64,128]{3,2,1,0:T(8,128)S(1)}, u32[]{:S(2)}, u32[]{:S(2)}) collective-permute-start(f32[8,2,64,128]{3,2,1,0:T(8,128)S(1)} %get-tuple-element.39), channel_id=1, source_target_pairs={{0,4},{4,8},{8,12},{12,16},{16,20},{20,24},{24,28},{28,32},{32,36}... | collective-permute-start | bytes 1572872 | tf_op jit(solution)/shard_map/ppermute | solution.py:350
  49.7 12.8 %collective-permute-start.13 = (f32[8,2,64,128]{3,2,1,0:T(8,128)S(1)}, f32[8,2,64,128]{3,2,1,0:T(8,128)S(1)}, u32[]{:S(2)}, u32[]{:S(2)}) collective-permute-start(f32[8,2,64,128]{3,2,1,0:T(8,128)S(1)} %get-tuple-element.40), channel_id=1, source_target_pairs={{0,124},{4,0},{8,4},{12,8},{16,12},{20,16},{24,20},{28,24},{32,28}... | collective-permute-start | bytes 1572872 | tf_op jit(solution)/shard_map/ppermute | solution.py:350
  55.0 1.6 collective-permute-start.10
  56.3 1.6 collective-permute-start.11
  58.0 1.0 copy-start.2
  61.7 0.8 copy-start.9
  62.5 0.8 copy-start.11
  63.3 36.0 %all-to-all-start.1 = ((f32[32,64,128]{2,1,0:T(8,128)}), f32[32,64,128]{2,1,0:T(8,128)S(1)}, u32[]{:S(2)}, u32[]{:S(2)}) async-start(f32[32,64,128]{2,1,0:T(8,128)} %bitcast.60), calls=%async_computation.1 | async-start | bytes 2097152 | tf_op jit(solution)/shard_map/all_to_all | solution.py:413
  73.7 31.8 %collective-permute-start.16 = (f32[8,2,64,128]{3,2,1,0:T(8,128)}, f32[8,2,64,128]{3,2,1,0:T(8,128)}, u32[]{:S(2)}, u32[]{:S(2)}) collective-permute-start(f32[8,2,64,128]{3,2,1,0:T(8,128)} %copy-done.14), channel_id=1, source_target_pairs={{0,4},{4,8},{8,12},{12,16},{16,20},{20,24},{24,28},{28,32},{32,36}... | collective-permute-start | bytes 1572872 | tf_op jit(solution)/shard_map/ppermute | solution.py:350
  75.2 33.5 %collective-permute-start.17 = (f32[8,2,64,128]{3,2,1,0:T(8,128)}, f32[8,2,64,128]{3,2,1,0:T(8,128)}, u32[]{:S(2)}, u32[]{:S(2)}) collective-permute-start(f32[8,2,64,128]{3,2,1,0:T(8,128)} %copy-done.13), channel_id=1, source_target_pairs={{0,124},{4,0},{8,4},{12,8},{16,12},{20,16},{24,20},{28,24},{32,28}... | collective-permute-start | bytes 1572872 | tf_op jit(solution)/shard_map/ppermute | solution.py:350
  99.3 11.0 %copy-start.6 = (f32[96,512]{1,0:T(8,128)S(1)}, f32[96,512]{1,0:T(8,128)}, u32[]{:S(2)}) copy-start(f32[96,512]{1,0:T(8,128)} %copy-done.5) | copy-start | bytes 589828
  100.1 1.6 copy-start.4
  101.7 8.6 %copy-start.8 = (f32[2,96,128]{2,1,0:T(8,128)S(1)}, f32[2,96,128]{2,1,0:T(8,128)}, u32[]{:S(2)}) copy-start(f32[2,96,128]{2,1,0:T(8,128)} %copy-done.7) | copy-start | bytes 294916
  101.7 8.6 %copy-start.10 = (f32[8,2,64,128]{3,2,1,0:T(8,128)S(1)}, f32[8,2,64,128]{3,2,1,0:T(8,128)}, u32[]{:S(2)}) copy-start(f32[8,2,64,128]{3,2,1,0:T(8,128)} %copy-done.9) | copy-start | bytes 1572868
  101.7 8.6 %copy-start.12 = (f32[8,2,64,128]{3,2,1,0:T(8,128)S(1)}, f32[8,2,64,128]{3,2,1,0:T(8,128)}, u32[]{:S(2)}) copy-start(f32[8,2,64,128]{3,2,1,0:T(8,128)} %copy-done.11) | copy-start | bytes 1572868
  103.2 5.5 %collective-permute-start.14 = (f32[8,8,128]{2,1,0:T(8,128)S(1)}, f32[8,8,128]{2,1,0:T(8,128)S(1)}, u32[]{:S(2)}, u32[]{:S(2)}) collective-permute-start(f32[8,8,128]{2,1,0:T(8,128)S(1)} %get-tuple-element.43), channel_id=1, source_target_pairs={{0,4},{4,8},{8,12},{12,16},{16,20},{20,24},{24,28},{28,32},{32,36}... | collective-permute-start | bytes 98312 | tf_op jit(solution)/shard_map/ppermute | solution.py:350
  104.8 5.3 %collective-permute-start.15 = (f32[8,8,128]{2,1,0:T(8,128)S(1)}, f32[8,8,128]{2,1,0:T(8,128)S(1)}, u32[]{:S(2)}, u32[]{:S(2)}) collective-permute-start(f32[8,8,128]{2,1,0:T(8,128)S(1)} %get-tuple-element.44), channel_id=1, source_target_pairs={{0,124},{4,0},{8,4},{12,8},{16,12},{20,16},{24,20},{28,24},{32,28}... | collective-permute-start | bytes 98312 | tf_op jit(solution)/shard_map/ppermute | solution.py:350
  105.5 4.8 %collective-permute-start.18 = (f32[8,8,128]{2,1,0:T(8,128)S(1)}, f32[8,8,128]{2,1,0:T(8,128)S(1)}, u32[]{:S(2)}, u32[]{:S(2)}) collective-permute-start(f32[8,8,128]{2,1,0:T(8,128)S(1)} %get-tuple-element.50), channel_id=1, source_target_pairs={{0,1},{1,2},{2,3},{3,0},{4,5},{5,6},{6,7},{7,4},{8,9},{9,10},{10,1... | collective-permute-start | bytes 98312 | tf_op jit(solution)/shard_map/ppermute | solution.py:350
  105.5 4.8 %collective-permute-start.19 = (f32[8,8,128]{2,1,0:T(8,128)S(1)}, f32[8,8,128]{2,1,0:T(8,128)S(1)}, u32[]{:S(2)}, u32[]{:S(2)}) collective-permute-start(f32[8,8,128]{2,1,0:T(8,128)S(1)} %get-tuple-element.51), channel_id=1, source_target_pairs={{0,3},{1,0},{2,1},{3,2},{4,7},{5,4},{6,5},{7,6},{8,11},{9,8},{10,9... | collective-permute-start | bytes 98312 | tf_op jit(solution)/shard_map/ppermute | solution.py:350
  117.5 8.4 %collective-permute-start.20 = (f32[68,8,128]{2,1,0:T(8,128)S(1)}, f32[68,8,128]{2,1,0:T(8,128)S(1)}, u32[]{:S(2)}, u32[]{:S(2)}) collective-permute-start(f32[68,8,128]{2,1,0:T(8,128)S(1)} %get-tuple-element.53), channel_id=1, source_target_pairs={{0,128},{1,129},{2,130},{3,131},{128,0},{129,1},{130,2},{131,3},{4... | collective-permute-start | bytes 835592 | tf_op jit(solution)/shard_map/ppermute | solution.py:402
  118.5 10.4 %collective-permute-start.21 = (f32[68,8,128]{2,1,0:T(8,128)S(1)}, f32[68,8,128]{2,1,0:T(8,128)S(1)}, u32[]{:S(2)}, u32[]{:S(2)}) collective-permute-start(f32[68,8,128]{2,1,0:T(8,128)S(1)} %get-tuple-element.54), channel_id=1, source_target_pairs={{0,130},{1,131},{2,128},{3,129},{128,2},{129,3},{130,0},{131,1},{4... | collective-permute-start | bytes 835592 | tf_op jit(solution)/shard_map/ppermute | solution.py:402
  126.0 3.1 %collective-permute-start.22 = (f32[68,8,128]{2,1,0:T(8,128)S(1)}, f32[68,8,128]{2,1,0:T(8,128)S(1)}, u32[]{:S(2)}, u32[]{:S(2)}) collective-permute-start(f32[68,8,128]{2,1,0:T(8,128)S(1)} %collective-permute-done.20.near), channel_id=1, source_target_pairs={{0,1},{1,0},{2,3},{3,2},{4,5},{5,4},{6,7},{7,6},{8,9},{9,8},{10,11... | collective-permute-start | bytes 835592 | tf_op jit(solution)/shard_map/ppermute | solution.py:407
  128.9 1.6 collective-permute-start.23

commit v5 on v4

--- a/solution.py
+++ b/solution.py
@@ -37,7 +37,7 @@
 
 BLOCK = (FIELDS, ROWS, COLS, SHELLS)
 HALF_BLOCK = (FIELDS, HALF, COLS, SHELLS)
-QUARTER = (FIELDS, HALF, COLS // 2, SHELLS)
+EARLY = 48
 RIM = (FIELDS, 8, SHELLS)
 PARCEL = 2 * N_THETA + 4
 CHUNK = 8
@@ -101,7 +101,7 @@
     if not second:
         pieces, refs = refs[:4], refs[4:]
     near_send, far_send, ext, donor, send, base, sems = refs
-    west, east, inside = pl.ds(PAD, COLS // 2), pl.ds(PAD + COLS // 2, COLS // 2), pl.ds(PAD, COLS)
+    west, east, inside = pl.ds(PAD, EARLY), pl.ds(PAD + EARLY, COLS - EARLY), pl.ds(PAD, COLS)
     high, low = slice(0, HALF), slice(ROWS + 2, ROWS + 2 + HALF)
     if second:
         parts = [(above_west, high, west), (above_east, high, east), (below_west, low, west), (below_east, low, east)]
@@ -233,7 +233,8 @@
     leaving = []
     if not second:
         for n, piece in enumerate(pieces):
-            part = new.at[:, pl.ds(HALF * (n // 2), HALF), pl.ds(COLS // 2 * (n % 2), COLS // 2)]
+            cols = (pl.ds(0, EARLY), pl.ds(EARLY, COLS - EARLY))[n % 2]
+            part = new.at[:, pl.ds(HALF * (n // 2), HALF), cols]
             leaving.append(pltpu.make_async_copy(part, piece, sems.at[6 + n]))
             leaving[-1].start()
 
@@ -261,17 +262,17 @@
 
 
 def run_step(second, args):
-    pieces = 0 if second else 4
+    pieces = () if second else tuple(struct(FIELDS, HALF, n, SHELLS) for n in (EARLY, COLS - EARLY)) * 2
     return pl.pallas_call(
         lambda *refs: step_kernel(second, *refs),
-        out_shape=(struct(*BLOCK),) + (struct(*QUARTER),) * pieces + (struct(PARCEL, FIELDS, SHELLS),) * 2,
+        out_shape=(struct(*BLOCK), *pieces) + (struct(PARCEL, FIELDS, SHELLS),) * 2,
         in_specs=([VMEM] * 2 + [ANY] * 5 if second else [ANY] * 2)
         + [ANY]
         + [VMEM] * 2
         + [SMEM] * 2
         + [VMEM] * 4
         + [SMEM],
-        out_specs=(VMEM,) + (ANY,) * pieces + (VMEM,) * 2,
+        out_specs=(VMEM,) + (ANY,) * len(pieces) + (VMEM,) * 2,
         scratch_shapes=[
             pltpu.VMEM((FIELDS, ROWS + 4, EXT, SHELLS), jnp.float32),
             pltpu.VMEM((SLOTS, FIELDS, SHELLS), jnp.float32),

time: 171 us -> 169 us (0.988)
  waiting for transfers between devices: 52.9 us -> 51 us
    ppermute x12, waiting for transfers between devices: 4.31 us -> 1.61 us  [shift(): return lax.ppermute(x, axis, [(i, (i + by) % size) for i in range(size)])]
  transfers between devices with their start and end apart: 26 -> 26, of which waited for: 15 -> 14; matrix products, arithmetic and copies ran while one was open for 3% -> 3% of each run, Pallas kernels for 1% -> 1%
where the time goes in v5:
time: 169 us
  waiting for transfers between devices  51 us (30%)
  starting transfers between devices  46.4 us (27%)
  blocking collectives  37.9 us (22%)
  Pallas kernels  20.6 us (12%)
  local copies, waits for them, and re-layouts  8.41 us (5%)
  other arithmetic  3.07 us (2%)
    all_to_all x1, blocking collectives, exchange(): moved = lax.all_to_all(chunks, 'theta', 0, 0, tiled=True)  37.9 us
    all_to_all x1, waiting for transfers between devices, exchange(): moved = lax.all_to_all(chunks, 'theta', 0, 0, tiled=True)  22.6 us
    ppermute x6, waiting for transfers between devices, across(): return lax.ppermute(x, ('patch', 'phi'), pairs)  15.8 us
    ppermute x12, starting transfers between devices, shift(): return lax.ppermute(x, axis, [(i, (i + by) % size) for i in range(size)])  15.1 us
    pallas_call x2, Pallas kernels, run_step(): pl.pallas_call(lambda *refs: step_kernel(second, *refs), out_shape=(struc...  14.8 us
    all_to_all x1, starting transfers between devices, exchange_ids(): moved = lax.all_to_all(chunks, 'theta', 0, 0, tiled=True)  12.5 us
    all_to_all x1, starting transfers between devices, exchange(): moved = lax.all_to_all(chunks, 'theta', 0, 0, tiled=True)  10.3 us
    all_to_all x1, waiting for transfers between devices, exchange_ids(): moved = lax.all_to_all(chunks, 'theta', 0, 0, tiled=True)  6.95 us
  transfers between devices with their start and end apart: 26, of which 14 were waited for; matrix products, arithmetic and copies ran while one was open for 3% of the time, Pallas kernels for 1%

profile of v5, /device:TPU:2, one launch (start us, length us, event | category | flops | bytes accessed | tf_op | source)
XLA Modules:
  0.0 168.7 jit_solution(16839527908111225157)
XLA Ops:
  0.0 1.6 copy-done
  1.7 1.4 shard_map.64
  3.1 0.1 collective-permute-start.2
  3.2 3.2 %collective-permute-start.3 = (f32[8,8,128]{2,1,0:T(8,128)S(1)}, f32[8,8,128]{2,1,0:T(8,128)S(1)}, u32[]{:S(2)}, u32[]{:S(2)}) collective-permute-start(f32[8,8,128]{2,1,0:T(8,128)S(1)} %get-tuple-element.33), channel_id=1, source_target_pairs={{0,3},{1,0},{2,1},{3,2},{4,7},{5,4},{6,5},{7,6},{8,11},{9,8},{10,9... | collective-permute-start | bytes 98312 | tf_op jit(solution)/shard_map/ppermute | solution.py:351
  6.4 1.5 collective-permute-start
  7.9 0.8 collective-permute-start.1
  8.8 0.2 convert_reduce_fusion.1
  9.0 0.1 select_reduce_fusion
  9.3 0.2 select_add_fusion.refs_9_.refs_14_
  9.6 2.8 %collective-permute-start.5 = (s32[1,128]{1,0:T(1,128)S(1)}, s32[1,128]{1,0:T(1,128)S(1)}, u32[]{:S(2)}, u32[]{:S(2)}) collective-permute-start(s32[1,128]{1,0:T(1,128)S(1)} %pad_bitcast_fusion), channel_id=1, source_target_pairs={{0,130},{1,131},{2,128},{3,129},{128,2},{129,3},{130,0},{131,1},{4... | collective-permute-start | bytes 1544 | tf_op jit(solution)/shard_map/ppermute | solution.py:403
  12.5 0.1 collective-permute-start.4
  12.6 1.8 %collective-permute-done.5 = s32[1,128]{1,0:T(1,128)S(1)} collective-permute-done((s32[1,128]{1,0:T(1,128)S(1)}, s32[1,128]{1,0:T(1,128)S(1)}, u32[]{:S(2)}, u32[]{:S(2)}) %collective-permute-start.5) | collective-permute-done | bytes 544 | tf_op jit(solution)/shard_map/ppermute | solution.py:403
  14.4 0.6 collective-permute-start.7
  15.0 1.0 collective-permute-done.4
  16.0 1.1 collective-permute-done.6
  17.3 0.1 copy.27
  17.4 0.1 copy.29
  17.5 0.1 reshape.301
  17.6 0.1 copy.28
  17.9 0.6 pad.13.clone
  18.5 12.5 %all-to-all-start = ((s32[32,1,128]{2,1,0:T(1,128)}), s32[32,1,128]{2,1,0:T(1,128)S(1)}, u32[]{:S(2)}, u32[]{:S(2)}) async-start(s32[32,1,128]{2,1,0:T(1,128)} %pad.13.clone), calls=%async_computation | async-start | bytes 32768 | tf_op jit(solution)/shard_map/all_to_all | solution.py:425
  31.0 0.8 fusion.13
  32.5 0.1 stack.45.refs_6_.refs_11_
  32.6 7.0 %all-to-all-done = s32[32,1,128]{2,1,0:T(1,128)S(1)} async-done(((s32[32,1,128]{2,1,0:T(1,128)}), s32[32,1,128]{2,1,0:T(1,128)S(1)}, u32[]{:S(2)}, u32[]{:S(2)}) %all-to-all-start) | async-done | bytes 16416 | tf_op jit(solution)/shard_map/all_to_all | solution.py:425
  39.6 0.1 select_n.155
  39.9 0.1 broadcast_in_dim.115.refs_7_.refs_12_
  40.0 7.5 %shard_map.65 = (f32[8,4,128,128]{3,2,1,0:T(8,128)S(1)}, f32[8,2,48,128]{3,2,1,0:T(8,128)S(1)}, f32[8,2,80,128]{3,2,1,0:T(8,128)S(1)}, f32[8,2,48,128]{3,2,1,0:T...) custom-call(f32[8,2,128,128]{3,2,1,0:T(8,128)} %collective-permute-done.refs_0_, ...), custom_call_target="tpu_custom_call" | custom-call | tf_op jit(solution)/shard_map/pallas_call | solution.py:266
  47.5 0.8 collective-permute-start.8
  48.3 0.8 collective-permute-start.9
  49.1 0.6 collective-permute-start.12
  49.7 1.4 collective-permute-start.13
  51.1 3.9 %collective-permute-done.8.near = f32[68,8,128]{2,1,0:T(8,128)S(1)} collective-permute-done((f32[68,8,128]{2,1,0:T(8,128)S(1)}, f32[68,8,128]{2,1,0:T(8,128)S(1)}, u32[]{:S(2)}, u32[]{:S(2)}) %collective-permute-start.8) | collective-permute-done | bytes 278560 | tf_op jit(solution)/shard_map/ppermute | solution.py:403
  55.0 1.3 collective-permute-done.9.far
  56.3 0.2 collective-permute-done.10.mate_near
  56.6 1.3 collective-permute-done.11.mate_far
  57.9 0.1 shard_map.66
  58.0 1.0 copy-done.2
  59.0 0.8 copy-done.9
  59.8 0.8 copy-done.11
  60.6 10.3 %all-to-all-start.1 = ((f32[32,64,128]{2,1,0:T(8,128)}), f32[32,64,128]{2,1,0:T(8,128)S(1)}, u32[]{:S(2)}, u32[]{:S(2)}) async-start(f32[32,64,128]{2,1,0:T(8,128)} %bitcast.60), calls=%async_computation.1 | async-start | bytes 2097152 | tf_op jit(solution)/shard_map/all_to_all | solution.py:414
  70.9 1.5 collective-permute-start.16
  72.4 0.6 collective-permute-start.17
  73.0 0.8 convert_reduce_fusion
  73.8 0.6 divide_select_fusion
  74.4 22.6 %all-to-all-done.1 = f32[32,64,128]{2,1,0:T(8,128)S(1)} async-done(((f32[32,64,128]{2,1,0:T(8,128)}), f32[32,64,128]{2,1,0:T(8,128)S(1)}, u32[]{:S(2)}, u32[]{:S(2)}) %all-to-all-start.1) | async-done | bytes 1048608 | tf_op jit(solution)/shard_map/all_to_all | solution.py:414
  96.9 0.8 broadcast_in_dim.127.refs_3_
  97.8 1.6 copy-done.4
  99.4 1.5 shard_map.67
  100.8 1.5 collective-permute-start.14
  102.4 0.6 collective-permute-start.15
  102.9 3.2 %collective-permute-start.19 = (f32[8,8,128]{2,1,0:T(8,128)S(1)}, f32[8,8,128]{2,1,0:T(8,128)S(1)}, u32[]{:S(2)}, u32[]{:S(2)}) collective-permute-start(f32[8,8,128]{2,1,0:T(8,128)S(1)} %get-tuple-element.51), channel_id=1, source_target_pairs={{0,3},{1,0},{2,1},{3,2},{4,7},{5,4},{6,5},{7,6},{8,11},{9,8},{10,9... | collective-permute-start | bytes 98312 | tf_op jit(solution)/shard_map/ppermute | solution.py:351
  106.2 1.2 collective-permute-done.15.refs_1_
  107.4 0.3 collective-permute-done.18.refs_8_
  107.8 7.3 %shard_map.68 = (f32[8,4,128,128]{3,2,1,0:T(8,128)S(1)}, f32[68,8,128]{2,1,0:T(8,128)S(1)}, f32[68,8,128]{2,1,0:T(8,128)S(1)}) custom-call(f32[8,8,128]{2,1,0:T(8,128)S(1)} %collective-permute-done.14.refs_0_, f32[8,8,128]{2,1,0:T(8,128)S(1)} %collective-permute-done.15.refs_1_, f32[8,4,128,128]{3,2,1,0:T(8,128)S(1)} %get-tuple-element.45.refs_2_, ...), custom_call_target="tpu_custom_call" | custom-call | tf_op jit(solution)/shard_map/pallas_call | solution.py:266
  115.1 0.7 collective-permute-start.20
  115.8 1.7 collective-permute-start.21
  117.5 6.4 %collective-permute-done.20.near = f32[68,8,128]{2,1,0:T(8,128)S(1)} collective-permute-done((f32[68,8,128]{2,1,0:T(8,128)S(1)}, f32[68,8,128]{2,1,0:T(8,128)S(1)}, u32[]{:S(2)}, u32[]{:S(2)}) %collective-permute-start.20) | collective-permute-done | bytes 278560 | tf_op jit(solution)/shard_map/ppermute | solution.py:403
  123.9 1.0 collective-permute-start.22
  124.8 1.4 collective-permute-done.21.far
  126.2 0.2 collective-permute-start.23
  126.4 1.4 collective-permute-done.23.mate_far
  127.8 0.1 shard_map.69
  127.9 37.9 %all_to_all.15 = f32[32,64,128]{2,1,0:T(8,128)S(1)} all-to-all(f32[32,64,128]{2,1,0:T(8,128)S(1)} %bitcast.61), channel_id=1, replica_groups=mesh['patch'=2,'theta'=32,'phi'=4] {'theta'}, dimensions={0} | all-to-all | bytes 2097152 | tf_op jit(solution)/shard_map/all_to_all | solution.py:414
  165.8 2.7 %shard_map.70 = f32[8,4,128,128]{3,2,1,0:T(8,128)} custom-call(f32[8,4,128,128]{3,2,1,0:T(8,128)S(1)} %get-tuple-element.52.refs_0_, f32[256,8,128]{2,1,0:T(8,128)S(1)} %bitcast.62, bf16[512,256]{1,0:T(8,128)(2,1)S(1)} %fusion.refs_2_, f32[512,128]{1,0:T(8,128)S(1)} %broadcast_in_dim.127.refs_3_), custom_call_target="tpu_custom_call" | custom-call | tf_op jit(solution)/shard_map/pallas_call | solution.py:336
  (83 shorter events, 1.0 us)
Async XLA Ops:
  0.0 12.4 %copy-start.21 = (pred[128]{0:T(512)(128)(4,1)S(1)}, pred[128]{0:T(512)(128)(4,1)}, u32[]{:S(2)}) copy-start(pred[128]{0:T(512)(128)(4,1)} %constant.119.clone.1) | copy-start | bytes 388
  0.0 8.8 %copy-start.18 = (s32[1,1,1,96]{3,2,1,0:T(1,128)S(1)}, s32[1,1,1,96]{3,2,1,0:T(1,128)}, u32[]{:S(2)}) copy-start(s32[1,1,1,96]{3,2,1,0:T(1,128)} %param.11) | copy-start | bytes 1156
  0.0 8.8 %copy-start.17 = (s32[1,1,1,96]{3,2,1,0:T(1,128)S(1)}, s32[1,1,1,96]{3,2,1,0:T(1,128)}, u32[]{:S(2)}) copy-start(s32[1,1,1,96]{3,2,1,0:T(1,128)} %param.10) | copy-start | bytes 1156
  0.0 9.2 %copy-start.19 = (s32[1,1,1,96]{3,2,1,0:T(1,128)S(1)}, s32[1,1,1,96]{3,2,1,0:T(1,128)}, u32[]{:S(2)}) copy-start(s32[1,1,1,96]{3,2,1,0:T(1,128)} %param.7) | copy-start | bytes 1156
  0.0 1.6 copy-start
  1.7 7.6 %copy-start.20 = (f32[1,1,1,96]{3,2,1,0:T(1,128)S(1)}, f32[1,1,1,96]{3,2,1,0:T(1,128)}, u32[]{:S(2)}) copy-start(f32[1,1,1,96]{3,2,1,0:T(1,128)} %param.9) | copy-start | bytes 1156
  1.7 7.6 %copy-start.16 = (f32[1,1,1,4,96]{4,3,2,1,0:T(4,128)S(1)}, f32[1,1,1,4,96]{4,3,2,1,0:T(4,128)}, u32[]{:S(2)}) copy-start(f32[1,1,1,4,96]{4,3,2,1,0:T(4,128)} %param.8) | copy-start | bytes 4612
  1.7 38.3 %copy-start.1 = (f32[1,8,4,128,128]{4,3,2,1,0:T(8,128)S(1)}, f32[1,8,4,128,128]{4,3,2,1,0:T(8,128)}, u32[]{:S(2)}) copy-start(f32[1,8,4,128,128]{4,3,2,1,0:T(8,128)} %param.6) | copy-start | bytes 6291460
  3.1 6.5 %collective-permute-start.2 = (f32[8,8,128]{2,1,0:T(8,128)S(1)}, f32[8,8,128]{2,1,0:T(8,128)S(1)}, u32[]{:S(2)}, u32[]{:S(2)}) collective-permute-start(f32[8,8,128]{2,1,0:T(8,128)S(1)} %get-tuple-element.32), channel_id=1, source_target_pairs={{0,1},{1,2},{2,3},{3,0},{4,5},{5,6},{6,7},{7,4},{8,9},{9,10},{10,1... | collective-permute-start | bytes 98312 | tf_op jit(solution)/shard_map/ppermute | solution.py:351
  3.2 6.4 %collective-permute-start.3 = (f32[8,8,128]{2,1,0:T(8,128)S(1)}, f32[8,8,128]{2,1,0:T(8,128)S(1)}, u32[]{:S(2)}, u32[]{:S(2)}) collective-permute-start(f32[8,8,128]{2,1,0:T(8,128)S(1)} %get-tuple-element.33), channel_id=1, source_target_pairs={{0,3},{1,0},{2,1},{3,2},{4,7},{5,4},{6,5},{7,6},{8,11},{9,8},{10,9... | collective-permute-start | bytes 98312 | tf_op jit(solution)/shard_map/ppermute | solution.py:351
  6.4 33.3 %collective-permute-start = (f32[8,2,128,128]{3,2,1,0:T(8,128)}, f32[8,2,128,128]{3,2,1,0:T(8,128)}, u32[]{:S(2)}, u32[]{:S(2)}) collective-permute-start(f32[8,2,128,128]{3,2,1,0:T(8,128)} %get-tuple-element.30), channel_id=1, source_target_pairs={{0,4},{4,8},{8,12},{12,16},{16,20},{20,24},{24,28},{28,32},{32,36}... | collective-permute-start | bytes 3145736 | tf_op jit(solution)/shard_map/ppermute | solution.py:351
  7.9 31.9 %collective-permute-start.1 = (f32[8,2,128,128]{3,2,1,0:T(8,128)}, f32[8,2,128,128]{3,2,1,0:T(8,128)}, u32[]{:S(2)}, u32[]{:S(2)}) collective-permute-start(f32[8,2,128,128]{3,2,1,0:T(8,128)} %get-tuple-element.31), channel_id=1, source_target_pairs={{0,124},{4,0},{8,4},{12,8},{16,12},{20,16},{24,20},{28,24},{32,28}... | collective-permute-start | bytes 3145736 | tf_op jit(solution)/shard_map/ppermute | solution.py:351
  9.5 38.0 %copy-start.5 = (f32[96,512]{1,0:T(8,128)}, f32[96,512]{1,0:T(8,128)S(1)}, u32[]{:S(2)}) copy-start(f32[96,512]{1,0:T(8,128)S(1)} %select_add_fusion.refs_9_.refs_14_) | copy-start | bytes 589828
  9.6 4.8 %collective-permute-start.5 = (s32[1,128]{1,0:T(1,128)S(1)}, s32[1,128]{1,0:T(1,128)S(1)}, u32[]{:S(2)}, u32[]{:S(2)}) collective-permute-start(s32[1,128]{1,0:T(1,128)S(1)} %pad_bitcast_fusion), channel_id=1, source_target_pairs={{0,130},{1,131},{2,128},{3,129},{128,2},{129,3},{130,0},{131,1},{4... | collective-permute-start | bytes 1544 | tf_op jit(solution)/shard_map/ppermute | solution.py:403
  12.5 3.5 %collective-permute-start.4 = (s32[1,128]{1,0:T(1,128)S(1)}, s32[1,128]{1,0:T(1,128)S(1)}, u32[]{:S(2)}, u32[]{:S(2)}) collective-permute-start(s32[1,128]{1,0:T(1,128)S(1)} %select_bitcast_fusion), channel_id=1, source_target_pairs={{0,128},{1,129},{2,130},{3,131},{128,0},{129,1},{130,2},{131,3},{4... | collective-permute-start | bytes 1544 | tf_op jit(solution)/shard_map/ppermute | solution.py:403
  14.4 1.6 collective-permute-start.7
  16.0 1.1 collective-permute-start.6
  18.5 21.0 %all-to-all-start = ((s32[32,1,128]{2,1,0:T(1,128)}), s32[32,1,128]{2,1,0:T(1,128)S(1)}, u32[]{:S(2)}, u32[]{:S(2)}) async-start(s32[32,1,128]{2,1,0:T(1,128)} %pad.13.clone), calls=%async_computation | async-start | bytes 32768 | tf_op jit(solution)/shard_map/all_to_all | solution.py:425
  39.6 20.9 %copy-start.15 = (s32[256]{0:T(256)}, s32[256]{0:T(256)S(1)}, u32[]{:S(2)}) copy-start(s32[256]{0:T(256)S(1)} %select_n.155) | copy-start | bytes 3076
  39.9 7.6 %copy-start.7 = (f32[2,96,128]{2,1,0:T(8,128)}, f32[2,96,128]{2,1,0:T(8,128)S(1)}, u32[]{:S(2)}) copy-start(f32[2,96,128]{2,1,0:T(8,128)S(1)} %broadcast_in_dim.126.refs_10_.refs_15_) | copy-start | bytes 294916
  47.5 10.5 %copy-start.3 = (f32[8,4,128,128]{3,2,1,0:T(8,128)}, f32[8,4,128,128]{3,2,1,0:T(8,128)S(1)}, u32[]{:S(2)}) copy-start(f32[8,4,128,128]{3,2,1,0:T(8,128)S(1)} %get-tuple-element.36.refs_0_) | copy-start | bytes 6291460
  47.5 12.3 %copy-start.13 = (f32[8,2,80,128]{3,2,1,0:T(8,128)}, f32[8,2,80,128]{3,2,1,0:T(8,128)S(1)}, u32[]{:S(2)}) copy-start(f32[8,2,80,128]{3,2,1,0:T(8,128)S(1)} %get-tuple-element.49) | copy-start | bytes 1966084
  47.5 12.3 %copy-start.14 = (f32[8,2,80,128]{3,2,1,0:T(8,128)}, f32[8,2,80,128]{3,2,1,0:T(8,128)S(1)}, u32[]{:S(2)}) copy-start(f32[8,2,80,128]{3,2,1,0:T(8,128)S(1)} %get-tuple-element.47) | copy-start | bytes 1966084
  47.5 7.5 %collective-permute-start.8 = (f32[68,8,128]{2,1,0:T(8,128)S(1)}, f32[68,8,128]{2,1,0:T(8,128)S(1)}, u32[]{:S(2)}, u32[]{:S(2)}) collective-permute-start(f32[68,8,128]{2,1,0:T(8,128)S(1)} %get-tuple-element.37), channel_id=1, source_target_pairs={{0,128},{1,129},{2,130},{3,131},{128,0},{129,1},{130,2},{131,3},{4... | collective-permute-start | bytes 835592 | tf_op jit(solution)/shard_map/ppermute | solution.py:403
  48.3 8.0 %collective-permute-start.9 = (f32[68,8,128]{2,1,0:T(8,128)S(1)}, f32[68,8,128]{2,1,0:T(8,128)S(1)}, u32[]{:S(2)}, u32[]{:S(2)}) collective-permute-start(f32[68,8,128]{2,1,0:T(8,128)S(1)} %get-tuple-element.38), channel_id=1, source_target_pairs={{0,130},{1,131},{2,128},{3,129},{128,2},{129,3},{130,0},{131,1},{4... | collective-permute-start | bytes 835592 | tf_op jit(solution)/shard_map/ppermute | solution.py:403
  49.1 9.9 %collective-permute-start.12 = (f32[8,2,48,128]{3,2,1,0:T(8,128)S(1)}, f32[8,2,48,128]{3,2,1,0:T(8,128)S(1)}, u32[]{:S(2)}, u32[]{:S(2)}) collective-permute-start(f32[8,2,48,128]{3,2,1,0:T(8,128)S(1)} %get-tuple-element.39), channel_id=1, source_target_pairs={{0,4},{4,8},{8,12},{12,16},{16,20},{20,24},{24,28},{28,32},{32,36}... | collective-permute-start | bytes 1179656 | tf_op jit(solution)/shard_map/ppermute | solution.py:351
  49.7 10.1 %collective-permute-start.13 = (f32[8,2,48,128]{3,2,1,0:T(8,128)S(1)}, f32[8,2,48,128]{3,2,1,0:T(8,128)S(1)}, u32[]{:S(2)}, u32[]{:S(2)}) collective-permute-start(f32[8,2,48,128]{3,2,1,0:T(8,128)S(1)} %get-tuple-element.40), channel_id=1, source_target_pairs={{0,124},{4,0},{8,4},{12,8},{16,12},{20,16},{24,20},{28,24},{32,28}... | collective-permute-start | bytes 1179656 | tf_op jit(solution)/shard_map/ppermute | solution.py:351
  55.0 1.6 collective-permute-start.10
  56.3 1.6 collective-permute-start.11
  58.0 1.0 copy-start.2
  59.0 0.8 copy-start.9
  59.8 0.8 copy-start.11
  60.6 36.3 %all-to-all-start.1 = ((f32[32,64,128]{2,1,0:T(8,128)}), f32[32,64,128]{2,1,0:T(8,128)S(1)}, u32[]{:S(2)}, u32[]{:S(2)}) async-start(f32[32,64,128]{2,1,0:T(8,128)} %bitcast.60), calls=%async_computation.1 | async-start | bytes 2097152 | tf_op jit(solution)/shard_map/all_to_all | solution.py:414
  70.9 32.1 %collective-permute-start.16 = (f32[8,2,80,128]{3,2,1,0:T(8,128)}, f32[8,2,80,128]{3,2,1,0:T(8,128)}, u32[]{:S(2)}, u32[]{:S(2)}) collective-permute-start(f32[8,2,80,128]{3,2,1,0:T(8,128)} %copy-done.14), channel_id=1, source_target_pairs={{0,4},{4,8},{8,12},{12,16},{16,20},{20,24},{24,28},{28,32},{32,36}... | collective-permute-start | bytes 1966088 | tf_op jit(solution)/shard_map/ppermute | solution.py:351
  72.4 33.8 %collective-permute-start.17 = (f32[8,2,80,128]{3,2,1,0:T(8,128)}, f32[8,2,80,128]{3,2,1,0:T(8,128)}, u32[]{:S(2)}, u32[]{:S(2)}) collective-permute-start(f32[8,2,80,128]{3,2,1,0:T(8,128)} %copy-done.13), channel_id=1, source_target_pairs={{0,124},{4,0},{8,4},{12,8},{16,12},{20,16},{24,20},{28,24},{32,28}... | collective-permute-start | bytes 1966088 | tf_op jit(solution)/shard_map/ppermute | solution.py:351
  96.9 10.9 %copy-start.6 = (f32[96,512]{1,0:T(8,128)S(1)}, f32[96,512]{1,0:T(8,128)}, u32[]{:S(2)}) copy-start(f32[96,512]{1,0:T(8,128)} %copy-done.5) | copy-start | bytes 589828
  97.8 1.6 copy-start.4
  99.4 8.4 %copy-start.8 = (f32[2,96,128]{2,1,0:T(8,128)S(1)}, f32[2,96,128]{2,1,0:T(8,128)}, u32[]{:S(2)}) copy-start(f32[2,96,128]{2,1,0:T(8,128)} %copy-done.7) | copy-start | bytes 294916
  99.4 8.4 %copy-start.10 = (f32[8,2,48,128]{3,2,1,0:T(8,128)S(1)}, f32[8,2,48,128]{3,2,1,0:T(8,128)}, u32[]{:S(2)}) copy-start(f32[8,2,48,128]{3,2,1,0:T(8,128)} %copy-done.9) | copy-start | bytes 1179652
  99.4 8.4 %copy-start.12 = (f32[8,2,48,128]{3,2,1,0:T(8,128)S(1)}, f32[8,2,48,128]{3,2,1,0:T(8,128)}, u32[]{:S(2)}) copy-start(f32[8,2,48,128]{3,2,1,0:T(8,128)} %copy-done.11) | copy-start | bytes 1179652
  100.8 5.4 %collective-permute-start.14 = (f32[8,8,128]{2,1,0:T(8,128)S(1)}, f32[8,8,128]{2,1,0:T(8,128)S(1)}, u32[]{:S(2)}, u32[]{:S(2)}) collective-permute-start(f32[8,8,128]{2,1,0:T(8,128)S(1)} %get-tuple-element.43), channel_id=1, source_target_pairs={{0,4},{4,8},{8,12},{12,16},{16,20},{20,24},{24,28},{28,32},{32,36}... | collective-permute-start | bytes 98312 | tf_op jit(solution)/shard_map/ppermute | solution.py:351
  102.4 5.1 %collective-permute-start.15 = (f32[8,8,128]{2,1,0:T(8,128)S(1)}, f32[8,8,128]{2,1,0:T(8,128)S(1)}, u32[]{:S(2)}, u32[]{:S(2)}) collective-permute-start(f32[8,8,128]{2,1,0:T(8,128)S(1)} %get-tuple-element.44), channel_id=1, source_target_pairs={{0,124},{4,0},{8,4},{12,8},{16,12},{20,16},{24,20},{28,24},{32,28}... | collective-permute-start | bytes 98312 | tf_op jit(solution)/shard_map/ppermute | solution.py:351
  102.9 4.8 %collective-permute-start.18 = (f32[8,8,128]{2,1,0:T(8,128)S(1)}, f32[8,8,128]{2,1,0:T(8,128)S(1)}, u32[]{:S(2)}, u32[]{:S(2)}) collective-permute-start(f32[8,8,128]{2,1,0:T(8,128)S(1)} %get-tuple-element.50), channel_id=1, source_target_pairs={{0,1},{1,2},{2,3},{3,0},{4,5},{5,6},{6,7},{7,4},{8,9},{9,10},{10,1... | collective-permute-start | bytes 98312 | tf_op jit(solution)/shard_map/ppermute | solution.py:351
  102.9 4.8 %collective-permute-start.19 = (f32[8,8,128]{2,1,0:T(8,128)S(1)}, f32[8,8,128]{2,1,0:T(8,128)S(1)}, u32[]{:S(2)}, u32[]{:S(2)}) collective-permute-start(f32[8,8,128]{2,1,0:T(8,128)S(1)} %get-tuple-element.51), channel_id=1, source_target_pairs={{0,3},{1,0},{2,1},{3,2},{4,7},{5,4},{6,5},{7,6},{8,11},{9,8},{10,9... | collective-permute-start | bytes 98312 | tf_op jit(solution)/shard_map/ppermute | solution.py:351
  115.1 8.8 %collective-permute-start.20 = (f32[68,8,128]{2,1,0:T(8,128)S(1)}, f32[68,8,128]{2,1,0:T(8,128)S(1)}, u32[]{:S(2)}, u32[]{:S(2)}) collective-permute-start(f32[68,8,128]{2,1,0:T(8,128)S(1)} %get-tuple-element.53), channel_id=1, source_target_pairs={{0,128},{1,129},{2,130},{3,131},{128,0},{129,1},{130,2},{131,3},{4... | collective-permute-start | bytes 835592 | tf_op jit(solution)/shard_map/ppermute | solution.py:403
  115.8 10.4 %collective-permute-start.21 = (f32[68,8,128]{2,1,0:T(8,128)S(1)}, f32[68,8,128]{2,1,0:T(8,128)S(1)}, u32[]{:S(2)}, u32[]{:S(2)}) collective-permute-start(f32[68,8,128]{2,1,0:T(8,128)S(1)} %get-tuple-element.54), channel_id=1, source_target_pairs={{0,130},{1,131},{2,128},{3,129},{128,2},{129,3},{130,0},{131,1},{4... | collective-permute-start | bytes 835592 | tf_op jit(solution)/shard_map/ppermute | solution.py:403
  123.9 2.5 %collective-permute-start.22 = (f32[68,8,128]{2,1,0:T(8,128)S(1)}, f32[68,8,128]{2,1,0:T(8,128)S(1)}, u32[]{:S(2)}, u32[]{:S(2)}) collective-permute-start(f32[68,8,128]{2,1,0:T(8,128)S(1)} %collective-permute-done.20.near), channel_id=1, source_target_pairs={{0,1},{1,0},{2,3},{3,2},{4,5},{5,4},{6,7},{7,6},{8,9},{9,8},{10,11... | collective-permute-start | bytes 835592 | tf_op jit(solution)/shard_map/ppermute | solution.py:408
  126.2 1.6 collective-permute-start.23

commit v6 on v5

--- a/solution.py
+++ b/solution.py
@@ -107,14 +107,19 @@
         parts = [(above_west, high, west), (above_east, high, east), (below_west, low, west), (below_east, low, east)]
     else:
         parts = [(above, high, inside), (below, low, inside)]
-    parts.append((block if second else fields, slice(2, 2 + ROWS), inside))
-    copies = [
-        pltpu.make_async_copy(ref, ext.at[:, rows, cols], sems.at[n]) for n, (ref, rows, cols) in enumerate(parts)
-    ]
+    half = len(parts) // 2
+    source = block if second else fields
+    moves = [(ref, ext.at[:, rows, cols]) for ref, rows, cols in parts[:half]]
+    moves += [(source.at[:, i], ext.at[:, 2 + i, inside]) for i in range(ROWS)]
+    moves += [(ref, ext.at[:, rows, cols]) for ref, rows, cols in parts[half:]]
     if second:
-        copies.append(pltpu.make_async_copy(fields, base, sems.at[5]))
+        moves += [(fields.at[:, i], base.at[:, i]) for i in range(ROWS)]
+    copies = [pltpu.make_async_copy(ref, into, sems.at[n]) for n, (ref, into) in enumerate(moves)]
     for copy in copies:
         copy.start()
+    needed = [copies[: half + 3], [copies[half + 3]], copies[half + 4 : 2 * half + 4], []]
+    if second:
+        needed = [list(some) + [copies[2 * half + 4 + i]] for i, some in enumerate(needed)]
     send[...] = jnp.zeros_like(send)
     west_edge, east_edge = edge[2] > 0, edge[3] > 0
     for f in range(FIELDS):
@@ -122,22 +127,18 @@
             pair = slice(2 * i, 2 * i + 2)
             ext[f, 2 + i, PAD - 2 : PAD, :] = jnp.where(west_edge, 0.0, before[f, pair, :])
             ext[f, 2 + i, PAD + COLS : PAD + COLS + 2, :] = jnp.where(east_edge, 0.0, after[f, pair, :])
-    for copy in copies:
-        copy.wait()
-    if second:
-        for f in range(FIELDS):
-            for i in range(HALF):
-                for start, ref in ((0, fix_above), (6, fix_below)):
-                    ext[f, start + i, PAD : PAD + 2, :] = ref[f, 4 * i : 4 * i + 2, :]
-                    ext[f, start + i, PAD + COLS - 2 : PAD + COLS, :] = ref[f, 4 * i + 2 : 4 * i + 4, :]
-
-    @pl.when(edge[0] > 0)
-    def _():
-        ext[:, 0:HALF] = jnp.zeros((FIELDS, HALF, EXT, SHELLS), jnp.float32)
-
-    @pl.when(edge[1] > 0)
-    def _():
-        ext[:, 6 : 6 + HALF] = jnp.zeros((FIELDS, HALF, EXT, SHELLS), jnp.float32)
+
+    def finish(n):
+        start, fix = ((0, fix_above), (6, fix_below))[n] if second else (6 * n, None)
+        if second:
+            for f in range(FIELDS):
+                for i in range(HALF):
+                    ext[f, start + i, PAD : PAD + 2, :] = fix[f, 4 * i : 4 * i + 2, :]
+                    ext[f, start + i, PAD + COLS - 2 : PAD + COLS, :] = fix[f, 4 * i + 2 : 4 * i + 4, :]
+
+        @pl.when(edge[n] > 0)
+        def _():
+            ext[:, start : start + HALF] = jnp.zeros((FIELDS, HALF, EXT, SHELLS), jnp.float32)
 
     lane = lax.broadcasted_iota(jnp.int32, (8, SHELLS), 1)
     first, second_lane = lane < 1, lane < 2
@@ -154,6 +155,10 @@
         return diff(far_low, near_low, near_high, far_high) * k_r
 
     for i in range(ROWS):
+        for copy in needed[i]:
+            copy.wait()
+        if i in (0, 2):
+            finish(i // 2)
         sine, cosine, cot, inv_sine = [row_const[i, k] for k in range(4)]
         omega_y, omega_z = row_const[i, 4], row_const[i, 5]
         g_p = inv_r * (inv_sine * (1.0 / (12.0 * PHI_STEP)))
@@ -235,7 +240,7 @@
         for n, piece in enumerate(pieces):
             cols = (pl.ds(0, EARLY), pl.ds(EARLY, COLS - EARLY))[n % 2]
             part = new.at[:, pl.ds(HALF * (n // 2), HALF), cols]
-            leaving.append(pltpu.make_async_copy(part, piece, sems.at[6 + n]))
+            leaving.append(pltpu.make_async_copy(part, piece, sems.at[12 + n]))
             leaving[-1].start()
 
     values = []
@@ -278,7 +283,7 @@
             pltpu.VMEM((SLOTS, FIELDS, SHELLS), jnp.float32),
             pltpu.VMEM((2 * PARCEL, FIELDS, SHELLS), jnp.float32),
             pltpu.VMEM((FIELDS, ROWS if second else 1, COLS, SHELLS), jnp.float32),
-            pltpu.SemaphoreType.DMA((10,)),
+            pltpu.SemaphoreType.DMA((16,)),
         ],
         compiler_params=params(20),
     )(*args)
@@ -305,8 +310,9 @@
 
 
 def merge_kernel(last, block, moved, pick, mean, merged, *refs):
-    kept, gathered, sem = refs[-3:]
-    copy = pltpu.make_async_copy(block, kept, sem)
+    kept, gathered, sems = refs[-3:]
+    copy = pltpu.make_async_copy(block, kept, sems.at[0])
+    leaving = []
     copy.start()
     columns = jnp.swapaxes(moved[...], 0, 1)
     for f in range(FIELDS):
@@ -320,7 +326,16 @@
             f = 2 * pair + n
             average = total[:, n * SHELLS : (n + 1) * SHELLS] * weight
             result = jnp.where(weight > 0.0, average, kept[f].reshape(CELLS, SHELLS))
-            merged[f] = result.reshape(ROWS, COLS, SHELLS)
+            if last:
+                kept[f] = result.reshape(ROWS, COLS, SHELLS)
+            else:
+                merged[f] = result.reshape(ROWS, COLS, SHELLS)
+        if last:
+            fields = pl.ds(2 * pair, 2)
+            leaving.append(pltpu.make_async_copy(kept.at[fields], merged.at[fields], sems.at[1 + pair]))
+            leaving[-1].start()
+    for copy in leaving:
+        copy.wait()
     if not last:
         west, east, head, foot = refs[:4]
         store_rims(merged, west, east, COLS)
@@ -337,11 +352,11 @@
         lambda *refs: merge_kernel(last, *refs),
         out_shape=shapes,
         in_specs=[ANY] + [VMEM] * 3,
-        out_specs=(VMEM,) * len(shapes),
+        out_specs=(ANY if last else VMEM,) + (VMEM,) * (len(shapes) - 1),
         scratch_shapes=[
             pltpu.VMEM(BLOCK, jnp.float32),
             pltpu.VMEM((FIELDS // 2, N_THETA * CHUNK, 2 * SHELLS), jnp.float32),
-            pltpu.SemaphoreType.DMA,
+            pltpu.SemaphoreType.DMA((5,)),
         ],
         compiler_params=params(16),
     )(*args)

time: 169 us -> 169 us (level)
  no operation moved by 1% of the time
where the time goes in v6:
time: 169 us; the launch traced here: 168 us
  waiting for transfers between devices  51 us (30%)
  starting transfers between devices  46.4 us (27%)
  blocking collectives  37.9 us (22%)
  Pallas kernels  20.1 us (12%)
  local copies, waits for them, and re-layouts  8.41 us (5%)
  other arithmetic  3.07 us (2%)
    all_to_all x1, blocking collectives, exchange(): moved = lax.all_to_all(chunks, 'theta', 0, 0, tiled=True)  37.9 us
    all_to_all x1, waiting for transfers between devices, exchange(): moved = lax.all_to_all(chunks, 'theta', 0, 0, tiled=True)  22.6 us
    ppermute x6, waiting for transfers between devices, across(): return lax.ppermute(x, ('patch', 'phi'), pairs)  15.8 us
    ppermute x12, starting transfers between devices, shift(): return lax.ppermute(x, axis, [(i, (i + by) % size) for i in range(size)])  15.1 us
    pallas_call x2, Pallas kernels, run_step(): pl.pallas_call(lambda *refs: step_kernel(second, *refs), out_shape=(struc...  14.4 us
    all_to_all x1, starting transfers between devices, exchange_ids(): moved = lax.all_to_all(chunks, 'theta', 0, 0, tiled=True)  12.5 us
    all_to_all x1, starting transfers between devices, exchange(): moved = lax.all_to_all(chunks, 'theta', 0, 0, tiled=True)  10.3 us
    all_to_all x1, waiting for transfers between devices, exchange_ids(): moved = lax.all_to_all(chunks, 'theta', 0, 0, tiled=True)  6.95 us
  transfers between devices with their start and end apart: 26, of which 14 were waited for; matrix products, arithmetic and copies ran while one was open for 3% of the time, Pallas kernels for 1%

profile of v6, /device:TPU:2, one launch (start us, length us, event | category | flops | bytes accessed | tf_op | source)
XLA Modules:
  0.0 168.1 jit_solution(17409540147020347768)
XLA Ops:
  0.0 1.6 copy-done
  1.7 1.4 shard_map.64
  3.1 0.1 collective-permute-start.2
  3.2 3.2 %collective-permute-start.3 = (f32[8,8,128]{2,1,0:T(8,128)S(1)}, f32[8,8,128]{2,1,0:T(8,128)S(1)}, u32[]{:S(2)}, u32[]{:S(2)}) collective-permute-start(f32[8,8,128]{2,1,0:T(8,128)S(1)} %get-tuple-element.33), channel_id=1, source_target_pairs={{0,3},{1,0},{2,1},{3,2},{4,7},{5,4},{6,5},{7,6},{8,11},{9,8},{10,9... | collective-permute-start | bytes 98312 | tf_op jit(solution)/shard_map/ppermute | solution.py:366
  6.4 1.5 collective-permute-start
  7.9 0.8 collective-permute-start.1
  8.8 0.2 convert_reduce_fusion.1
  9.0 0.1 select_reduce_fusion
  9.3 0.2 select_add_fusion.refs_9_.refs_14_
  9.6 2.8 %collective-permute-start.5 = (s32[1,128]{1,0:T(1,128)S(1)}, s32[1,128]{1,0:T(1,128)S(1)}, u32[]{:S(2)}, u32[]{:S(2)}) collective-permute-start(s32[1,128]{1,0:T(1,128)S(1)} %pad_bitcast_fusion), channel_id=1, source_target_pairs={{0,130},{1,131},{2,128},{3,129},{128,2},{129,3},{130,0},{131,1},{4... | collective-permute-start | bytes 1544 | tf_op jit(solution)/shard_map/ppermute | solution.py:418
  12.5 0.1 collective-permute-start.4
  12.6 1.8 %collective-permute-done.5 = s32[1,128]{1,0:T(1,128)S(1)} collective-permute-done((s32[1,128]{1,0:T(1,128)S(1)}, s32[1,128]{1,0:T(1,128)S(1)}, u32[]{:S(2)}, u32[]{:S(2)}) %collective-permute-start.5) | collective-permute-done | bytes 544 | tf_op jit(solution)/shard_map/ppermute | solution.py:418
  14.4 0.6 collective-permute-start.7
  15.0 1.0 collective-permute-done.4
  16.0 1.1 collective-permute-done.6
  17.3 0.1 copy.27
  17.4 0.1 copy.29
  17.5 0.1 reshape.301
  17.6 0.1 copy.28
  17.9 0.6 pad.13.clone
  18.5 12.5 %all-to-all-start = ((s32[32,1,128]{2,1,0:T(1,128)}), s32[32,1,128]{2,1,0:T(1,128)S(1)}, u32[]{:S(2)}, u32[]{:S(2)}) async-start(s32[32,1,128]{2,1,0:T(1,128)} %pad.13.clone), calls=%async_computation | async-start | bytes 32768 | tf_op jit(solution)/shard_map/all_to_all | solution.py:440
  31.0 0.8 fusion.13
  32.5 0.1 stack.45.refs_6_.refs_11_
  32.6 7.0 %all-to-all-done = s32[32,1,128]{2,1,0:T(1,128)S(1)} async-done(((s32[32,1,128]{2,1,0:T(1,128)}), s32[32,1,128]{2,1,0:T(1,128)S(1)}, u32[]{:S(2)}, u32[]{:S(2)}) %all-to-all-start) | async-done | bytes 16416 | tf_op jit(solution)/shard_map/all_to_all | solution.py:440
  39.6 0.1 select_n.155
  39.9 0.1 broadcast_in_dim.115.refs_7_.refs_12_
  40.0 7.3 %shard_map.65 = (f32[8,4,128,128]{3,2,1,0:T(8,128)S(1)}, f32[8,2,48,128]{3,2,1,0:T(8,128)S(1)}, f32[8,2,80,128]{3,2,1,0:T(8,128)S(1)}, f32[8,2,48,128]{3,2,1,0:T...) custom-call(f32[8,2,128,128]{3,2,1,0:T(8,128)} %collective-permute-done.refs_0_, ...), custom_call_target="tpu_custom_call" | custom-call | tf_op jit(solution)/shard_map/pallas_call | solution.py:271
  47.3 0.8 collective-permute-start.8
  48.1 0.8 collective-permute-start.9
  48.9 0.6 collective-permute-start.12
  49.5 1.4 collective-permute-start.13
  50.9 3.9 %collective-permute-done.8.near = f32[68,8,128]{2,1,0:T(8,128)S(1)} collective-permute-done((f32[68,8,128]{2,1,0:T(8,128)S(1)}, f32[68,8,128]{2,1,0:T(8,128)S(1)}, u32[]{:S(2)}, u32[]{:S(2)}) %collective-permute-start.8) | collective-permute-done | bytes 278560 | tf_op jit(solution)/shard_map/ppermute | solution.py:418
  54.8 1.3 collective-permute-done.9.far
  56.1 0.2 collective-permute-done.10.mate_near
  56.3 1.3 collective-permute-done.11.mate_far
  57.6 0.1 shard_map.66
  57.8 1.0 copy-done.2
  58.8 0.8 copy-done.9
  59.6 0.8 copy-done.11
  60.3 10.3 %all-to-all-start.1 = ((f32[32,64,128]{2,1,0:T(8,128)}), f32[32,64,128]{2,1,0:T(8,128)S(1)}, u32[]{:S(2)}, u32[]{:S(2)}) async-start(f32[32,64,128]{2,1,0:T(8,128)} %bitcast.60), calls=%async_computation.1 | async-start | bytes 2097152 | tf_op jit(solution)/shard_map/all_to_all | solution.py:429
  70.6 1.5 collective-permute-start.16
  72.2 0.6 collective-permute-start.17
  72.7 0.8 convert_reduce_fusion
  73.5 0.6 divide_select_fusion
  74.1 22.6 %all-to-all-done.1 = f32[32,64,128]{2,1,0:T(8,128)S(1)} async-done(((f32[32,64,128]{2,1,0:T(8,128)}), f32[32,64,128]{2,1,0:T(8,128)S(1)}, u32[]{:S(2)}, u32[]{:S(2)}) %all-to-all-start.1) | async-done | bytes 1048608 | tf_op jit(solution)/shard_map/all_to_all | solution.py:429
  96.7 0.8 broadcast_in_dim.127.refs_3_
  97.5 1.6 copy-done.4
  99.1 1.5 shard_map.67
  100.6 1.5 collective-permute-start.14
  102.2 0.6 collective-permute-start.15
  102.7 3.2 %collective-permute-start.19 = (f32[8,8,128]{2,1,0:T(8,128)S(1)}, f32[8,8,128]{2,1,0:T(8,128)S(1)}, u32[]{:S(2)}, u32[]{:S(2)}) collective-permute-start(f32[8,8,128]{2,1,0:T(8,128)S(1)} %get-tuple-element.51), channel_id=1, source_target_pairs={{0,3},{1,0},{2,1},{3,2},{4,7},{5,4},{6,5},{7,6},{8,11},{9,8},{10,9... | collective-permute-start | bytes 98312 | tf_op jit(solution)/shard_map/ppermute | solution.py:366
  106.0 1.2 collective-permute-done.15.refs_1_
  107.2 0.4 collective-permute-done.18.refs_8_
  107.6 7.1 %shard_map.68 = (f32[8,4,128,128]{3,2,1,0:T(8,128)S(1)}, f32[68,8,128]{2,1,0:T(8,128)S(1)}, f32[68,8,128]{2,1,0:T(8,128)S(1)}) custom-call(f32[8,8,128]{2,1,0:T(8,128)S(1)} %collective-permute-done.14.refs_0_, f32[8,8,128]{2,1,0:T(8,128)S(1)} %collective-permute-done.15.refs_1_, f32[8,4,128,128]{3,2,1,0:T(8,128)S(1)} %get-tuple-element.45.refs_2_, ...), custom_call_target="tpu_custom_call" | custom-call | tf_op jit(solution)/shard_map/pallas_call | solution.py:271
  114.8 0.7 collective-permute-start.20
  115.5 1.7 collective-permute-start.21
  117.1 6.4 %collective-permute-done.20.near = f32[68,8,128]{2,1,0:T(8,128)S(1)} collective-permute-done((f32[68,8,128]{2,1,0:T(8,128)S(1)}, f32[68,8,128]{2,1,0:T(8,128)S(1)}, u32[]{:S(2)}, u32[]{:S(2)}) %collective-permute-start.20) | collective-permute-done | bytes 278560 | tf_op jit(solution)/shard_map/ppermute | solution.py:418
  123.6 0.9 collective-permute-start.22
  124.5 1.4 collective-permute-done.21.far
  125.9 0.2 collective-permute-start.23
  126.0 1.4 collective-permute-done.23.mate_far
  127.4 0.1 shard_map.69
  127.6 37.9 %all_to_all.15 = f32[32,64,128]{2,1,0:T(8,128)S(1)} all-to-all(f32[32,64,128]{2,1,0:T(8,128)S(1)} %bitcast.61), channel_id=1, replica_groups=mesh['patch'=2,'theta'=32,'phi'=4] {'theta'}, dimensions={0} | all-to-all | bytes 2097152 | tf_op jit(solution)/shard_map/all_to_all | solution.py:429
  165.4 2.5 %shard_map.70 = f32[8,4,128,128]{3,2,1,0:T(8,128)} custom-call(f32[8,4,128,128]{3,2,1,0:T(8,128)S(1)} %get-tuple-element.52.refs_0_, f32[256,8,128]{2,1,0:T(8,128)S(1)} %bitcast.62, bf16[512,256]{1,0:T(8,128)(2,1)S(1)} %fusion.refs_2_, f32[512,128]{1,0:T(8,128)S(1)} %broadcast_in_dim.127.refs_3_), custom_call_target="tpu_custom_call" | custom-call | tf_op jit(solution)/shard_map/pallas_call | solution.py:351
  (83 shorter events, 1.0 us)
Async XLA Ops:
  0.0 12.4 %copy-start.21 = (pred[128]{0:T(512)(128)(4,1)S(1)}, pred[128]{0:T(512)(128)(4,1)}, u32[]{:S(2)}) copy-start(pred[128]{0:T(512)(128)(4,1)} %constant.119.clone.1) | copy-start | bytes 388
  0.0 8.8 %copy-start.18 = (s32[1,1,1,96]{3,2,1,0:T(1,128)S(1)}, s32[1,1,1,96]{3,2,1,0:T(1,128)}, u32[]{:S(2)}) copy-start(s32[1,1,1,96]{3,2,1,0:T(1,128)} %param.11) | copy-start | bytes 1156
  0.0 8.8 %copy-start.17 = (s32[1,1,1,96]{3,2,1,0:T(1,128)S(1)}, s32[1,1,1,96]{3,2,1,0:T(1,128)}, u32[]{:S(2)}) copy-start(s32[1,1,1,96]{3,2,1,0:T(1,128)} %param.10) | copy-start | bytes 1156
  0.0 9.2 %copy-start.19 = (s32[1,1,1,96]{3,2,1,0:T(1,128)S(1)}, s32[1,1,1,96]{3,2,1,0:T(1,128)}, u32[]{:S(2)}) copy-start(s32[1,1,1,96]{3,2,1,0:T(1,128)} %param.7) | copy-start | bytes 1156
  0.0 1.6 copy-start
  1.7 7.6 %copy-start.20 = (f32[1,1,1,96]{3,2,1,0:T(1,128)S(1)}, f32[1,1,1,96]{3,2,1,0:T(1,128)}, u32[]{:S(2)}) copy-start(f32[1,1,1,96]{3,2,1,0:T(1,128)} %param.9) | copy-start | bytes 1156
  1.7 7.6 %copy-start.16 = (f32[1,1,1,4,96]{4,3,2,1,0:T(4,128)S(1)}, f32[1,1,1,4,96]{4,3,2,1,0:T(4,128)}, u32[]{:S(2)}) copy-start(f32[1,1,1,4,96]{4,3,2,1,0:T(4,128)} %param.8) | copy-start | bytes 4612
  1.7 38.3 %copy-start.1 = (f32[1,8,4,128,128]{4,3,2,1,0:T(8,128)S(1)}, f32[1,8,4,128,128]{4,3,2,1,0:T(8,128)}, u32[]{:S(2)}) copy-start(f32[1,8,4,128,128]{4,3,2,1,0:T(8,128)} %param.6) | copy-start | bytes 6291460
  3.1 6.5 %collective-permute-start.2 = (f32[8,8,128]{2,1,0:T(8,128)S(1)}, f32[8,8,128]{2,1,0:T(8,128)S(1)}, u32[]{:S(2)}, u32[]{:S(2)}) collective-permute-start(f32[8,8,128]{2,1,0:T(8,128)S(1)} %get-tuple-element.32), channel_id=1, source_target_pairs={{0,1},{1,2},{2,3},{3,0},{4,5},{5,6},{6,7},{7,4},{8,9},{9,10},{10,1... | collective-permute-start | bytes 98312 | tf_op jit(solution)/shard_map/ppermute | solution.py:366
  3.2 6.4 %collective-permute-start.3 = (f32[8,8,128]{2,1,0:T(8,128)S(1)}, f32[8,8,128]{2,1,0:T(8,128)S(1)}, u32[]{:S(2)}, u32[]{:S(2)}) collective-permute-start(f32[8,8,128]{2,1,0:T(8,128)S(1)} %get-tuple-element.33), channel_id=1, source_target_pairs={{0,3},{1,0},{2,1},{3,2},{4,7},{5,4},{6,5},{7,6},{8,11},{9,8},{10,9... | collective-permute-start | bytes 98312 | tf_op jit(solution)/shard_map/ppermute | solution.py:366
  6.4 33.3 %collective-permute-start = (f32[8,2,128,128]{3,2,1,0:T(8,128)}, f32[8,2,128,128]{3,2,1,0:T(8,128)}, u32[]{:S(2)}, u32[]{:S(2)}) collective-permute-start(f32[8,2,128,128]{3,2,1,0:T(8,128)} %get-tuple-element.30), channel_id=1, source_target_pairs={{0,4},{4,8},{8,12},{12,16},{16,20},{20,24},{24,28},{28,32},{32,36}... | collective-permute-start | bytes 3145736 | tf_op jit(solution)/shard_map/ppermute | solution.py:366
  7.9 31.9 %collective-permute-start.1 = (f32[8,2,128,128]{3,2,1,0:T(8,128)}, f32[8,2,128,128]{3,2,1,0:T(8,128)}, u32[]{:S(2)}, u32[]{:S(2)}) collective-permute-start(f32[8,2,128,128]{3,2,1,0:T(8,128)} %get-tuple-element.31), channel_id=1, source_target_pairs={{0,124},{4,0},{8,4},{12,8},{16,12},{20,16},{24,20},{28,24},{32,28}... | collective-permute-start | bytes 3145736 | tf_op jit(solution)/shard_map/ppermute | solution.py:366
  9.5 37.7 %copy-start.5 = (f32[96,512]{1,0:T(8,128)}, f32[96,512]{1,0:T(8,128)S(1)}, u32[]{:S(2)}) copy-start(f32[96,512]{1,0:T(8,128)S(1)} %select_add_fusion.refs_9_.refs_14_) | copy-start | bytes 589828
  9.6 4.8 %collective-permute-start.5 = (s32[1,128]{1,0:T(1,128)S(1)}, s32[1,128]{1,0:T(1,128)S(1)}, u32[]{:S(2)}, u32[]{:S(2)}) collective-permute-start(s32[1,128]{1,0:T(1,128)S(1)} %pad_bitcast_fusion), channel_id=1, source_target_pairs={{0,130},{1,131},{2,128},{3,129},{128,2},{129,3},{130,0},{131,1},{4... | collective-permute-start | bytes 1544 | tf_op jit(solution)/shard_map/ppermute | solution.py:418
  12.5 3.5 %collective-permute-start.4 = (s32[1,128]{1,0:T(1,128)S(1)}, s32[1,128]{1,0:T(1,128)S(1)}, u32[]{:S(2)}, u32[]{:S(2)}) collective-permute-start(s32[1,128]{1,0:T(1,128)S(1)} %select_bitcast_fusion), channel_id=1, source_target_pairs={{0,128},{1,129},{2,130},{3,131},{128,0},{129,1},{130,2},{131,3},{4... | collective-permute-start | bytes 1544 | tf_op jit(solution)/shard_map/ppermute | solution.py:418
  14.4 1.6 collective-permute-start.7
  16.0 1.1 collective-permute-start.6
  18.5 21.0 %all-to-all-start = ((s32[32,1,128]{2,1,0:T(1,128)}), s32[32,1,128]{2,1,0:T(1,128)S(1)}, u32[]{:S(2)}, u32[]{:S(2)}) async-start(s32[32,1,128]{2,1,0:T(1,128)} %pad.13.clone), calls=%async_computation | async-start | bytes 32768 | tf_op jit(solution)/shard_map/all_to_all | solution.py:440
  39.6 20.7 %copy-start.15 = (s32[256]{0:T(256)}, s32[256]{0:T(256)S(1)}, u32[]{:S(2)}) copy-start(s32[256]{0:T(256)S(1)} %select_n.155) | copy-start | bytes 3076
  39.9 7.4 %copy-start.7 = (f32[2,96,128]{2,1,0:T(8,128)}, f32[2,96,128]{2,1,0:T(8,128)S(1)}, u32[]{:S(2)}) copy-start(f32[2,96,128]{2,1,0:T(8,128)S(1)} %broadcast_in_dim.126.refs_10_.refs_15_) | copy-start | bytes 294916
  47.3 10.5 %copy-start.3 = (f32[8,4,128,128]{3,2,1,0:T(8,128)}, f32[8,4,128,128]{3,2,1,0:T(8,128)S(1)}, u32[]{:S(2)}) copy-start(f32[8,4,128,128]{3,2,1,0:T(8,128)S(1)} %get-tuple-element.36.refs_0_) | copy-start | bytes 6291460
  47.3 12.3 %copy-start.13 = (f32[8,2,80,128]{3,2,1,0:T(8,128)}, f32[8,2,80,128]{3,2,1,0:T(8,128)S(1)}, u32[]{:S(2)}) copy-start(f32[8,2,80,128]{3,2,1,0:T(8,128)S(1)} %get-tuple-element.49) | copy-start | bytes 1966084
  47.3 12.3 %copy-start.14 = (f32[8,2,80,128]{3,2,1,0:T(8,128)}, f32[8,2,80,128]{3,2,1,0:T(8,128)S(1)}, u32[]{:S(2)}) copy-start(f32[8,2,80,128]{3,2,1,0:T(8,128)S(1)} %get-tuple-element.47) | copy-start | bytes 1966084
  47.3 7.5 %collective-permute-start.8 = (f32[68,8,128]{2,1,0:T(8,128)S(1)}, f32[68,8,128]{2,1,0:T(8,128)S(1)}, u32[]{:S(2)}, u32[]{:S(2)}) collective-permute-start(f32[68,8,128]{2,1,0:T(8,128)S(1)} %get-tuple-element.37), channel_id=1, source_target_pairs={{0,128},{1,129},{2,130},{3,131},{128,0},{129,1},{130,2},{131,3},{4... | collective-permute-start | bytes 835592 | tf_op jit(solution)/shard_map/ppermute | solution.py:418
  48.1 8.0 %collective-permute-start.9 = (f32[68,8,128]{2,1,0:T(8,128)S(1)}, f32[68,8,128]{2,1,0:T(8,128)S(1)}, u32[]{:S(2)}, u32[]{:S(2)}) collective-permute-start(f32[68,8,128]{2,1,0:T(8,128)S(1)} %get-tuple-element.38), channel_id=1, source_target_pairs={{0,130},{1,131},{2,128},{3,129},{128,2},{129,3},{130,0},{131,1},{4... | collective-permute-start | bytes 835592 | tf_op jit(solution)/shard_map/ppermute | solution.py:418
  48.9 9.9 %collective-permute-start.12 = (f32[8,2,48,128]{3,2,1,0:T(8,128)S(1)}, f32[8,2,48,128]{3,2,1,0:T(8,128)S(1)}, u32[]{:S(2)}, u32[]{:S(2)}) collective-permute-start(f32[8,2,48,128]{3,2,1,0:T(8,128)S(1)} %get-tuple-element.39), channel_id=1, source_target_pairs={{0,4},{4,8},{8,12},{12,16},{16,20},{20,24},{24,28},{28,32},{32,36}... | collective-permute-start | bytes 1179656 | tf_op jit(solution)/shard_map/ppermute | solution.py:366
  49.5 10.1 %collective-permute-start.13 = (f32[8,2,48,128]{3,2,1,0:T(8,128)S(1)}, f32[8,2,48,128]{3,2,1,0:T(8,128)S(1)}, u32[]{:S(2)}, u32[]{:S(2)}) collective-permute-start(f32[8,2,48,128]{3,2,1,0:T(8,128)S(1)} %get-tuple-element.40), channel_id=1, source_target_pairs={{0,124},{4,0},{8,4},{12,8},{16,12},{20,16},{24,20},{28,24},{32,28}... | collective-permute-start | bytes 1179656 | tf_op jit(solution)/shard_map/ppermute | solution.py:366
  54.8 1.6 collective-permute-start.10
  56.1 1.6 collective-permute-start.11
  57.8 1.0 copy-start.2
  58.8 0.8 copy-start.9
  59.6 0.8 copy-start.11
  60.3 36.3 %all-to-all-start.1 = ((f32[32,64,128]{2,1,0:T(8,128)}), f32[32,64,128]{2,1,0:T(8,128)S(1)}, u32[]{:S(2)}, u32[]{:S(2)}) async-start(f32[32,64,128]{2,1,0:T(8,128)} %bitcast.60), calls=%async_computation.1 | async-start | bytes 2097152 | tf_op jit(solution)/shard_map/all_to_all | solution.py:429
  70.6 32.1 %collective-permute-start.16 = (f32[8,2,80,128]{3,2,1,0:T(8,128)}, f32[8,2,80,128]{3,2,1,0:T(8,128)}, u32[]{:S(2)}, u32[]{:S(2)}) collective-permute-start(f32[8,2,80,128]{3,2,1,0:T(8,128)} %copy-done.14), channel_id=1, source_target_pairs={{0,4},{4,8},{8,12},{12,16},{16,20},{20,24},{24,28},{28,32},{32,36}... | collective-permute-start | bytes 1966088 | tf_op jit(solution)/shard_map/ppermute | solution.py:366
  72.2 33.8 %collective-permute-start.17 = (f32[8,2,80,128]{3,2,1,0:T(8,128)}, f32[8,2,80,128]{3,2,1,0:T(8,128)}, u32[]{:S(2)}, u32[]{:S(2)}) collective-permute-start(f32[8,2,80,128]{3,2,1,0:T(8,128)} %copy-done.13), channel_id=1, source_target_pairs={{0,124},{4,0},{8,4},{12,8},{16,12},{20,16},{24,20},{28,24},{32,28}... | collective-permute-start | bytes 1966088 | tf_op jit(solution)/shard_map/ppermute | solution.py:366
  96.7 10.9 %copy-start.6 = (f32[96,512]{1,0:T(8,128)S(1)}, f32[96,512]{1,0:T(8,128)}, u32[]{:S(2)}) copy-start(f32[96,512]{1,0:T(8,128)} %copy-done.5) | copy-start | bytes 589828
  97.5 1.6 copy-start.4
  99.1 8.5 %copy-start.8 = (f32[2,96,128]{2,1,0:T(8,128)S(1)}, f32[2,96,128]{2,1,0:T(8,128)}, u32[]{:S(2)}) copy-start(f32[2,96,128]{2,1,0:T(8,128)} %copy-done.7) | copy-start | bytes 294916
  99.1 8.5 %copy-start.10 = (f32[8,2,48,128]{3,2,1,0:T(8,128)S(1)}, f32[8,2,48,128]{3,2,1,0:T(8,128)}, u32[]{:S(2)}) copy-start(f32[8,2,48,128]{3,2,1,0:T(8,128)} %copy-done.9) | copy-start | bytes 1179652
  99.1 8.5 %copy-start.12 = (f32[8,2,48,128]{3,2,1,0:T(8,128)S(1)}, f32[8,2,48,128]{3,2,1,0:T(8,128)}, u32[]{:S(2)}) copy-start(f32[8,2,48,128]{3,2,1,0:T(8,128)} %copy-done.11) | copy-start | bytes 1179652
  100.6 5.4 %collective-permute-start.14 = (f32[8,8,128]{2,1,0:T(8,128)S(1)}, f32[8,8,128]{2,1,0:T(8,128)S(1)}, u32[]{:S(2)}, u32[]{:S(2)}) collective-permute-start(f32[8,8,128]{2,1,0:T(8,128)S(1)} %get-tuple-element.43), channel_id=1, source_target_pairs={{0,4},{4,8},{8,12},{12,16},{16,20},{20,24},{24,28},{28,32},{32,36}... | collective-permute-start | bytes 98312 | tf_op jit(solution)/shard_map/ppermute | solution.py:366
  102.2 5.0 %collective-permute-start.15 = (f32[8,8,128]{2,1,0:T(8,128)S(1)}, f32[8,8,128]{2,1,0:T(8,128)S(1)}, u32[]{:S(2)}, u32[]{:S(2)}) collective-permute-start(f32[8,8,128]{2,1,0:T(8,128)S(1)} %get-tuple-element.44), channel_id=1, source_target_pairs={{0,124},{4,0},{8,4},{12,8},{16,12},{20,16},{24,20},{28,24},{32,28}... | collective-permute-start | bytes 98312 | tf_op jit(solution)/shard_map/ppermute | solution.py:366
  102.7 4.8 %collective-permute-start.18 = (f32[8,8,128]{2,1,0:T(8,128)S(1)}, f32[8,8,128]{2,1,0:T(8,128)S(1)}, u32[]{:S(2)}, u32[]{:S(2)}) collective-permute-start(f32[8,8,128]{2,1,0:T(8,128)S(1)} %get-tuple-element.50), channel_id=1, source_target_pairs={{0,1},{1,2},{2,3},{3,0},{4,5},{5,6},{6,7},{7,4},{8,9},{9,10},{10,1... | collective-permute-start | bytes 98312 | tf_op jit(solution)/shard_map/ppermute | solution.py:366
  102.7 4.8 %collective-permute-start.19 = (f32[8,8,128]{2,1,0:T(8,128)S(1)}, f32[8,8,128]{2,1,0:T(8,128)S(1)}, u32[]{:S(2)}, u32[]{:S(2)}) collective-permute-start(f32[8,8,128]{2,1,0:T(8,128)S(1)} %get-tuple-element.51), channel_id=1, source_target_pairs={{0,3},{1,0},{2,1},{3,2},{4,7},{5,4},{6,5},{7,6},{8,11},{9,8},{10,9... | collective-permute-start | bytes 98312 | tf_op jit(solution)/shard_map/ppermute | solution.py:366
  114.8 8.8 %collective-permute-start.20 = (f32[68,8,128]{2,1,0:T(8,128)S(1)}, f32[68,8,128]{2,1,0:T(8,128)S(1)}, u32[]{:S(2)}, u32[]{:S(2)}) collective-permute-start(f32[68,8,128]{2,1,0:T(8,128)S(1)} %get-tuple-element.53), channel_id=1, source_target_pairs={{0,128},{1,129},{2,130},{3,131},{128,0},{129,1},{130,2},{131,3},{4... | collective-permute-start | bytes 835592 | tf_op jit(solution)/shard_map/ppermute | solution.py:418
  115.5 10.4 %collective-permute-start.21 = (f32[68,8,128]{2,1,0:T(8,128)S(1)}, f32[68,8,128]{2,1,0:T(8,128)S(1)}, u32[]{:S(2)}, u32[]{:S(2)}) collective-permute-start(f32[68,8,128]{2,1,0:T(8,128)S(1)} %get-tuple-element.54), channel_id=1, source_target_pairs={{0,130},{1,131},{2,128},{3,129},{128,2},{129,3},{130,0},{131,1},{4... | collective-permute-start | bytes 835592 | tf_op jit(solution)/shard_map/ppermute | solution.py:418
  123.6 2.5 %collective-permute-start.22 = (f32[68,8,128]{2,1,0:T(8,128)S(1)}, f32[68,8,128]{2,1,0:T(8,128)S(1)}, u32[]{:S(2)}, u32[]{:S(2)}) collective-permute-start(f32[68,8,128]{2,1,0:T(8,128)S(1)} %collective-permute-done.20.near), channel_id=1, source_target_pairs={{0,1},{1,0},{2,3},{3,2},{4,5},{5,4},{6,7},{7,6},{8,9},{9,8},{10,11... | collective-permute-start | bytes 835592 | tf_op jit(solution)/shard_map/ppermute | solution.py:423
  125.9 1.6 collective-permute-start.23

commit v7 on v6

--- a/solution.py
+++ b/solution.py
@@ -233,7 +233,7 @@
                 new[f, i, rows, :] = value
             return carry
 
-        lax.fori_loop(0, COLS // 8, tile, 0, unroll=4)
+        lax.fori_loop(0, COLS // 8, tile, 0, unroll=8)
 
     leaving = []
     if not second:
@@ -431,7 +431,8 @@
 
     def exchange_ids(sent):
         lanes = [jnp.pad(sent[n * PARCEL : (n + 1) * PARCEL], (0, SHELLS - PARCEL))[None] for n in range(2)]
-        parts = jnp.concatenate(gather_pair(*lanes))
+        own = jnp.concatenate([across(lanes[0], 0), across(lanes[1], 2)])
+        parts = jnp.concatenate([own, lax.ppermute(own, "phi", [(0, 1), (1, 0), (2, 3), (3, 2)])])
         inside = parts[:, 4 : PARCEL - 4].reshape(4, N_THETA - 2, 2)
         first = lax.dynamic_slice_in_dim(parts, 2 * core[0], 2, 1)[:, None]
         final = lax.dynamic_slice_in_dim(parts, PARCEL - 4 + 2 * core[0], 2, 1)[:, None]

time: 169 us -> 168 us (level)
  transfers between devices with their start and end apart: 26 -> 25, of which waited for: 14 -> 14; matrix products, arithmetic and copies ran while one was open for 3% -> 3% of each run, Pallas kernels for 1% -> 1%
where the time goes in v7:
time: 168 us
  waiting for transfers between devices  51.6 us (31%)
  starting transfers between devices  45.8 us (27%)
  blocking collectives  38.1 us (23%)
  Pallas kernels  19.5 us (12%)
  local copies, waits for them, and re-layouts  8.39 us (5%)
  other arithmetic  2.94 us (2%)
    all_to_all x1, blocking collectives, exchange(): moved = lax.all_to_all(chunks, 'theta', 0, 0, tiled=True)  38.1 us
    all_to_all x1, waiting for transfers between devices, exchange(): moved = lax.all_to_all(chunks, 'theta', 0, 0, tiled=True)  22.7 us
    ppermute x6, waiting for transfers between devices, across(): return lax.ppermute(x, ('patch', 'phi'), pairs)  16.2 us
    ppermute x12, starting transfers between devices, shift(): return lax.ppermute(x, axis, [(i, (i + by) % size) for i in range(size)])  15.1 us
    pallas_call x2, Pallas kernels, run_step(): pl.pallas_call(lambda *refs: step_kernel(second, *refs), out_shape=(struc...  13.9 us
    all_to_all x1, starting transfers between devices, exchange_ids(): moved = lax.all_to_all(chunks, 'theta', 0, 0, tiled=True)  12.5 us
    all_to_all x1, starting transfers between devices, exchange(): moved = lax.all_to_all(chunks, 'theta', 0, 0, tiled=True)  10.1 us
    all_to_all x1, waiting for transfers between devices, exchange_ids(): moved = lax.all_to_all(chunks, 'theta', 0, 0, tiled=True)  7.16 us
  transfers between devices with their start and end apart: 25, of which 14 were waited for; matrix products, arithmetic and copies ran while one was open for 3% of the time, Pallas kernels for 1%

profile of v7, /device:TPU:2, one launch (start us, length us, event | category | flops | bytes accessed | tf_op | source)
XLA Modules:
  0.0 167.6 jit_solution(16561996615003854851)
XLA Ops:
  0.0 1.6 copy-done
  1.7 1.4 shard_map.64
  3.1 0.1 collective-permute-start.2
  3.1 3.2 %collective-permute-start.3 = (f32[8,8,128]{2,1,0:T(8,128)S(1)}, f32[8,8,128]{2,1,0:T(8,128)S(1)}, u32[]{:S(2)}, u32[]{:S(2)}) collective-permute-start(f32[8,8,128]{2,1,0:T(8,128)S(1)} %get-tuple-element.33), channel_id=1, source_target_pairs={{0,3},{1,0},{2,1},{3,2},{4,7},{5,4},{6,5},{7,6},{8,11},{9,8},{10,9... | collective-permute-start | bytes 98312 | tf_op jit(solution)/shard_map/ppermute | solution.py:366
  6.4 1.5 collective-permute-start
  7.9 0.8 collective-permute-start.1
  8.8 0.2 convert_reduce_fusion.1
  9.0 0.1 select_reduce_fusion
  9.3 0.2 select_add_fusion.refs_9_.refs_14_
  9.6 2.9 %collective-permute-start.5 = (s32[1,128]{1,0:T(1,128)S(1)}, s32[1,128]{1,0:T(1,128)S(1)}, u32[]{:S(2)}, u32[]{:S(2)}) collective-permute-start(s32[1,128]{1,0:T(1,128)S(1)} %pad_bitcast_fusion), channel_id=1, source_target_pairs={{0,130},{1,131},{2,128},{3,129},{128,2},{129,3},{130,0},{131,1},{4... | collective-permute-start | bytes 1544 | tf_op jit(solution)/shard_map/ppermute | solution.py:418
  12.5 0.1 collective-permute-start.4
  12.6 1.8 %collective-permute-done.5 = s32[1,128]{1,0:T(1,128)S(1)} collective-permute-done((s32[1,128]{1,0:T(1,128)S(1)}, s32[1,128]{1,0:T(1,128)S(1)}, u32[]{:S(2)}, u32[]{:S(2)}) %collective-permute-start.5) | collective-permute-done | bytes 544 | tf_op jit(solution)/shard_map/ppermute | solution.py:418
  14.5 1.6 collective-permute-done.4
  16.1 1.1 collective-permute-done.6
  17.3 0.1 copy.27
  17.4 0.1 copy.29
  17.5 0.1 reshape.301
  17.7 0.1 copy.28
  17.9 0.6 pad.13.clone
  18.5 12.5 %all-to-all-start = ((s32[32,1,128]{2,1,0:T(1,128)}), s32[32,1,128]{2,1,0:T(1,128)S(1)}, u32[]{:S(2)}, u32[]{:S(2)}) async-start(s32[32,1,128]{2,1,0:T(1,128)} %pad.13.clone), calls=%async_computation | async-start | bytes 32768 | tf_op jit(solution)/shard_map/all_to_all | solution.py:441
  31.0 0.7 fusion.13
  32.3 0.1 stack.45.refs_6_.refs_11_
  32.4 7.2 %all-to-all-done = s32[32,1,128]{2,1,0:T(1,128)S(1)} async-done(((s32[32,1,128]{2,1,0:T(1,128)}), s32[32,1,128]{2,1,0:T(1,128)S(1)}, u32[]{:S(2)}, u32[]{:S(2)}) %all-to-all-start) | async-done | bytes 16416 | tf_op jit(solution)/shard_map/all_to_all | solution.py:441
  39.6 0.1 select_n.155
  39.8 0.1 broadcast_in_dim.126.refs_10_.refs_15_
  39.9 0.1 broadcast_in_dim.115.refs_7_.refs_12_
  40.0 7.0 %shard_map.65 = (f32[8,4,128,128]{3,2,1,0:T(8,128)S(1)}, f32[8,2,48,128]{3,2,1,0:T(8,128)S(1)}, f32[8,2,80,128]{3,2,1,0:T(8,128)S(1)}, f32[8,2,48,128]{3,2,1,0:T...) custom-call(f32[8,2,128,128]{3,2,1,0:T(8,128)} %collective-permute-done.refs_0_, ...), custom_call_target="tpu_custom_call" | custom-call | tf_op jit(solution)/shard_map/pallas_call | solution.py:271
  47.1 0.8 collective-permute-start.7
  47.8 0.7 collective-permute-start.8
  48.6 0.6 collective-permute-start.11
  49.2 1.4 collective-permute-start.12
  50.6 3.9 %collective-permute-done.7.near = f32[68,8,128]{2,1,0:T(8,128)S(1)} collective-permute-done((f32[68,8,128]{2,1,0:T(8,128)S(1)}, f32[68,8,128]{2,1,0:T(8,128)S(1)}, u32[]{:S(2)}, u32[]{:S(2)}) %collective-permute-start.7) | collective-permute-done | bytes 278560 | tf_op jit(solution)/shard_map/ppermute | solution.py:418
  54.5 1.3 collective-permute-done.8.far
  55.8 0.2 collective-permute-done.9.mate_near
  56.1 1.3 collective-permute-done.10.mate_far
  57.4 0.1 shard_map.66
  57.5 1.0 copy-done.2
  58.5 0.8 copy-done.9
  59.3 0.8 copy-done.11
  60.1 10.1 %all-to-all-start.1 = ((f32[32,64,128]{2,1,0:T(8,128)}), f32[32,64,128]{2,1,0:T(8,128)S(1)}, u32[]{:S(2)}, u32[]{:S(2)}) async-start(f32[32,64,128]{2,1,0:T(8,128)} %bitcast.60), calls=%async_computation.1 | async-start | bytes 2097152 | tf_op jit(solution)/shard_map/all_to_all | solution.py:429
  70.2 1.5 collective-permute-start.15
  71.8 0.6 collective-permute-start.16
  72.3 0.8 convert_reduce_fusion
  73.1 0.6 divide_select_fusion
  73.7 22.7 %all-to-all-done.1 = f32[32,64,128]{2,1,0:T(8,128)S(1)} async-done(((f32[32,64,128]{2,1,0:T(8,128)}), f32[32,64,128]{2,1,0:T(8,128)S(1)}, u32[]{:S(2)}, u32[]{:S(2)}) %all-to-all-start.1) | async-done | bytes 1048608 | tf_op jit(solution)/shard_map/all_to_all | solution.py:429
  96.4 0.8 broadcast_in_dim.127.refs_3_
  97.3 1.6 copy-done.4
  98.9 1.5 shard_map.67
  100.4 1.5 collective-permute-start.13
  101.9 0.6 collective-permute-start.14
  102.5 3.2 %collective-permute-start.18 = (f32[8,8,128]{2,1,0:T(8,128)S(1)}, f32[8,8,128]{2,1,0:T(8,128)S(1)}, u32[]{:S(2)}, u32[]{:S(2)}) collective-permute-start(f32[8,8,128]{2,1,0:T(8,128)S(1)} %get-tuple-element.51), channel_id=1, source_target_pairs={{0,3},{1,0},{2,1},{3,2},{4,7},{5,4},{6,5},{7,6},{8,11},{9,8},{10,9... | collective-permute-start | bytes 98312 | tf_op jit(solution)/shard_map/ppermute | solution.py:366
  105.7 1.1 collective-permute-done.14.refs_1_
  106.8 0.5 collective-permute-done.17.refs_8_
  107.3 6.9 %shard_map.68 = (f32[8,4,128,128]{3,2,1,0:T(8,128)S(1)}, f32[68,8,128]{2,1,0:T(8,128)S(1)}, f32[68,8,128]{2,1,0:T(8,128)S(1)}) custom-call(f32[8,8,128]{2,1,0:T(8,128)S(1)} %collective-permute-done.13.refs_0_, f32[8,8,128]{2,1,0:T(8,128)S(1)} %collective-permute-done.14.refs_1_, f32[8,4,128,128]{3,2,1,0:T(8,128)S(1)} %get-tuple-element.45.refs_2_, ...), custom_call_target="tpu_custom_call" | custom-call | tf_op jit(solution)/shard_map/pallas_call | solution.py:271
  114.2 0.7 collective-permute-start.19
  114.9 1.7 %collective-permute-start.20 = (f32[68,8,128]{2,1,0:T(8,128)S(1)}, f32[68,8,128]{2,1,0:T(8,128)S(1)}, u32[]{:S(2)}, u32[]{:S(2)}) collective-permute-start(f32[68,8,128]{2,1,0:T(8,128)S(1)} %get-tuple-element.54), channel_id=1, source_target_pairs={{0,130},{1,131},{2,128},{3,129},{128,2},{129,3},{130,0},{131,1},{4... | collective-permute-start | bytes 835592 | tf_op jit(solution)/shard_map/ppermute | solution.py:418
  116.6 6.4 %collective-permute-done.19.near = f32[68,8,128]{2,1,0:T(8,128)S(1)} collective-permute-done((f32[68,8,128]{2,1,0:T(8,128)S(1)}, f32[68,8,128]{2,1,0:T(8,128)S(1)}, u32[]{:S(2)}, u32[]{:S(2)}) %collective-permute-start.19) | collective-permute-done | bytes 278560 | tf_op jit(solution)/shard_map/ppermute | solution.py:418
  123.0 0.9 collective-permute-start.21
  123.9 1.1 collective-permute-done.20.far
  125.1 0.4 collective-permute-start.22
  125.4 1.2 collective-permute-done.22.mate_far
  126.6 0.1 shard_map.69
  126.8 38.1 %all_to_all.15 = f32[32,64,128]{2,1,0:T(8,128)S(1)} all-to-all(f32[32,64,128]{2,1,0:T(8,128)S(1)} %bitcast.61), channel_id=1, replica_groups=mesh['patch'=2,'theta'=32,'phi'=4] {'theta'}, dimensions={0} | all-to-all | bytes 2097152 | tf_op jit(solution)/shard_map/all_to_all | solution.py:429
  164.9 2.5 %shard_map.70 = f32[8,4,128,128]{3,2,1,0:T(8,128)} custom-call(f32[8,4,128,128]{3,2,1,0:T(8,128)S(1)} %get-tuple-element.52.refs_0_, f32[256,8,128]{2,1,0:T(8,128)S(1)} %bitcast.62, bf16[512,256]{1,0:T(8,128)(2,1)S(1)} %fusion.refs_2_, f32[512,128]{1,0:T(8,128)S(1)} %broadcast_in_dim.127.refs_3_), custom_call_target="tpu_custom_call" | custom-call | tf_op jit(solution)/shard_map/pallas_call | solution.py:351
  (82 shorter events, 0.9 us)
Async XLA Ops:
  0.0 9.6 %copy-start.21 = (pred[128]{0:T(512)(128)(4,1)S(1)}, pred[128]{0:T(512)(128)(4,1)}, u32[]{:S(2)}) copy-start(pred[128]{0:T(512)(128)(4,1)} %constant.119.clone.1) | copy-start | bytes 388
  0.0 8.8 %copy-start.18 = (s32[1,1,1,96]{3,2,1,0:T(1,128)S(1)}, s32[1,1,1,96]{3,2,1,0:T(1,128)}, u32[]{:S(2)}) copy-start(s32[1,1,1,96]{3,2,1,0:T(1,128)} %param.11) | copy-start | bytes 1156
  0.0 8.8 %copy-start.17 = (s32[1,1,1,96]{3,2,1,0:T(1,128)S(1)}, s32[1,1,1,96]{3,2,1,0:T(1,128)}, u32[]{:S(2)}) copy-start(s32[1,1,1,96]{3,2,1,0:T(1,128)} %param.10) | copy-start | bytes 1156
  0.0 9.2 %copy-start.19 = (s32[1,1,1,96]{3,2,1,0:T(1,128)S(1)}, s32[1,1,1,96]{3,2,1,0:T(1,128)}, u32[]{:S(2)}) copy-start(s32[1,1,1,96]{3,2,1,0:T(1,128)} %param.7) | copy-start | bytes 1156
  0.0 1.6 copy-start
  1.7 7.6 %copy-start.20 = (f32[1,1,1,96]{3,2,1,0:T(1,128)S(1)}, f32[1,1,1,96]{3,2,1,0:T(1,128)}, u32[]{:S(2)}) copy-start(f32[1,1,1,96]{3,2,1,0:T(1,128)} %param.9) | copy-start | bytes 1156
  1.7 7.6 %copy-start.16 = (f32[1,1,1,4,96]{4,3,2,1,0:T(4,128)S(1)}, f32[1,1,1,4,96]{4,3,2,1,0:T(4,128)}, u32[]{:S(2)}) copy-start(f32[1,1,1,4,96]{4,3,2,1,0:T(4,128)} %param.8) | copy-start | bytes 4612
  1.7 38.3 %copy-start.1 = (f32[1,8,4,128,128]{4,3,2,1,0:T(8,128)S(1)}, f32[1,8,4,128,128]{4,3,2,1,0:T(8,128)}, u32[]{:S(2)}) copy-start(f32[1,8,4,128,128]{4,3,2,1,0:T(8,128)} %param.6) | copy-start | bytes 6291460
  3.1 6.5 %collective-permute-start.2 = (f32[8,8,128]{2,1,0:T(8,128)S(1)}, f32[8,8,128]{2,1,0:T(8,128)S(1)}, u32[]{:S(2)}, u32[]{:S(2)}) collective-permute-start(f32[8,8,128]{2,1,0:T(8,128)S(1)} %get-tuple-element.32), channel_id=1, source_target_pairs={{0,1},{1,2},{2,3},{3,0},{4,5},{5,6},{6,7},{7,4},{8,9},{9,10},{10,1... | collective-permute-start | bytes 98312 | tf_op jit(solution)/shard_map/ppermute | solution.py:366
  3.1 6.4 %collective-permute-start.3 = (f32[8,8,128]{2,1,0:T(8,128)S(1)}, f32[8,8,128]{2,1,0:T(8,128)S(1)}, u32[]{:S(2)}, u32[]{:S(2)}) collective-permute-start(f32[8,8,128]{2,1,0:T(8,128)S(1)} %get-tuple-element.33), channel_id=1, source_target_pairs={{0,3},{1,0},{2,1},{3,2},{4,7},{5,4},{6,5},{7,6},{8,11},{9,8},{10,9... | collective-permute-start | bytes 98312 | tf_op jit(solution)/shard_map/ppermute | solution.py:366
  6.4 33.4 %collective-permute-start = (f32[8,2,128,128]{3,2,1,0:T(8,128)}, f32[8,2,128,128]{3,2,1,0:T(8,128)}, u32[]{:S(2)}, u32[]{:S(2)}) collective-permute-start(f32[8,2,128,128]{3,2,1,0:T(8,128)} %get-tuple-element.30), channel_id=1, source_target_pairs={{0,4},{4,8},{8,12},{12,16},{16,20},{20,24},{24,28},{28,32},{32,36}... | collective-permute-start | bytes 3145736 | tf_op jit(solution)/shard_map/ppermute | solution.py:366
  7.9 31.9 %collective-permute-start.1 = (f32[8,2,128,128]{3,2,1,0:T(8,128)}, f32[8,2,128,128]{3,2,1,0:T(8,128)}, u32[]{:S(2)}, u32[]{:S(2)}) collective-permute-start(f32[8,2,128,128]{3,2,1,0:T(8,128)} %get-tuple-element.31), channel_id=1, source_target_pairs={{0,124},{4,0},{8,4},{12,8},{16,12},{20,16},{24,20},{28,24},{32,28}... | collective-permute-start | bytes 3145736 | tf_op jit(solution)/shard_map/ppermute | solution.py:366
  9.5 37.5 %copy-start.5 = (f32[96,512]{1,0:T(8,128)}, f32[96,512]{1,0:T(8,128)S(1)}, u32[]{:S(2)}) copy-start(f32[96,512]{1,0:T(8,128)S(1)} %select_add_fusion.refs_9_.refs_14_) | copy-start | bytes 589828
  9.6 4.8 %collective-permute-start.5 = (s32[1,128]{1,0:T(1,128)S(1)}, s32[1,128]{1,0:T(1,128)S(1)}, u32[]{:S(2)}, u32[]{:S(2)}) collective-permute-start(s32[1,128]{1,0:T(1,128)S(1)} %pad_bitcast_fusion), channel_id=1, source_target_pairs={{0,130},{1,131},{2,128},{3,129},{128,2},{129,3},{130,0},{131,1},{4... | collective-permute-start | bytes 1544 | tf_op jit(solution)/shard_map/ppermute | solution.py:418
  12.5 3.5 %collective-permute-start.4 = (s32[1,128]{1,0:T(1,128)S(1)}, s32[1,128]{1,0:T(1,128)S(1)}, u32[]{:S(2)}, u32[]{:S(2)}) collective-permute-start(s32[1,128]{1,0:T(1,128)S(1)} %select_bitcast_fusion), channel_id=1, source_target_pairs={{0,128},{1,129},{2,130},{3,131},{128,0},{129,1},{130,2},{131,3},{4... | collective-permute-start | bytes 1544 | tf_op jit(solution)/shard_map/ppermute | solution.py:418
  16.0 1.1 collective-permute-start.6
  18.5 21.0 %all-to-all-start = ((s32[32,1,128]{2,1,0:T(1,128)}), s32[32,1,128]{2,1,0:T(1,128)S(1)}, u32[]{:S(2)}, u32[]{:S(2)}) async-start(s32[32,1,128]{2,1,0:T(1,128)} %pad.13.clone), calls=%async_computation | async-start | bytes 32768 | tf_op jit(solution)/shard_map/all_to_all | solution.py:441
  39.7 20.4 %copy-start.15 = (s32[256]{0:T(256)}, s32[256]{0:T(256)S(1)}, u32[]{:S(2)}) copy-start(s32[256]{0:T(256)S(1)} %select_n.155) | copy-start | bytes 3076
  39.9 7.2 %copy-start.7 = (f32[2,96,128]{2,1,0:T(8,128)}, f32[2,96,128]{2,1,0:T(8,128)S(1)}, u32[]{:S(2)}) copy-start(f32[2,96,128]{2,1,0:T(8,128)S(1)} %broadcast_in_dim.126.refs_10_.refs_15_) | copy-start | bytes 294916
  47.0 10.5 %copy-start.3 = (f32[8,4,128,128]{3,2,1,0:T(8,128)}, f32[8,4,128,128]{3,2,1,0:T(8,128)S(1)}, u32[]{:S(2)}) copy-start(f32[8,4,128,128]{3,2,1,0:T(8,128)S(1)} %get-tuple-element.36.refs_0_) | copy-start | bytes 6291460
  47.1 12.2 %copy-start.13 = (f32[8,2,80,128]{3,2,1,0:T(8,128)}, f32[8,2,80,128]{3,2,1,0:T(8,128)S(1)}, u32[]{:S(2)}) copy-start(f32[8,2,80,128]{3,2,1,0:T(8,128)S(1)} %get-tuple-element.49) | copy-start | bytes 1966084
  47.1 12.2 %copy-start.14 = (f32[8,2,80,128]{3,2,1,0:T(8,128)}, f32[8,2,80,128]{3,2,1,0:T(8,128)S(1)}, u32[]{:S(2)}) copy-start(f32[8,2,80,128]{3,2,1,0:T(8,128)S(1)} %get-tuple-element.47) | copy-start | bytes 1966084
  47.1 7.4 %collective-permute-start.7 = (f32[68,8,128]{2,1,0:T(8,128)S(1)}, f32[68,8,128]{2,1,0:T(8,128)S(1)}, u32[]{:S(2)}, u32[]{:S(2)}) collective-permute-start(f32[68,8,128]{2,1,0:T(8,128)S(1)} %get-tuple-element.37), channel_id=1, source_target_pairs={{0,128},{1,129},{2,130},{3,131},{128,0},{129,1},{130,2},{131,3},{4... | collective-permute-start | bytes 835592 | tf_op jit(solution)/shard_map/ppermute | solution.py:418
  47.8 8.0 %collective-permute-start.8 = (f32[68,8,128]{2,1,0:T(8,128)S(1)}, f32[68,8,128]{2,1,0:T(8,128)S(1)}, u32[]{:S(2)}, u32[]{:S(2)}) collective-permute-start(f32[68,8,128]{2,1,0:T(8,128)S(1)} %get-tuple-element.38), channel_id=1, source_target_pairs={{0,130},{1,131},{2,128},{3,129},{128,2},{129,3},{130,0},{131,1},{4... | collective-permute-start | bytes 835592 | tf_op jit(solution)/shard_map/ppermute | solution.py:418
  48.6 10.0 %collective-permute-start.11 = (f32[8,2,48,128]{3,2,1,0:T(8,128)S(1)}, f32[8,2,48,128]{3,2,1,0:T(8,128)S(1)}, u32[]{:S(2)}, u32[]{:S(2)}) collective-permute-start(f32[8,2,48,128]{3,2,1,0:T(8,128)S(1)} %get-tuple-element.39), channel_id=1, source_target_pairs={{0,4},{4,8},{8,12},{12,16},{16,20},{20,24},{24,28},{28,32},{32,36}... | collective-permute-start | bytes 1179656 | tf_op jit(solution)/shard_map/ppermute | solution.py:366
  49.2 10.1 %collective-permute-start.12 = (f32[8,2,48,128]{3,2,1,0:T(8,128)S(1)}, f32[8,2,48,128]{3,2,1,0:T(8,128)S(1)}, u32[]{:S(2)}, u32[]{:S(2)}) collective-permute-start(f32[8,2,48,128]{3,2,1,0:T(8,128)S(1)} %get-tuple-element.40), channel_id=1, source_target_pairs={{0,124},{4,0},{8,4},{12,8},{16,12},{20,16},{24,20},{28,24},{32,28}... | collective-permute-start | bytes 1179656 | tf_op jit(solution)/shard_map/ppermute | solution.py:366
  54.5 1.6 collective-permute-start.9
  55.8 1.6 collective-permute-start.10
  57.5 1.0 copy-start.2
  58.5 0.8 copy-start.9
  59.3 0.8 copy-start.11
  60.1 36.3 %all-to-all-start.1 = ((f32[32,64,128]{2,1,0:T(8,128)}), f32[32,64,128]{2,1,0:T(8,128)S(1)}, u32[]{:S(2)}, u32[]{:S(2)}) async-start(f32[32,64,128]{2,1,0:T(8,128)} %bitcast.60), calls=%async_computation.1 | async-start | bytes 2097152 | tf_op jit(solution)/shard_map/all_to_all | solution.py:429
  70.2 32.2 %collective-permute-start.15 = (f32[8,2,80,128]{3,2,1,0:T(8,128)}, f32[8,2,80,128]{3,2,1,0:T(8,128)}, u32[]{:S(2)}, u32[]{:S(2)}) collective-permute-start(f32[8,2,80,128]{3,2,1,0:T(8,128)} %copy-done.14), channel_id=1, source_target_pairs={{0,4},{4,8},{8,12},{12,16},{16,20},{20,24},{24,28},{28,32},{32,36}... | collective-permute-start | bytes 1966088 | tf_op jit(solution)/shard_map/ppermute | solution.py:366
  71.8 34.0 %collective-permute-start.16 = (f32[8,2,80,128]{3,2,1,0:T(8,128)}, f32[8,2,80,128]{3,2,1,0:T(8,128)}, u32[]{:S(2)}, u32[]{:S(2)}) collective-permute-start(f32[8,2,80,128]{3,2,1,0:T(8,128)} %copy-done.13), channel_id=1, source_target_pairs={{0,124},{4,0},{8,4},{12,8},{16,12},{20,16},{24,20},{28,24},{32,28}... | collective-permute-start | bytes 1966088 | tf_op jit(solution)/shard_map/ppermute | solution.py:366
  96.4 10.9 %copy-start.6 = (f32[96,512]{1,0:T(8,128)S(1)}, f32[96,512]{1,0:T(8,128)}, u32[]{:S(2)}) copy-start(f32[96,512]{1,0:T(8,128)} %copy-done.5) | copy-start | bytes 589828
  97.3 1.6 copy-start.4
  98.8 8.5 %copy-start.8 = (f32[2,96,128]{2,1,0:T(8,128)S(1)}, f32[2,96,128]{2,1,0:T(8,128)}, u32[]{:S(2)}) copy-start(f32[2,96,128]{2,1,0:T(8,128)} %copy-done.7) | copy-start | bytes 294916
  98.9 8.5 %copy-start.10 = (f32[8,2,48,128]{3,2,1,0:T(8,128)S(1)}, f32[8,2,48,128]{3,2,1,0:T(8,128)}, u32[]{:S(2)}) copy-start(f32[8,2,48,128]{3,2,1,0:T(8,128)} %copy-done.9) | copy-start | bytes 1179652
  98.9 8.5 %copy-start.12 = (f32[8,2,48,128]{3,2,1,0:T(8,128)S(1)}, f32[8,2,48,128]{3,2,1,0:T(8,128)}, u32[]{:S(2)}) copy-start(f32[8,2,48,128]{3,2,1,0:T(8,128)} %copy-done.11) | copy-start | bytes 1179652
  100.4 5.4 %collective-permute-start.13 = (f32[8,8,128]{2,1,0:T(8,128)S(1)}, f32[8,8,128]{2,1,0:T(8,128)S(1)}, u32[]{:S(2)}, u32[]{:S(2)}) collective-permute-start(f32[8,8,128]{2,1,0:T(8,128)S(1)} %get-tuple-element.43), channel_id=1, source_target_pairs={{0,4},{4,8},{8,12},{12,16},{16,20},{20,24},{24,28},{28,32},{32,36}... | collective-permute-start | bytes 98312 | tf_op jit(solution)/shard_map/ppermute | solution.py:366
  101.9 4.9 %collective-permute-start.14 = (f32[8,8,128]{2,1,0:T(8,128)S(1)}, f32[8,8,128]{2,1,0:T(8,128)S(1)}, u32[]{:S(2)}, u32[]{:S(2)}) collective-permute-start(f32[8,8,128]{2,1,0:T(8,128)S(1)} %get-tuple-element.44), channel_id=1, source_target_pairs={{0,124},{4,0},{8,4},{12,8},{16,12},{20,16},{24,20},{28,24},{32,28}... | collective-permute-start | bytes 98312 | tf_op jit(solution)/shard_map/ppermute | solution.py:366
  102.5 4.8 %collective-permute-start.17 = (f32[8,8,128]{2,1,0:T(8,128)S(1)}, f32[8,8,128]{2,1,0:T(8,128)S(1)}, u32[]{:S(2)}, u32[]{:S(2)}) collective-permute-start(f32[8,8,128]{2,1,0:T(8,128)S(1)} %get-tuple-element.50), channel_id=1, source_target_pairs={{0,1},{1,2},{2,3},{3,0},{4,5},{5,6},{6,7},{7,4},{8,9},{9,10},{10,1... | collective-permute-start | bytes 98312 | tf_op jit(solution)/shard_map/ppermute | solution.py:366
  102.5 4.8 %collective-permute-start.18 = (f32[8,8,128]{2,1,0:T(8,128)S(1)}, f32[8,8,128]{2,1,0:T(8,128)S(1)}, u32[]{:S(2)}, u32[]{:S(2)}) collective-permute-start(f32[8,8,128]{2,1,0:T(8,128)S(1)} %get-tuple-element.51), channel_id=1, source_target_pairs={{0,3},{1,0},{2,1},{3,2},{4,7},{5,4},{6,5},{7,6},{8,11},{9,8},{10,9... | collective-permute-start | bytes 98312 | tf_op jit(solution)/shard_map/ppermute | solution.py:366
  114.2 8.8 %collective-permute-start.19 = (f32[68,8,128]{2,1,0:T(8,128)S(1)}, f32[68,8,128]{2,1,0:T(8,128)S(1)}, u32[]{:S(2)}, u32[]{:S(2)}) collective-permute-start(f32[68,8,128]{2,1,0:T(8,128)S(1)} %get-tuple-element.53), channel_id=1, source_target_pairs={{0,128},{1,129},{2,130},{3,131},{128,0},{129,1},{130,2},{131,3},{4... | collective-permute-start | bytes 835592 | tf_op jit(solution)/shard_map/ppermute | solution.py:418
  114.9 10.2 %collective-permute-start.20 = (f32[68,8,128]{2,1,0:T(8,128)S(1)}, f32[68,8,128]{2,1,0:T(8,128)S(1)}, u32[]{:S(2)}, u32[]{:S(2)}) collective-permute-start(f32[68,8,128]{2,1,0:T(8,128)S(1)} %get-tuple-element.54), channel_id=1, source_target_pairs={{0,130},{1,131},{2,128},{3,129},{128,2},{129,3},{130,0},{131,1},{4... | collective-permute-start | bytes 835592 | tf_op jit(solution)/shard_map/ppermute | solution.py:418
  123.0 2.4 %collective-permute-start.21 = (f32[68,8,128]{2,1,0:T(8,128)S(1)}, f32[68,8,128]{2,1,0:T(8,128)S(1)}, u32[]{:S(2)}, u32[]{:S(2)}) collective-permute-start(f32[68,8,128]{2,1,0:T(8,128)S(1)} %collective-permute-done.19.near), channel_id=1, source_target_pairs={{0,1},{1,0},{2,3},{3,2},{4,5},{5,4},{6,7},{7,6},{8,9},{9,8},{10,11... | collective-permute-start | bytes 835592 | tf_op jit(solution)/shard_map/ppermute | solution.py:423
  125.1 1.6 collective-permute-start.22
